TPU v7x, 512 devices: a whole 4x8x8 slice. The times are simulated.
512 devices in a mesh: pts: 32 (over z_hi, y, core), val: 16 (over z_lo, x).
Axes of the slice: x: 4, y: 8, z: 8 (z_hi: 2, z_lo: 4; z = z_hi * 4 + z_lo), core: 2. Of those that a mesh axis runs over, the one named last changes fastest.
Arguments:
- vectors: float32 [1, 512, 2048], P(None, 'val', 'pts'), may hold values from -6 to 6
- eval_energy: float32 [512], P('val'), may hold values from -2 to -0.2
- cond_energy: float32 [2048], P('pts'), may hold values from 0.2 to 2
- val_orbitals: float32 [512, 8192], P('pts', 'val'), may hold values from -0.25 to 0.25
- cond_orbitals: float32 [2048, 8192], P('val', 'pts'), may hold values from -0.125 to 0.125
- screened: float32 [8192, 8192], P('val', 'pts'), may hold values from -1.5 to 1.5
Outputs:
- filtered: float32 [1, 512, 2048], P(None, 'val', 'pts')
All inputs are finite; a program needn't handle non-finite values.
Results may differ from a plain program's by a relative error of at most 0.00013.
Values sent between devices are 32-bit elements; how exact they have to be, the bound alone decides.
No kernel may reach another device: no remote copies, remote signals or barrier semaphores. Data moves between devices by JAX's collectives and lax.ppermute only.
A program may use at most 64 MiB of HBM per device.

v0:
```python
import jax
import jax.numpy as jnp
from jax import lax
from jax.sharding import Mesh
from jax.sharding import PartitionSpec as P

ITERS = 2
PTS = ("pts_0", "pts_1", "pts_2")


CENTER = 2.2
HALF_WIDTH = 2.0


def laid_out(blocks, dim):
    blocks = jnp.moveaxis(blocks, 0, dim)
    dims = blocks.shape
    return blocks.reshape(*dims[:dim], dims[dim] * dims[dim + 1], *dims[dim + 2 :])


def copy_for_each(array, axis):
    peers = lax.axis_size(axis)
    return lax.all_to_all(
        jnp.broadcast_to(array[None], (peers, *array.shape)), axis, 0, 0, tiled=True
    )


def gather_directly(array, axis, dim):
    return laid_out(copy_for_each(array, axis), dim)


def stacked_from(array, axes, turns):
    blocks = array[None]
    for k in turns:
        blocks = lax.all_gather(blocks, axes[k], axis=0, tiled=True)
    held = [lax.axis_size(axes[k]) for k in reversed(turns)]
    blocks = blocks.reshape(*held, *array.shape)
    turned = sorted(range(len(turns)), key=lambda place: turns[len(turns) - 1 - place])
    return blocks.transpose(*turned, *range(len(turns), blocks.ndim)).reshape(-1, *array.shape)


def gathered_by_axis(array, axes, turns, dim):
    return laid_out(stacked_from(array, axes, turns), dim)


def in_blocks(array, dim, peers):
    before, after = (array.shape[:dim], array.shape[dim + 1 :])
    return jnp.moveaxis(array.reshape(*before, peers, -1, *after), dim, 0)


def sent_and_summed(array, axis, dim):
    peers = lax.axis_size(axis)
    blocks = lax.all_to_all(in_blocks(array, dim, peers), axis, 0, 0, tiled=True)
    return jnp.sum(blocks, axis=0)


def per_device(vectors, eval_energy, cond_energy, val_orbitals, cond_orbitals, screened):
    highest = lax.Precision.HIGHEST
    cond_whole = gather_directly(cond_orbitals, "val", 0)
    val_whole = gathered_by_axis(val_orbitals, (("pts_0", "pts_1"), "pts_2"), (0, 1), 0)
    ediff = cond_energy[None, None, :] - eval_energy[None, :, None]
    older = vectors
    newer = vectors
    for step in range(ITERS):
        direct_full_x = gather_directly(newer, PTS, 2)
        pair = jnp.einsum(
            "bvc,cn->bvn",
            direct_full_x,
            cond_whole,
            precision=highest,
            preferred_element_type=jnp.float32,
        )
        pair_all = gather_directly(pair, "val", 1)
        mixed = jnp.einsum(
            "vm,bvn->bmn",
            val_whole,
            pair_all,
            precision=highest,
            preferred_element_type=jnp.float32,
        )
        weighted = mixed * screened[None, :, :]
        back_terms = jnp.einsum(
            "vm,bmn->bvn",
            val_whole,
            weighted,
            precision=highest,
            preferred_element_type=jnp.float32,
        )
        back = sent_and_summed(back_terms, "val", 1)
        hamil = ediff * newer - sent_and_summed(
            jnp.einsum(
                "bvn,cn->bvc",
                back,
                cond_whole,
                precision=highest,
                preferred_element_type=jnp.float32,
            ),
            PTS,
            2,
        )
        scaled = (hamil - CENTER * newer) / HALF_WIDTH
        if step == 0:
            following = scaled
        else:
            following = 2.0 * scaled - older
        older = newer
        newer = following
    return newer


def solution(mesh):
    torus = Mesh(
        mesh.devices.reshape(2, 8, 2, mesh.shape["val"]), ("pts_0", "pts_1", "pts_2", "val")
    )
    placed = (P(None, "val", PTS), P("val"), P(PTS), P(PTS, "val"), P("val", PTS), P("val", PTS))
    return jax.shard_map(
        per_device, mesh=torus, in_specs=placed, out_specs=P(None, "val", PTS), check_vma=False
    )
```

profile of v0, /device:TPU:1, one launch (start us, length us, event | category | flops | bytes accessed | tf_op | source)
XLA Modules:
  0.0 292.8 jit_solution(11212002882304272839)
XLA Ops:
  7.6 32.8 %all_to_all.45 = f32[32,1,2048]{2,1,0:T(1,128)S(1)} all-to-all(f32[32,1,2048]{2,1,0:T(1,128)S(1)} %reshape.138), channel_id=1, replica_groups=mesh['pts_0'=2,'pts_1'=8,'pts_2'=2,'val'=16] {'pts_0','pts_1','pts_2'}, dimensions={0} | all-to-all | bytes 524288 | tf_op jit(solution)/shard_map/all_to_all | solution.py:23
  40.5 2.5 broadcast_in_dim.20
  42.9 7.0 %all-to-all-start.1 = ((f32[16,128,256]{2,1,0:T(8,128)}), f32[16,128,256]{2,1,0:T(8,128)S(1)}, u32[]{:S(2)}, u32[]{:S(2)}) async-start(f32[16,128,256]{2,1,0:T(8,128)} %broadcast_in_dim.20), calls=%async_computation.1 | async-start | bytes 4194304 | tf_op jit(solution)/shard_map/all_to_all | solution.py:23
  50.0 47.2 %all-gather = f32[256,512]{1,0:T(8,128)} all-gather(f32[16,512]{1,0:T(8,128)S(1)} %copy-done.3), channel_id=2, replica_groups=mesh['pts_0'=2,'pts_1'=8,'pts_2'=2,'val'=16] {'pts_0','pts_1'}, dimensions={0}, use_global_device_ids=true | all-gather | bytes 557056 | tf_op jit(solution)/shard_map/all_gather | solution.py:35
  99.7 2.2 all-to-all-done.1
  103.8 12.0 %all-to-all-start.2 = ((f32[16,1,32,256]{3,2,1,0:T(8,128)}), f32[16,1,32,256]{3,2,1,0:T(8,128)}, u32[]{:S(2)}, u32[]{:S(2)}) async-start(f32[16,1,32,256]{3,2,1,0:T(8,128)} %broadcast_in_dim.21), calls=%async_computation.2 | async-start | bytes 1048576 | tf_op jit(solution)/shard_map/all_to_all | solution.py:23
  116.8 3.0 %all-gather.3.cloned.1.call-done = f32[32,16,512]{2,1,0:T(8,128)} async-done(((f32[16,16,512]{2,1,0:T(8,128)}), f32[32,16,512]{2,1,0:T(8,128)}) %all-gather.3.cloned.1.call-update) | async-done | bytes 1048592 | tf_op jit(solution)/shard_map/all_gather | solution.py:35
  121.1 8.0 %all-to-all-done.2 = f32[16,1,32,256]{3,2,1,0:T(8,128)} async-done(((f32[16,1,32,256]{3,2,1,0:T(8,128)}), f32[16,1,32,256]{3,2,1,0:T(8,128)}, u32[]{:S(2)}, u32[]{:S(2)}) %all-to-all-start.2) | async-done | bytes 524320 | tf_op jit(solution)/shard_map/all_to_all | solution.py:23
  129.0 2.3 fusion.3
  131.3 1.9 convolution_bitcast_fusion.4
  133.2 2.1 copy.18
  135.2 18.4 %all_to_all.46 = f32[16,1,32,256]{3,2,1,0:T(8,128)} all-to-all(f32[16,1,32,256]{3,2,1,0:T(8,128)} %bitcast.106), channel_id=1, replica_groups=mesh['pts_0'=2,'pts_1'=8,'pts_2'=2,'val'=16] {'val'}, dimensions={0} | all-to-all | bytes 1048576 | tf_op jit(solution)/shard_map/all_to_all | solution.py:53
  154.8 3.8 %convolution_bitcast_fusion.1 = f32[32,1,32,64]{3,2,1,0:T(8,128)} fusion(f32[32,64,256]{2,1,0:T(8,128)S(1)} %bitcast.96, f32[32,256]{1,0:T(8,128)S(1)} %reduce_sum.40), kind=kOutput, calls=%fused_computation.1 | convolution fusion | flops 201326592 | bytes 2392064 | tf_op jit(solution)/shard_map/bvn,cn->bvc/dot_general | solution.py:91
  158.5 1.4 reshape.140
  159.9 23.0 %all_to_all.47 = f32[32,1,2048]{2,1,0:T(1,128)} all-to-all(f32[32,1,2048]{2,1,0:T(1,128)S(1)} %reshape.140), channel_id=1, replica_groups=mesh['pts_0'=2,'pts_1'=8,'pts_2'=2,'val'=16] {'pts_0','pts_1','pts_2'}, dimensions={0} | all-to-all | bytes 524288 | tf_op jit(solution)/shard_map/all_to_all | solution.py:53
  182.9 2.2 reduce.5
  189.6 20.7 %all_to_all.48 = f32[32,1,2048]{2,1,0:T(1,128)} all-to-all(f32[32,1,2048]{2,1,0:T(1,128)S(1)} %reshape.142), channel_id=1, replica_groups=mesh['pts_0'=2,'pts_1'=8,'pts_2'=2,'val'=16] {'pts_0','pts_1','pts_2'}, dimensions={0} | all-to-all | bytes 524288 | tf_op jit(solution)/shard_map/all_to_all | solution.py:23
  210.3 2.2 reduce.6
  213.6 2.2 copy.21
  218.1 17.1 %all_to_all.49 = f32[16,1,32,256]{3,2,1,0:T(8,128)S(1)} all-to-all(f32[16,1,32,256]{3,2,1,0:T(8,128)S(1)} %broadcast_in_dim.51), channel_id=1, replica_groups=mesh['pts_0'=2,'pts_1'=8,'pts_2'=2,'val'=16] {'val'}, dimensions={0} | all-to-all | bytes 1048576 | tf_op jit(solution)/shard_map/all_to_all | solution.py:23
  236.3 1.8 convolution_bitcast_fusion.2
  239.4 18.1 %all_to_all.50 = f32[16,1,32,256]{3,2,1,0:T(8,128)S(1)} all-to-all(f32[16,1,32,256]{3,2,1,0:T(8,128)S(1)} %bitcast.108), channel_id=1, replica_groups=mesh['pts_0'=2,'pts_1'=8,'pts_2'=2,'val'=16] {'val'}, dimensions={0} | all-to-all | bytes 1048576 | tf_op jit(solution)/shard_map/all_to_all | solution.py:53
  257.5 2.9 %convolution_bitcast_fusion = f32[32,1,32,64]{3,2,1,0:T(8,128)S(1)} fusion(f32[32,64,256]{2,1,0:T(8,128)S(1)} %bitcast.98, f32[32,256]{1,0:T(8,128)S(1)} %reduce_sum.43), kind=kOutput, calls=%fused_computation | convolution fusion | flops 201326592 | bytes 2392064 | tf_op jit(solution)/shard_map/bvn,cn->bvc/dot_general | solution.py:91
  260.8 22.9 %all_to_all.51 = f32[32,1,2048]{2,1,0:T(1,128)S(1)} all-to-all(f32[32,1,2048]{2,1,0:T(1,128)S(1)} %reshape.144), channel_id=1, replica_groups=mesh['pts_0'=2,'pts_1'=8,'pts_2'=2,'val'=16] {'pts_0','pts_1','pts_2'}, dimensions={0} | all-to-all | bytes 524288 | tf_op jit(solution)/shard_map/all_to_all | solution.py:53
  (43 shorter events, 21.7 us)
Async XLA Ops:
  42.9 7.0 %copy-start.3 = (f32[16,512]{1,0:T(8,128)S(1)}, f32[16,512]{1,0:T(8,128)}, u32[]{:S(2)}) copy-start(f32[16,512]{1,0:T(8,128)} %param.9) | copy-start | bytes 98308
  42.9 58.9 %all-to-all-start.1 = ((f32[16,128,256]{2,1,0:T(8,128)}), f32[16,128,256]{2,1,0:T(8,128)S(1)}, u32[]{:S(2)}, u32[]{:S(2)}) async-start(f32[16,128,256]{2,1,0:T(8,128)} %broadcast_in_dim.20), calls=%async_computation.1 | async-start | bytes 4194304 | tf_op jit(solution)/shard_map/all_to_all | solution.py:23
  49.9 69.9 %all-gather.3.cloned.1.call-start = ((), (), s32[]{:S(2)}) async-start(), calls=%async_computation.9 | async-start | bytes 1572864 | tf_op jit(solution)/shard_map/all_gather | solution.py:35
  99.7 16.1 %copy-start.1 = (f32[512,256]{1,0:T(8,128)S(1)}, f32[512,256]{1,0:T(8,128)}, u32[]{:S(2)}) copy-start(f32[512,256]{1,0:T(8,128)} %param.11) | copy-start | bytes 1572868
  103.8 25.2 %all-to-all-start.2 = ((f32[16,1,32,256]{3,2,1,0:T(8,128)}), f32[16,1,32,256]{3,2,1,0:T(8,128)}, u32[]{:S(2)}, u32[]{:S(2)}) async-start(f32[16,1,32,256]{3,2,1,0:T(8,128)} %broadcast_in_dim.21), calls=%async_computation.2 | async-start | bytes 1048576 | tf_op jit(solution)/shard_map/all_to_all | solution.py:23
  158.5 28.7 %copy-start.2 = (f32[1,32,64]{2,1,0:T(8,128)S(1)}, f32[1,32,64]{2,1,0:T(8,128)}, u32[]{:S(2)}) copy-start(f32[1,32,64]{2,1,0:T(8,128)} %param.6) | copy-start | bytes 24580
  158.5 28.7 %copy-start.4 = (f32[32]{0:T(128)S(1)}, f32[32]{0:T(128)}, u32[]{:S(2)}) copy-start(f32[32]{0:T(128)} %param.7) | copy-start | bytes 388
  158.5 28.7 %copy-start.5 = (f32[64]{0:T(128)S(1)}, f32[64]{0:T(128)}, u32[]{:S(2)}) copy-start(f32[64]{0:T(128)} %param.8) | copy-start | bytes 772
  217.0 18.3 %copy-start = (f32[512,256]{0,1:T(8,128)S(1)}, f32[512,256]{0,1:T(8,128)}, u32[]{:S(2)}) copy-start(f32[512,256]{0,1:T(8,128)} %copy.17) | copy-start | bytes 1572868
Sparse Core Ops, SparseCore 0:
  97.3 22.4 all-gather.2
where the time goes:
time: 294 us; the launch traced here: 293 us
  blocking collectives  200 us (68%)
  local copies, waits for them, and re-layouts  20.9 us (7%)
  starting transfers between devices  19 us (6%)
  matrix products  15.9 us (5%)
  between operations  13.6 us (5%)
  waiting for transfers between devices  13.1 us (4%)
  other arithmetic  9.98 us (3%)
    all_to_all x4, blocking collectives, sent_and_summed(): lax.all_to_all(in_blocks(array, dim, peers), axis, 0, 0, tiled=True)  82.4 us
    all_to_all x3, blocking collectives, copy_for_each(): lax.all_to_all(jnp.broadcast_to(array[None], (peers, *array.shape)), axis...  70.7 us
    all_gather x1, blocking collectives, stacked_from(): blocks = lax.all_gather(blocks, axes[k], axis=0, tiled=True)  47.2 us
    all_to_all x2, starting transfers between devices, copy_for_each(): lax.all_to_all(jnp.broadcast_to(array[None], (peers, *array.shape)), axis...  19 us
    all_to_all x2, waiting for transfers between devices, copy_for_each(): lax.all_to_all(jnp.broadcast_to(array[None], (peers, *array.shape)), axis...  10.1 us
    unnamed x21, local copies, waits for them, and re-layouts  6.91 us
    dot_general x2, matrix products, per_device(): jnp.einsum('bvn,cn->bvc', back, cond_whole, precision=highest, preferred_...  6.69 us
  transfers between devices with their start and end apart: 3, of which 3 were waited for; matrix products, arithmetic and copies ran while one was open for 2% of the time, Pallas kernels for 0%

commit v1 on v0

v1 whole, which is shorter than its diff:
```python
import functools

import jax
import jax.numpy as jnp
from jax import lax
from jax.experimental import pallas as pl
from jax.experimental.pallas import tpu as pltpu
from jax.sharding import Mesh
from jax.sharding import PartitionSpec as P

ITERS = 2
CENTER = 2.2
HALF_WIDTH = 2.0

ROWS = ("zh", "y")
PTS = ("zh", "y", "core")
VAL = ("zl", "x")

F32 = jnp.float32
BF16 = jnp.bfloat16
PARAMS = pltpu.CompilerParams(vmem_limit_bytes=20 * 1024 * 1024)


def split(a):
    hi = a.astype(BF16)
    return hi, (a - hi.astype(F32)).astype(BF16)


def dot(a, b):
    return jnp.dot(a, b, preferred_element_type=F32)


def dot_nt(a, b):
    return lax.dot_general(a, b, (((1,), (1,)), ((), ())), preferred_element_type=F32)


def exchange(blocks, axes):
    return lax.all_to_all(blocks, axes, 0, 0, tiled=True)


def copied(array, axes):
    return exchange(jnp.broadcast_to(array[None], (lax.axis_size(axes), *array.shape)), axes)


def packed(block):
    half = block.shape[0] // 2
    return jnp.concatenate([block[:half], block[half:]], axis=1)


def join_pairs(gathered_ref, xh_ref, xl_ref, order):
    half, width = gathered_ref.shape[1:]
    left = lax.broadcasted_iota(jnp.int32, (half, width), 1) < width // 2
    for q, place in enumerate(order):
        a, b = gathered_ref[2 * q], gathered_ref[2 * q + 1]
        upper = jnp.where(left, a, pltpu.roll(b, width // 2, 1))
        lower = jnp.where(left, pltpu.roll(a, width // 2, 1), b)
        cols = slice(place * width, (place + 1) * width)
        for part, rows in ((upper, slice(0, half)), (lower, slice(half, 2 * half))):
            hi, lo = split(part)
            xh_ref[rows, cols] = hi
            xl_ref[rows, cols] = lo


def pair_first_kernel(order, gathered_ref, cond_ref, pair_ref, ch_ref, cl_ref, xh_ref, xl_ref):
    join_pairs(gathered_ref, xh_ref, xl_ref, order)
    ch, cl = split(cond_ref[...])
    ch_ref[...] = ch
    cl_ref[...] = cl
    pair = dot(xh_ref[...], ch) + (dot(xh_ref[...], cl) + dot(xl_ref[...], ch))
    pair_ref[...] = jnp.broadcast_to(pair[None], pair_ref.shape)


def pair_kernel(order, gathered_ref, ch_ref, cl_ref, pair_ref, xh_ref, xl_ref):
    join_pairs(gathered_ref, xh_ref, xl_ref, order)
    ch, cl = ch_ref[...], cl_ref[...]
    pair = dot(xh_ref[...], ch) + (dot(xh_ref[...], cl) + dot(xl_ref[...], ch))
    pair_ref[...] = jnp.broadcast_to(pair[None], pair_ref.shape)


def orbitals_kernel(val_ref, vh_ref, vl_ref, th_ref, tl_ref):
    cores, chips, depth, _ = val_ref.shape
    for chip in range(chips):
        for core in range(cores):
            at = (chip * cores + core) * depth
            hi, lo = split(val_ref[core, chip])
            vh_ref[at : at + depth, :] = hi
            vl_ref[at : at + depth, :] = lo
    whole = jnp.concatenate(
        [val_ref[core, chip] for chip in range(chips) for core in range(cores)], axis=0
    )
    hi, lo = split(whole.T)
    th_ref[...] = hi
    tl_ref[...] = lo


def screen_kernel(pair_ref, screened_ref, vh_ref, vl_ref, th_ref, tl_ref, back_ref):
    ph, pl_ = split(pair_ref[...])
    mixed = dot(th_ref[...], ph) + (dot(th_ref[...], pl_) + dot(tl_ref[...], ph))
    wh, wl = split(mixed * screened_ref[...])
    back_ref[...] = dot(vh_ref[...], wh) + (dot(vh_ref[...], wl) + dot(vl_ref[...], wh))


def direct_kernel(order, terms_ref, ch_ref, cl_ref, out_ref):
    bh, bl = split(jnp.sum(terms_ref[...], axis=0))
    ch, cl = ch_ref[...], cl_ref[...]
    direct = dot_nt(bh, ch) + (dot_nt(bl, ch) + dot_nt(bh, cl))
    half, width = out_ref.shape[1:]
    left = lax.broadcasted_iota(jnp.int32, (half, width), 1) < width // 2
    for q, place in enumerate(order):
        upper = direct[:half, place * width : (place + 1) * width]
        lower = direct[half:, place * width : (place + 1) * width]
        out_ref[2 * q] = jnp.where(left, upper, pltpu.roll(lower, width // 2, 1))
        out_ref[2 * q + 1] = jnp.where(left, pltpu.roll(upper, width // 2, 1), lower)


def scaled(terms_ref, vec, ediff_ref):
    hamil = ediff_ref[...] * vec - jnp.sum(terms_ref[...], axis=0)
    return (hamil - CENTER * vec) / HALF_WIDTH


def first_kernel(terms_ref, vec_ref, ediff_ref, new_ref, copies_ref):
    new = scaled(terms_ref, vec_ref[...], ediff_ref)
    new_ref[...] = new
    copies_ref[...] = jnp.broadcast_to(new[None], copies_ref.shape)


def last_kernel(terms_ref, vec_ref, older_ref, ediff_ref, out_ref):
    new = 2.0 * scaled(terms_ref, vec_ref[...], ediff_ref) - older_ref[...]
    half, width = new.shape
    out_ref[:half, :] = new[:, : width // 2]
    out_ref[half:, :] = new[:, width // 2 :]


def call(kernel, out_shapes, scratch=()):
    shapes = [jax.ShapeDtypeStruct(s, d) for s, d in out_shapes]
    return pl.pallas_call(
        kernel,
        out_shape=shapes if len(shapes) > 1 else shapes[0],
        scratch_shapes=[pltpu.VMEM(s, d) for s, d in scratch],
        compiler_params=PARAMS,
    )


def per_device(vectors, eval_energy, cond_energy, val_orbitals, cond_orbitals, screened):
    _, rows, cols = vectors.shape
    pts, val = lax.axis_size(PTS), lax.axis_size(VAL)
    nzl, nx = lax.axis_size("zl"), lax.axis_size("x")
    depth_c, points_c = cond_orbitals.shape
    depth_v, points_v = val_orbitals.shape
    nv, nc = rows * val, cols * pts
    half, width = rows // 2, cols * 2
    order = [x * nzl + zl for zl in range(nzl) for x in range(nx)]

    older = packed(vectors[0])
    ediff = packed(cond_energy[None, :] - eval_energy[:, None])

    cond_zl = copied(cond_orbitals, "zl")
    gathered = copied(older, PTS)
    val_chips = copied(val_orbitals, ROWS)
    cond_all = copied(cond_zl.reshape(nzl * depth_c, points_c), "x").reshape(nc, points_c)
    val_all = copied(val_chips, "core")
    vh, vl, th, tl = call(
        orbitals_kernel, [((nv, points_v), BF16)] * 2 + [((points_v, nv), BF16)] * 2
    )(val_all)

    newer = older
    for step in range(ITERS):
        scratch = [((rows, nc), BF16)] * 2
        if step == 0:
            pair, ch, cl = call(
                functools.partial(pair_first_kernel, order),
                [((val, rows, points_c), F32), ((nc, points_c), BF16), ((nc, points_c), BF16)],
                scratch,
            )(gathered, cond_all)
        else:
            pair = call(
                functools.partial(pair_kernel, order), [((val, rows, points_c), F32)], scratch
            )(gathered, ch, cl)
        pair_all = exchange(pair, VAL).reshape(nv, points_c)
        back = call(screen_kernel, [((nv, points_c), F32)])(pair_all, screened, vh, vl, th, tl)
        back = exchange(back.reshape(val, rows, points_c), VAL)
        direct = call(functools.partial(direct_kernel, order), [((pts, half, width), F32)])(
            back, ch, cl
        )
        direct = exchange(direct, PTS)
        if step < ITERS - 1:
            newer, copies = call(
                first_kernel, [((half, width), F32), ((pts, half, width), F32)]
            )(direct, older, ediff)
            gathered = exchange(copies, PTS)
    out = call(last_kernel, [((rows, cols), F32)])(direct, newer, older, ediff)
    return out[None]


def solution(mesh):
    torus = Mesh(mesh.devices.reshape(2, 8, 2, 4, 4), ("zh", "y", "core", "zl", "x"))
    placed = (P(None, VAL, PTS), P(VAL), P(PTS), P(PTS, VAL), P(VAL, PTS), P(VAL, PTS))
    return jax.shard_map(
        per_device, mesh=torus, in_specs=placed, out_specs=P(None, VAL, PTS), check_vma=False
    )
```

time: 294 us -> 267 us (0.908)
  matrix products: 15.9 us -> 0 us
  waiting for transfers between devices: 13.1 us -> 26.9 us
  between operations: 13.6 us -> 0.19 us
  Pallas kernels: 0 us -> 10.2 us
  other arithmetic: 9.98 us -> 0.23 us
  blocking collectives: 200 us -> 193 us
  local copies, waits for them, and re-layouts: 20.9 us -> 13.9 us
    all_gather x1 -> x0, blocking collectives: 47.2 us -> none  [stacked_from(): blocks = lax.all_gather(blocks, axes[k], axis=0, tiled=True)]
    all_to_all x7 -> x9, blocking collectives: 153 us -> 193 us  [exchange(): return lax.all_to_all(blocks, axes, 0, 0, tiled=True)]
    all_to_all x2 -> x3, waiting for transfers between devices: 10.1 us -> 26.9 us  [exchange(): return lax.all_to_all(blocks, axes, 0, 0, tiled=True)]
    dot_general x8 -> x0, matrix products: 15.9 us -> none  [the longest x2 6.69 us: per_device(): jnp.einsum('bvn,cn->bvc', back, cond_whole, precision=highest, preferred_...]
    pallas_call x0 -> x9, Pallas kernels: none -> 10.2 us  [the longest x2 4.67 us: per_device(): call(screen_kernel, [((nv, points_c), F32)])]
    transpose x5 -> x0, local copies, waits for them, and re-layouts: 7.06 us -> none  [the longest x2 3.29 us: per_device(): jnp.einsum('vm,bmn->bvn', val_whole, weighted, precision=highest, preferr...]
    all_to_all x4 -> x0, other arithmetic: 6.95 us -> none  [the longest x2 3.48 us: sent_and_summed(): lax.all_to_all(in_blocks(array, dim, peers), axis, 0, 0, tiled=True)]
    unnamed x21 -> x38, local copies, waits for them, and re-layouts: 6.91 us -> 10.8 us
  transfers between devices with their start and end apart: 3 -> 3, of which waited for: 3 -> 2; matrix products, arithmetic and copies ran while one was open for 2% -> 0% of each run, Pallas kernels for 0% -> 0%
where the time goes in v1:
time: 267 us; the launch traced here: 266 us
  blocking collectives  193 us (72%)
  waiting for transfers between devices  26.9 us (10%)
  starting transfers between devices  21.7 us (8%)
  local copies, waits for them, and re-layouts  13.9 us (5%)
  Pallas kernels  10.2 us (4%)
    all_to_all x9, blocking collectives, exchange(): return lax.all_to_all(blocks, axes, 0, 0, tiled=True)  193 us
    all_to_all x3, waiting for transfers between devices, exchange(): return lax.all_to_all(blocks, axes, 0, 0, tiled=True)  26.9 us
    all_to_all x3, starting transfers between devices, exchange(): return lax.all_to_all(blocks, axes, 0, 0, tiled=True)  21.7 us
    unnamed x38, local copies, waits for them, and re-layouts  10.8 us
  transfers between devices with their start and end apart: 3, of which 2 were waited for; matrix products, arithmetic and copies ran while one was open for 0% of the time, Pallas kernels for 0%

profile of v1, /device:TPU:1, one launch (start us, length us, event | category | flops | bytes accessed | tf_op | source)
XLA Modules:
  0.0 266.4 jit_solution(7184390078147094619)
XLA Ops:
  0.8 32.8 %all_to_all.60.gathered_ref = f32[32,16,128]{2,1,0:T(8,128)S(1)} all-to-all(f32[32,16,128]{2,1,0:T(8,128)S(1)} %broadcast_in_dim.14), channel_id=1, replica_groups=mesh['zh'=2,'y'=8,'core'=2,'zl'=4,'x'=4] {'zh','y','core'}, dimensions={0} | all-to-all | bytes 524288 | tf_op jit(solution)/shard_map/all_to_all | solution.py:38
  34.6 17.6 %all_to_all.61 = f32[4,128,256]{2,1,0:T(8,128)S(1)} all-to-all(f32[4,128,256]{2,1,0:T(8,128)S(1)} %broadcast_in_dim.15), channel_id=1, replica_groups=mesh['zh'=2,'y'=8,'core'=2,'zl'=4,'x'=4] {'zl'}, dimensions={0} | all-to-all | bytes 1048576 | tf_op jit(solution)/shard_map/all_to_all | solution.py:38
  52.3 20.0 %all_to_all.62 = f32[16,16,512]{2,1,0:T(8,128)S(1)} all-to-all(f32[16,16,512]{2,1,0:T(8,128)S(1)} %broadcast_in_dim.18), channel_id=1, replica_groups=mesh['zh'=2,'y'=8,'core'=2,'zl'=4,'x'=4] {'zh','y'}, dimensions={0} | all-to-all | bytes 1048576 | tf_op jit(solution)/shard_map/all_to_all | solution.py:38
  72.5 26.6 %all_to_all.63 = f32[4,512,256]{2,1,0:T(8,128)} all-to-all(f32[4,512,256]{2,1,0:T(8,128)S(1)} %broadcast_in_dim.17), channel_id=1, replica_groups=mesh['zh'=2,'y'=8,'core'=2,'zl'=4,'x'=4] {'x'}, dimensions={0} | all-to-all | bytes 4194304 | tf_op jit(solution)/shard_map/all_to_all | solution.py:38
  99.1 1.1 broadcast_in_dim.19
  100.2 8.2 %all-to-all-start.5 = ((f32[2,16,16,512]{3,2,1,0:T(8,128)}), f32[2,16,16,512]{3,2,1,0:T(8,128)S(1)}, u32[]{:S(2)}, u32[]{:S(2)}) async-start(f32[2,16,16,512]{3,2,1,0:T(8,128)} %broadcast_in_dim.19), calls=%async_computation.5 | async-start | bytes 2097152 | tf_op jit(solution)/shard_map/all_to_all | solution.py:38
  108.4 1.6 copy-done
  111.6 4.2 %all-to-all-start.3 = ((f32[16,32,256]{2,1,0:T(8,128)}), f32[16,32,256]{2,1,0:T(8,128)}, u32[]{:S(2)}, u32[]{:S(2)}) async-start(f32[16,32,256]{2,1,0:T(8,128)} %copy-done.15), calls=%async_computation.3 | async-start | bytes 1048576 | tf_op jit(solution)/shard_map/all_to_all | solution.py:38
  119.5 11.2 %all-to-all-done.3 = f32[16,32,256]{2,1,0:T(8,128)} async-done(((f32[16,32,256]{2,1,0:T(8,128)}), f32[16,32,256]{2,1,0:T(8,128)}, u32[]{:S(2)}, u32[]{:S(2)}) %all-to-all-start.3) | async-done | bytes 524320 | tf_op jit(solution)/shard_map/all_to_all | solution.py:38
  130.7 1.0 copy-done.1
  132.8 1.0 copy-done.7
  133.8 1.0 copy-done.10
  134.9 1.0 copy-done.13
  135.9 2.9 %shard_map.66 = f32[512,256]{1,0:T(8,128)S(1)} custom-call(f32[512,256]{1,0:T(8,128)} %bitcast.4.pair_ref, f32[512,256]{1,0:T(8,128)S(1)} %copy-done.1, bf16[512,512]{1,0:T(8,128)(2,1)S(1)} %copy-done.4, bf16[512,512]{1,0:T(8,128)(2,1)S(1)} %copy-done.7, bf16[512,512]{1,0:T(8,128)(2,1)S(1)} %copy-done.10, bf16[512,512]{1,0:T(8,128)(2,1)S(1)} %copy-done.13), custom_call_target="tpu_custom_call" | custom-call | tf_op jit(solution)/shard_map/pallas_call | solution.py:180
  138.8 17.9 %all_to_all.64.terms_ref = f32[16,32,256]{2,1,0:T(8,128)S(1)} all-to-all(f32[16,32,256]{2,1,0:T(8,128)S(1)} %bitcast.14), channel_id=1, replica_groups=mesh['zh'=2,'y'=8,'core'=2,'zl'=4,'x'=4] {'zl','x'}, dimensions={0} | all-to-all | bytes 1048576 | tf_op jit(solution)/shard_map/all_to_all | solution.py:38
  156.7 1.8 shard_map.67
  158.5 9.3 %all-to-all-start.7 = ((f32[32,16,128]{2,1,0:T(8,128)}), f32[32,16,128]{2,1,0:T(8,128)S(1)}, u32[]{:S(2)}, u32[]{:S(2)}) async-start(f32[32,16,128]{2,1,0:T(8,128)} %shard_map.67), calls=%async_computation.7 | async-start | bytes 524288 | tf_op jit(solution)/shard_map/all_to_all | solution.py:38
  167.9 15.6 %all-to-all-done.7.terms_ref = f32[32,16,128]{2,1,0:T(8,128)S(1)} async-done(((f32[32,16,128]{2,1,0:T(8,128)}), f32[32,16,128]{2,1,0:T(8,128)S(1)}, u32[]{:S(2)}, u32[]{:S(2)}) %all-to-all-start.7) | async-done | bytes 262176 | tf_op jit(solution)/shard_map/all_to_all | solution.py:38
  183.6 20.1 %all_to_all.65.gathered_ref = f32[32,16,128]{2,1,0:T(8,128)S(1)} all-to-all(f32[32,16,128]{2,1,0:T(8,128)S(1)} %get-tuple-element.21), channel_id=1, replica_groups=mesh['zh'=2,'y'=8,'core'=2,'zl'=4,'x'=4] {'zh','y','core'}, dimensions={0} | all-to-all | bytes 524288 | tf_op jit(solution)/shard_map/all_to_all | solution.py:38
  204.5 17.2 %all_to_all.66 = f32[16,32,256]{2,1,0:T(8,128)S(1)} all-to-all(f32[16,32,256]{2,1,0:T(8,128)S(1)} %shard_map.69), channel_id=1, replica_groups=mesh['zh'=2,'y'=8,'core'=2,'zl'=4,'x'=4] {'zl','x'}, dimensions={0} | all-to-all | bytes 1048576 | tf_op jit(solution)/shard_map/all_to_all | solution.py:38
  221.7 1.8 shard_map.70
  223.6 18.1 %all_to_all.67.terms_ref = f32[16,32,256]{2,1,0:T(8,128)S(1)} all-to-all(f32[16,32,256]{2,1,0:T(8,128)S(1)} %bitcast.13), channel_id=1, replica_groups=mesh['zh'=2,'y'=8,'core'=2,'zl'=4,'x'=4] {'zl','x'}, dimensions={0} | all-to-all | bytes 1048576 | tf_op jit(solution)/shard_map/all_to_all | solution.py:38
  241.7 1.1 shard_map.71
  242.8 22.9 %all_to_all.68.terms_ref = f32[32,16,128]{2,1,0:T(8,128)S(1)} all-to-all(f32[32,16,128]{2,1,0:T(8,128)S(1)} %shard_map.71), channel_id=1, replica_groups=mesh['zh'=2,'y'=8,'core'=2,'zl'=4,'x'=4] {'zh','y','core'}, dimensions={0} | all-to-all | bytes 524288 | tf_op jit(solution)/shard_map/all_to_all | solution.py:38
  (48 shorter events, 9.9 us)
Async XLA Ops:
  0.0 52.2 %copy-start.16 = (f32[16,512]{1,0:T(8,128)S(1)}, f32[16,512]{1,0:T(8,128)}, u32[]{:S(2)}) copy-start(f32[16,512]{1,0:T(8,128)} %param.9) | copy-start | bytes 98308
  100.2 11.3 %all-to-all-start.5 = ((f32[2,16,16,512]{3,2,1,0:T(8,128)}), f32[2,16,16,512]{3,2,1,0:T(8,128)S(1)}, u32[]{:S(2)}, u32[]{:S(2)}) async-start(f32[2,16,16,512]{3,2,1,0:T(8,128)} %broadcast_in_dim.19), calls=%async_computation.5 | async-start | bytes 2097152 | tf_op jit(solution)/shard_map/all_to_all | solution.py:38
  108.4 1.6 copy-start
  110.7 0.8 copy-start.15
  111.6 19.1 %all-to-all-start.3 = ((f32[16,32,256]{2,1,0:T(8,128)}), f32[16,32,256]{2,1,0:T(8,128)}, u32[]{:S(2)}, u32[]{:S(2)}) async-start(f32[16,32,256]{2,1,0:T(8,128)} %copy-done.15), calls=%async_computation.3 | async-start | bytes 1048576 | tf_op jit(solution)/shard_map/all_to_all | solution.py:38
  116.2 0.8 copy-start.3
  117.0 0.8 copy-start.6
  117.9 0.8 copy-start.9
  118.7 0.8 copy-start.12
  130.7 1.0 copy-start.1
  131.7 1.0 copy-start.4
  132.8 1.0 copy-start.7
  133.8 1.0 copy-start.10
  134.9 1.0 copy-start.13
  138.8 29.0 %copy-start.17 = (f32[32]{0:T(128)S(1)}, f32[32]{0:T(128)}, u32[]{:S(2)}) copy-start(f32[32]{0:T(128)} %param.7) | copy-start | bytes 388
  138.8 29.0 %copy-start.18 = (f32[64]{0:T(128)S(1)}, f32[64]{0:T(128)}, u32[]{:S(2)}) copy-start(f32[64]{0:T(128)} %param.8) | copy-start | bytes 772
  158.5 25.1 %all-to-all-start.7 = ((f32[32,16,128]{2,1,0:T(8,128)}), f32[32,16,128]{2,1,0:T(8,128)S(1)}, u32[]{:S(2)}, u32[]{:S(2)}) async-start(f32[32,16,128]{2,1,0:T(8,128)} %shard_map.67), calls=%async_computation.7 | async-start | bytes 524288 | tf_op jit(solution)/shard_map/all_to_all | solution.py:38
  203.7 18.0 %copy-start.2 = (f32[512,256]{1,0:T(8,128)S(1)}, f32[512,256]{1,0:T(8,128)}, u32[]{:S(2)}) copy-start(f32[512,256]{1,0:T(8,128)} %screened_ref.3) | copy-start | bytes 1572868
  203.7 18.0 %copy-start.5 = (bf16[512,512]{1,0:T(8,128)(2,1)S(1)}, bf16[512,512]{1,0:T(8,128)(2,1)}, u32[]{:S(2)}) copy-start(bf16[512,512]{1,0:T(8,128)(2,1)} %copy-done.3) | copy-start | bytes 1572868
  203.7 18.0 %copy-start.8 = (bf16[512,512]{1,0:T(8,128)(2,1)S(1)}, bf16[512,512]{1,0:T(8,128)(2,1)}, u32[]{:S(2)}) copy-start(bf16[512,512]{1,0:T(8,128)(2,1)} %copy-done.6) | copy-start | bytes 1572868
  203.7 18.0 %copy-start.11 = (bf16[512,512]{1,0:T(8,128)(2,1)S(1)}, bf16[512,512]{1,0:T(8,128)(2,1)}, u32[]{:S(2)}) copy-start(bf16[512,512]{1,0:T(8,128)(2,1)} %copy-done.9) | copy-start | bytes 1572868
  203.7 18.0 %copy-start.14 = (bf16[512,512]{1,0:T(8,128)(2,1)S(1)}, bf16[512,512]{1,0:T(8,128)(2,1)}, u32[]{:S(2)}) copy-start(bf16[512,512]{1,0:T(8,128)(2,1)} %copy-done.12) | copy-start | bytes 1572868

commit v2 on v1

v2 whole, which is shorter than its diff:
```python
import jax
import jax.numpy as jnp
from jax import lax
from jax.experimental import pallas as pl
from jax.experimental.pallas import tpu as pltpu
from jax.sharding import Mesh
from jax.sharding import PartitionSpec as P

ITERS = 2
CENTER = 2.2
HALF_WIDTH = 2.0

ROWS = ("zh", "y")
PTS = ("zh", "y", "core")
VAL = ("zl", "x")

NZ, NX = 4, 4
WIDTH = 128

F32 = jnp.float32
BF16 = jnp.bfloat16
PARAMS = pltpu.CompilerParams(vmem_limit_bytes=20 * 1024 * 1024)


def split(a):
    hi = a.astype(BF16)
    return hi, (a - hi.astype(F32)).astype(BF16)


def dot(a, b):
    return jnp.dot(a, b, preferred_element_type=F32)


def dot_nt(a, b):
    return lax.dot_general(a, b, (((1,), (1,)), ((), ())), preferred_element_type=F32)


def exchange(blocks, axes):
    return lax.all_to_all(blocks, axes, 0, 0, tiled=True)


def shifted(array, axis, by):
    n = lax.axis_size(axis)
    return lax.ppermute(array, axis, [(i, (i + by) % n) for i in range(n)])


def copied(array, axes):
    return exchange(jnp.broadcast_to(array[None], (lax.axis_size(axes), *array.shape)), axes)


def packed(block):
    half = block.shape[0] // 2
    return jnp.concatenate([block[:half], block[half:]], axis=1)


def place_pair(a, b, place, xh_ref, xl_ref):
    half, width = a.shape
    left = lax.broadcasted_iota(jnp.int32, (half, width), 1) < width // 2
    upper = jnp.where(left, a, pltpu.roll(b, width // 2, 1))
    lower = jnp.where(left, pltpu.roll(a, width // 2, 1), b)
    cols = slice(place * width, (place + 1) * width)
    for part, rows in ((upper, slice(0, half)), (lower, slice(half, 2 * half))):
        hi, lo = split(part)
        xh_ref[rows, cols] = hi
        xl_ref[rows, cols] = lo


def by_core(core, own, other):
    return jnp.where(core == 0, own, other), jnp.where(core == 0, other, own)


def begin_kernel(
    where_ref, own_hbm, other_hbm, ediff_ref, older_ref, mine_hbm, left_hbm, upper_hbm, lower_hbm, right_hbm,
    pair_ref, ch_ref, cl_ref, vh_ref, vl_ref, th_ref, tl_ref, ediff_out_ref, older_out_ref,
    own_ref, other_ref, cond_ref, xh_ref, xl_ref, sems,
):
    depth = mine_hbm.shape[0]
    part = upper_hbm.shape[0]
    copies = [
        pltpu.make_async_copy(own_hbm, own_ref, sems.at[0]),
        pltpu.make_async_copy(other_hbm, other_ref, sems.at[1]),
    ]
    at = 0
    for i, ref in enumerate((mine_hbm, left_hbm, upper_hbm, lower_hbm, right_hbm)):
        rows = ref.shape[0]
        copies.append(
            pltpu.make_async_copy(ref, cond_ref.at[pl.ds(at, rows)], sems.at[2 + i])
        )
        at += rows
    for copy in copies:
        copy.start()
    ediff_out_ref[...] = ediff_ref[...]
    older_out_ref[...] = older_ref[...]
    core = where_ref[NX * NZ]
    copies[0].wait()
    copies[1].wait()
    def slot_of(chip):
        return where_ref[NX * NZ + 1 + chip]

    for place in range(NX * NZ):
        q = slot_of(where_ref[place])
        own, other = own_ref[q][:, -WIDTH:], other_ref[q][:, -WIDTH:]
        place_pair(*by_core(core, own, other), place, xh_ref, xl_ref)
    points = vh_ref.shape[1]
    rows = []
    for chip in range(own_ref.shape[0]):
        q = slot_of(chip)
        rows.extend(by_core(core, own_ref[q][:, :points], other_ref[q][:, :points]))
    whole = jnp.concatenate(rows, axis=0)
    hi, lo = split(whole)
    vh_ref[...] = hi
    vl_ref[...] = lo
    hi, lo = split(whole.T)
    th_ref[...] = hi
    tl_ref[...] = lo
    for copy in copies[2:]:
        copy.wait()
    ch, cl = split(cond_ref[...])
    ch_ref[...] = ch
    cl_ref[...] = cl
    pair = dot(xh_ref[...], ch) + (dot(xh_ref[...], cl) + dot(xl_ref[...], ch))
    pair_ref[...] = jnp.broadcast_to(pair[None], pair_ref.shape)


def pair_kernel(where_ref, gathered_ref, ch_ref, cl_ref, pair_ref, xh_ref, xl_ref):
    for jx in range(NX):
        for jz in range(NZ):
            q = where_ref[jx * NZ + jz]
            place_pair(
                gathered_ref[2 * q], gathered_ref[2 * q + 1], jx * NZ + jz, xh_ref, xl_ref
            )
    ch, cl = ch_ref[...], cl_ref[...]
    pair = dot(xh_ref[...], ch) + (dot(xh_ref[...], cl) + dot(xl_ref[...], ch))
    pair_ref[...] = jnp.broadcast_to(pair[None], pair_ref.shape)


def screen_kernel(pair_ref, screened_ref, vh_ref, vl_ref, th_ref, tl_ref, back_ref):
    ph, pl_ = split(pair_ref[...])
    mixed = dot(th_ref[...], ph) + (dot(th_ref[...], pl_) + dot(tl_ref[...], ph))
    wh, wl = split(mixed * screened_ref[...])
    back_ref[...] = dot(vh_ref[...], wh) + (dot(vh_ref[...], wl) + dot(vl_ref[...], wh))


def direct_kernel(where_ref, terms_ref, ch_ref, cl_ref, out_ref):
    bh, bl = split(jnp.sum(terms_ref[...], axis=0))
    ch, cl = ch_ref[...], cl_ref[...]
    direct = dot_nt(bh, ch) + (dot_nt(bl, ch) + dot_nt(bh, cl))
    half, width = out_ref.shape[1:]
    left = lax.broadcasted_iota(jnp.int32, (half, width), 1) < width // 2
    for place in range(NX * NZ):
        q = where_ref[place]
        upper = direct[:half, place * width : (place + 1) * width]
        lower = direct[half:, place * width : (place + 1) * width]
        out_ref[2 * q] = jnp.where(left, upper, pltpu.roll(lower, width // 2, 1))
        out_ref[2 * q + 1] = jnp.where(left, pltpu.roll(upper, width // 2, 1), lower)


def scaled(terms_ref, vec, ediff_ref):
    hamil = ediff_ref[...] * vec - jnp.sum(terms_ref[...], axis=0)
    return (hamil - CENTER * vec) / HALF_WIDTH


def first_kernel(terms_ref, vec_ref, ediff_ref, new_ref, copies_ref):
    new = scaled(terms_ref, vec_ref[...], ediff_ref)
    new_ref[...] = new
    copies_ref[...] = jnp.broadcast_to(new[None], copies_ref.shape)


def last_kernel(terms_ref, vec_ref, older_ref, ediff_ref, out_ref):
    new = 2.0 * scaled(terms_ref, vec_ref[...], ediff_ref) - older_ref[...]
    half, width = new.shape
    out_ref[:half, :] = new[:, : width // 2]
    out_ref[half:, :] = new[:, width // 2 :]


def call(kernel, out_shapes, operands, scratch=(), far=()):
    shapes = [jax.ShapeDtypeStruct(s, d) for s, d in out_shapes]
    spaces = [pltpu.SMEM if a.dtype == jnp.int32 else pltpu.VMEM for a in operands]
    for i in far:
        spaces[i] = pltpu.HBM
        operands[i] = pltpu.with_memory_space_constraint(operands[i], pltpu.HBM)
    return pl.pallas_call(
        kernel,
        out_shape=shapes if len(shapes) > 1 else shapes[0],
        scratch_shapes=list(scratch),
        in_specs=[pl.BlockSpec(memory_space=space) for space in spaces],
        compiler_params=PARAMS,
    )(*operands)


def per_device(vectors, eval_energy, cond_energy, val_orbitals, cond_orbitals, screened):
    _, rows, cols = vectors.shape
    pts, val = lax.axis_size(PTS), lax.axis_size(VAL)
    depth_c, points_c = cond_orbitals.shape
    depth_v, points_v = val_orbitals.shape
    nv, nc = rows * val, cols * pts
    half, width = rows // 2, cols * 2

    x, core = lax.axis_index("x"), lax.axis_index("core")
    steps = jnp.arange(NX * NZ)
    chips = steps % NZ * NX + ((x - steps // NZ) & (NX - 1))
    ny = lax.axis_size("y")
    slots = steps % ny * 2 + (steps // ny ^ lax.axis_index("zh"))
    where = jnp.concatenate([chips, core[None], slots]).astype(jnp.int32)
    older = packed(vectors[0])
    ediff = packed(cond_energy[None, :] - eval_energy[:, None])

    mine = copied(cond_orbitals, "zl").reshape(-1, points_c)
    parcel = jnp.concatenate([val_orbitals, older], axis=1)
    parcel = jnp.concatenate([parcel, shifted(parcel, "zh", 1)], axis=0)
    mine, parcel = lax.optimization_barrier((mine, parcel))
    own = copied(parcel, "y").reshape(-1, depth_v, points_v + width)
    other = shifted(own, "core", 1)
    left, right = shifted(mine, "x", 1), shifted(mine, "x", -1)
    part = mine.shape[0] // 2
    upper, lower = shifted(left[:part], "x", 1), shifted(right[part:], "x", -1)

    newer = older
    scratch = [pltpu.VMEM((rows, nc), BF16)] * 2
    pair, ch, cl, vh, vl, th, tl, ediff, older = call(
        begin_kernel,
        [((val, rows, points_c), F32)]
        + [((nc, points_c), BF16)] * 2
        + [((nv, points_v), BF16)] * 2
        + [((points_v, nv), BF16)] * 2
        + [((half, width), F32)] * 2,
        [where, own, other, ediff, older, mine, left, upper, lower, right],
        [pltpu.VMEM(own.shape, F32)] * 2
        + [pltpu.VMEM((nc, points_c), F32)]
        + scratch
        + [pltpu.SemaphoreType.DMA((7,))],
        far=(1, 2, 5, 6, 7, 8, 9),
    )
    for step in range(ITERS):
        if step > 0:
            pair = call(
                pair_kernel,
                [((val, rows, points_c), F32)],
                [where, exchange(copies, PTS), ch, cl],
                scratch,
            )
        pair_all = exchange(pair, VAL).reshape(nv, points_c)
        back = call(
            screen_kernel, [((nv, points_c), F32)], [pair_all, screened, vh, vl, th, tl]
        )
        back = exchange(back.reshape(val, rows, points_c), VAL)
        direct = call(direct_kernel, [((pts, half, width), F32)], [where, back, ch, cl])
        direct = exchange(direct, PTS)
        if step < ITERS - 1:
            newer, copies = call(
                first_kernel,
                [((half, width), F32), ((pts, half, width), F32)],
                [direct, older, ediff],
            )
    out = call(last_kernel, [((rows, cols), F32)], [direct, newer, older, ediff])
    return out[None]


def solution(mesh):
    torus = Mesh(mesh.devices.reshape(2, 8, 2, 4, 4), ("zh", "y", "core", "zl", "x"))
    placed = (P(None, VAL, PTS), P(VAL), P(PTS), P(PTS, VAL), P(VAL, PTS), P(VAL, PTS))
    return jax.shard_map(
        per_device, mesh=torus, in_specs=placed, out_specs=P(None, VAL, PTS), check_vma=False
    )
```

time: 267 us -> 226 us (0.85)
  blocking collectives: 193 us -> 140 us
  starting transfers between devices: 21.7 us -> 40.6 us
  local copies, waits for them, and re-layouts: 13.9 us -> 5.07 us
    all_to_all x9 -> x7, blocking collectives: 193 us -> 140 us  [exchange(): return lax.all_to_all(blocks, axes, 0, 0, tiled=True)]
    ppermute x0 -> x6, starting transfers between devices: none -> 25.9 us  [shifted(): return lax.ppermute(array, axis, [(i, (i + by) % n) for i in range(n)])]
    all_to_all x3 -> x2, waiting for transfers between devices: 26.9 us -> 11.4 us  [exchange(): return lax.all_to_all(blocks, axes, 0, 0, tiled=True)]
    ppermute x0 -> x6, waiting for transfers between devices: none -> 15.4 us  [shifted(): return lax.ppermute(array, axis, [(i, (i + by) % n) for i in range(n)])]
    unnamed x38 -> x24, local copies, waits for them, and re-layouts: 10.8 us -> 2.32 us
    all_to_all x3 -> x2, starting transfers between devices: 21.7 us -> 14.8 us  [exchange(): return lax.all_to_all(blocks, axes, 0, 0, tiled=True)]
    pallas_call x9 -> x8, Pallas kernels: 10.2 us -> 12.2 us  [call(): pl.pallas_call(kernel, out_shape=shapes if len(shapes) > 1 else shapes[0]...]
  transfers between devices with their start and end apart: 3 -> 8, of which waited for: 2 -> 4; matrix products, arithmetic and copies ran while one was open for 0% -> 0% of each run, Pallas kernels for 0% -> 0%
where the time goes in v2:
time: 226 us; the launch traced here: 225 us
  blocking collectives  140 us (62%)
  starting transfers between devices  40.6 us (18%)
  waiting for transfers between devices  26.8 us (12%)
  Pallas kernels  12.2 us (5%)
  local copies, waits for them, and re-layouts  5.07 us (2%)
    all_to_all x7, blocking collectives, exchange(): return lax.all_to_all(blocks, axes, 0, 0, tiled=True)  140 us
    ppermute x6, starting transfers between devices, shifted(): return lax.ppermute(array, axis, [(i, (i + by) % n) for i in range(n)])  25.9 us
    ppermute x6, waiting for transfers between devices, shifted(): return lax.ppermute(array, axis, [(i, (i + by) % n) for i in range(n)])  15.4 us
    all_to_all x2, starting transfers between devices, exchange(): return lax.all_to_all(blocks, axes, 0, 0, tiled=True)  14.8 us
    pallas_call x8, Pallas kernels, call(): pl.pallas_call(kernel, out_shape=shapes if len(shapes) > 1 else shapes[0]...  12.2 us
    all_to_all x2, waiting for transfers between devices, exchange(): return lax.all_to_all(blocks, axes, 0, 0, tiled=True)  11.4 us
  transfers between devices with their start and end apart: 8, of which 4 were waited for; matrix products, arithmetic and copies ran while one was open for 0% of the time, Pallas kernels for 0%

profile of v2, /device:TPU:1, one launch (start us, length us, event | category | flops | bytes accessed | tf_op | source)
XLA Modules:
  0.0 225.0 jit_solution(17671105572635631305)
XLA Ops:
  0.0 1.7 broadcast_in_dim.9
  1.7 7.9 %all-to-all-start = ((f32[4,128,256]{2,1,0:T(8,128)}), f32[4,128,256]{2,1,0:T(8,128)S(1)}, u32[]{:S(2)}, u32[]{:S(2)}) async-start(f32[4,128,256]{2,1,0:T(8,128)} %broadcast_in_dim.9), calls=%async_computation | async-start | bytes 1048576 | tf_op jit(solution)/shard_map/all_to_all | solution.py:39
  10.5 7.9 %collective-permute-start = (f32[16,640]{1,0:T(8,128)S(1)}, f32[16,640]{1,0:T(8,128)S(1)}, u32[]{:S(2)}, u32[]{:S(2)}) collective-permute-start(f32[16,640]{1,0:T(8,128)S(1)} %pad_maximum_fusion.1), channel_id=1, source_target_pairs={{0,256},{256,0},{1,257},{257,1},{2,258},{258,2},{3,259},{259,3},{4... | collective-permute-start | bytes 122888 | tf_op jit(solution)/shard_map/ppermute | solution.py:44
  18.5 6.8 %collective-permute-done = f32[16,640]{1,0:T(8,128)S(1)} collective-permute-done((f32[16,640]{1,0:T(8,128)S(1)}, f32[16,640]{1,0:T(8,128)S(1)}, u32[]{:S(2)}, u32[]{:S(2)}) %collective-permute-start) | collective-permute-done | bytes 40992 | tf_op jit(solution)/shard_map/ppermute | solution.py:44
  26.3 6.8 %all-to-all-start.1 = ((f32[8,32,640]{2,1,0:T(8,128)}), f32[8,32,640]{2,1,0:T(8,128)S(1)}, u32[]{:S(2)}, u32[]{:S(2)}) async-start(f32[8,32,640]{2,1,0:T(8,128)} %broadcast_in_dim.10), calls=%async_computation.1 | async-start | bytes 1310720 | tf_op jit(solution)/shard_map/all_to_all | solution.py:39
  33.2 4.5 %collective-permute-start.4 = (f32[512,256]{1,0:T(8,128)S(1)}, f32[512,256]{1,0:T(8,128)S(1)}, u32[]{:S(2)}, u32[]{:S(2)}) collective-permute-start(f32[512,256]{1,0:T(8,128)S(1)} %bitcast.18), channel_id=1, source_target_pairs={{0,3},{1,0},{2,1},{3,2},{4,7},{5,4},{6,5},{7,6},{8,11},{9,8},{10,9... | collective-permute-start | bytes 1572872 | tf_op jit(solution)/shard_map/ppermute | solution.py:44
  37.7 1.9 collective-permute-start.2
  39.7 11.4 %all-to-all-done.1 = f32[8,32,640]{2,1,0:T(8,128)S(1)} async-done(((f32[8,32,640]{2,1,0:T(8,128)}), f32[8,32,640]{2,1,0:T(8,128)S(1)}, u32[]{:S(2)}, u32[]{:S(2)}) %all-to-all-start.1) | async-done | bytes 655392 | tf_op jit(solution)/shard_map/all_to_all | solution.py:39
  51.2 5.2 %collective-permute-start.1 = (f32[16,16,640]{2,1,0:T(8,128)S(1)}, f32[16,16,640]{2,1,0:T(8,128)S(1)}, u32[]{:S(2)}, u32[]{:S(2)}) collective-permute-start(f32[16,16,640]{2,1,0:T(8,128)S(1)} %bitcast.16), channel_id=1, source_target_pairs={{0,16},{16,0},{1,17},{17,1},{2,18},{18,2},{3,19},{19,3},{4,20},{20... | collective-permute-start | bytes 1966088 | tf_op jit(solution)/shard_map/ppermute | solution.py:44
  56.5 4.4 %collective-permute-start.5 = (f32[256,256]{1,0:T(8,128)S(1)}, f32[256,256]{1,0:T(8,128)S(1)}, u32[]{:S(2)}, u32[]{:S(2)}) collective-permute-start(f32[256,256]{1,0:T(8,128)S(1)} %slice.35), channel_id=1, source_target_pairs={{0,3},{1,0},{2,1},{3,2},{4,7},{5,4},{6,5},{7,6},{8,11},{9,8},{10,9... | collective-permute-start | bytes 786440 | tf_op jit(solution)/shard_map/ppermute | solution.py:44
  60.9 1.9 collective-permute-start.3
  63.1 3.5 %collective-permute-done.5.lower_hbm = f32[256,256]{1,0:T(8,128)S(1)} collective-permute-done((f32[256,256]{1,0:T(8,128)S(1)}, f32[256,256]{1,0:T(8,128)S(1)}, u32[]{:S(2)}, u32[]{:S(2)}) %collective-permute-start.5) | collective-permute-done | bytes 262176 | tf_op jit(solution)/shard_map/ppermute | solution.py:44
  66.6 5.1 %collective-permute-done.3.upper_hbm = f32[256,256]{1,0:T(8,128)S(1)} collective-permute-done((f32[256,256]{1,0:T(8,128)S(1)}, f32[256,256]{1,0:T(8,128)S(1)}, u32[]{:S(2)}, u32[]{:S(2)}) %collective-permute-start.3) | collective-permute-done | bytes 262176 | tf_op jit(solution)/shard_map/ppermute | solution.py:44
  73.2 3.2 %shard_map.64 = (f32[16,32,256]{2,1,0:T(8,128)S(1)}, bf16[2048,256]{1,0:T(8,128)(2,1)S(1)}, bf16[2048,256]{1,0:T(8,128)(2,1)S(1)}, bf16[512,512]{1,0:T(8,128)(2,...) custom-call(s32[33]{0:T(128)S(1)} %pad_add_fusion.where_ref, ...), custom_call_target="tpu_custom_call" | custom-call | tf_op jit(solution)/shard_map/pallas_call | solution.py:182
  76.4 18.4 %all_to_all.45 = f32[16,32,256]{2,1,0:T(8,128)S(1)} all-to-all(f32[16,32,256]{2,1,0:T(8,128)S(1)} %get-tuple-element.20), channel_id=1, replica_groups=mesh['zh'=2,'y'=8,'core'=2,'zl'=4,'x'=4] {'zl','x'}, dimensions={0} | all-to-all | bytes 1048576 | tf_op jit(solution)/shard_map/all_to_all | solution.py:39
  94.8 1.8 shard_map.65
  96.7 18.5 %all_to_all.46.terms_ref = f32[16,32,256]{2,1,0:T(8,128)S(1)} all-to-all(f32[16,32,256]{2,1,0:T(8,128)S(1)} %bitcast.15), channel_id=1, replica_groups=mesh['zh'=2,'y'=8,'core'=2,'zl'=4,'x'=4] {'zl','x'}, dimensions={0} | all-to-all | bytes 1048576 | tf_op jit(solution)/shard_map/all_to_all | solution.py:39
  116.8 24.5 %all_to_all.47.terms_ref = f32[32,16,128]{2,1,0:T(8,128)S(1)} all-to-all(f32[32,16,128]{2,1,0:T(8,128)S(1)} %shard_map.66), channel_id=1, replica_groups=mesh['zh'=2,'y'=8,'core'=2,'zl'=4,'x'=4] {'zh','y','core'}, dimensions={0} | all-to-all | bytes 524288 | tf_op jit(solution)/shard_map/all_to_all | solution.py:39
  141.3 20.1 %all_to_all.48.gathered_ref = f32[32,16,128]{2,1,0:T(8,128)S(1)} all-to-all(f32[32,16,128]{2,1,0:T(8,128)S(1)} %get-tuple-element.29), channel_id=1, replica_groups=mesh['zh'=2,'y'=8,'core'=2,'zl'=4,'x'=4] {'zh','y','core'}, dimensions={0} | all-to-all | bytes 524288 | tf_op jit(solution)/shard_map/all_to_all | solution.py:39
  162.7 17.1 %all_to_all.49 = f32[16,32,256]{2,1,0:T(8,128)S(1)} all-to-all(f32[16,32,256]{2,1,0:T(8,128)S(1)} %shard_map.68), channel_id=1, replica_groups=mesh['zh'=2,'y'=8,'core'=2,'zl'=4,'x'=4] {'zl','x'}, dimensions={0} | all-to-all | bytes 1048576 | tf_op jit(solution)/shard_map/all_to_all | solution.py:39
  179.8 1.8 shard_map.69
  181.6 18.1 %all_to_all.50.terms_ref = f32[16,32,256]{2,1,0:T(8,128)S(1)} all-to-all(f32[16,32,256]{2,1,0:T(8,128)S(1)} %bitcast.13), channel_id=1, replica_groups=mesh['zh'=2,'y'=8,'core'=2,'zl'=4,'x'=4] {'zl','x'}, dimensions={0} | all-to-all | bytes 1048576 | tf_op jit(solution)/shard_map/all_to_all | solution.py:39
  199.7 1.6 shard_map.70
  201.4 22.9 %all_to_all.51.terms_ref = f32[32,16,128]{2,1,0:T(8,128)S(1)} all-to-all(f32[32,16,128]{2,1,0:T(8,128)S(1)} %shard_map.70), channel_id=1, replica_groups=mesh['zh'=2,'y'=8,'core'=2,'zl'=4,'x'=4] {'zh','y','core'}, dimensions={0} | all-to-all | bytes 524288 | tf_op jit(solution)/shard_map/all_to_all | solution.py:39
  (44 shorter events, 7.5 us)
Async XLA Ops:
  1.7 7.9 %copy-start.9 = (f32[1,32,64]{2,1,0:T(8,128)S(1)}, f32[1,32,64]{2,1,0:T(8,128)}, u32[]{:S(2)}) copy-start(f32[1,32,64]{2,1,0:T(8,128)} %param.6) | copy-start | bytes 24580
  1.7 23.6 %all-to-all-start = ((f32[4,128,256]{2,1,0:T(8,128)}), f32[4,128,256]{2,1,0:T(8,128)S(1)}, u32[]{:S(2)}, u32[]{:S(2)}) async-start(f32[4,128,256]{2,1,0:T(8,128)} %broadcast_in_dim.9), calls=%async_computation | async-start | bytes 1048576 | tf_op jit(solution)/shard_map/all_to_all | solution.py:39
  9.7 0.8 copy-start.8
  10.5 14.8 %collective-permute-start = (f32[16,640]{1,0:T(8,128)S(1)}, f32[16,640]{1,0:T(8,128)S(1)}, u32[]{:S(2)}, u32[]{:S(2)}) collective-permute-start(f32[16,640]{1,0:T(8,128)S(1)} %pad_maximum_fusion.1), channel_id=1, source_target_pairs={{0,256},{256,0},{1,257},{257,1},{2,258},{258,2},{3,259},{259,3},{4... | collective-permute-start | bytes 122888 | tf_op jit(solution)/shard_map/ppermute | solution.py:44
  25.4 12.3 %copy-start.2 = (f32[4,128,256]{2,1,0:T(8,128)}, f32[4,128,256]{2,1,0:T(8,128)S(1)}, u32[]{:S(2)}) copy-start(f32[4,128,256]{2,1,0:T(8,128)S(1)} %all-to-all-done) | copy-start | bytes 1572868
  26.3 24.8 %all-to-all-start.1 = ((f32[8,32,640]{2,1,0:T(8,128)}), f32[8,32,640]{2,1,0:T(8,128)S(1)}, u32[]{:S(2)}, u32[]{:S(2)}) async-start(f32[8,32,640]{2,1,0:T(8,128)} %broadcast_in_dim.10), calls=%async_computation.1 | async-start | bytes 1310720 | tf_op jit(solution)/shard_map/all_to_all | solution.py:39
  33.2 6.5 %copy-start.10 = (f32[32]{0:T(128)S(1)}, f32[32]{0:T(128)}, u32[]{:S(2)}) copy-start(f32[32]{0:T(128)} %param.7) | copy-start | bytes 388
  33.2 6.5 %copy-start.11 = (f32[64]{0:T(128)S(1)}, f32[64]{0:T(128)}, u32[]{:S(2)}) copy-start(f32[64]{0:T(128)} %param.8) | copy-start | bytes 772
  33.2 23.2 %collective-permute-start.4 = (f32[512,256]{1,0:T(8,128)S(1)}, f32[512,256]{1,0:T(8,128)S(1)}, u32[]{:S(2)}, u32[]{:S(2)}) collective-permute-start(f32[512,256]{1,0:T(8,128)S(1)} %bitcast.18), channel_id=1, source_target_pairs={{0,3},{1,0},{2,1},{3,2},{4,7},{5,4},{6,5},{7,6},{8,11},{9,8},{10,9... | collective-permute-start | bytes 1572872 | tf_op jit(solution)/shard_map/ppermute | solution.py:44
  37.7 23.1 %collective-permute-start.2 = (f32[512,256]{1,0:T(8,128)S(1)}, f32[512,256]{1,0:T(8,128)S(1)}, u32[]{:S(2)}, u32[]{:S(2)}) collective-permute-start(f32[512,256]{1,0:T(8,128)S(1)} %bitcast.19), channel_id=1, source_target_pairs={{0,1},{1,2},{2,3},{3,0},{4,5},{5,6},{6,7},{7,4},{8,9},{9,10},{10,1... | collective-permute-start | bytes 1572872 | tf_op jit(solution)/shard_map/ppermute | solution.py:44
  51.2 20.4 %copy-start.1 = (f32[8,32,640]{2,1,0:T(8,128)}, f32[8,32,640]{2,1,0:T(8,128)S(1)}, u32[]{:S(2)}) copy-start(f32[8,32,640]{2,1,0:T(8,128)S(1)} %all-to-all-done.1) | copy-start | bytes 1966084
  51.2 20.4 %collective-permute-start.1 = (f32[16,16,640]{2,1,0:T(8,128)S(1)}, f32[16,16,640]{2,1,0:T(8,128)S(1)}, u32[]{:S(2)}, u32[]{:S(2)}) collective-permute-start(f32[16,16,640]{2,1,0:T(8,128)S(1)} %bitcast.16), channel_id=1, source_target_pairs={{0,16},{16,0},{1,17},{17,1},{2,18},{18,2},{3,19},{19,3},{4,20},{20... | collective-permute-start | bytes 1966088 | tf_op jit(solution)/shard_map/ppermute | solution.py:44
  56.4 15.2 %copy-start.3 = (f32[512,256]{1,0:T(8,128)}, f32[512,256]{1,0:T(8,128)S(1)}, u32[]{:S(2)}) copy-start(f32[512,256]{1,0:T(8,128)S(1)} %collective-permute-done.4.right_hbm) | copy-start | bytes 1572868
  56.5 10.1 %collective-permute-start.5 = (f32[256,256]{1,0:T(8,128)S(1)}, f32[256,256]{1,0:T(8,128)S(1)}, u32[]{:S(2)}, u32[]{:S(2)}) collective-permute-start(f32[256,256]{1,0:T(8,128)S(1)} %slice.35), channel_id=1, source_target_pairs={{0,3},{1,0},{2,1},{3,2},{4,7},{5,4},{6,5},{7,6},{8,11},{9,8},{10,9... | collective-permute-start | bytes 786440 | tf_op jit(solution)/shard_map/ppermute | solution.py:44
  60.9 10.8 %copy-start.4 = (f32[512,256]{1,0:T(8,128)}, f32[512,256]{1,0:T(8,128)S(1)}, u32[]{:S(2)}) copy-start(f32[512,256]{1,0:T(8,128)S(1)} %collective-permute-done.2.left_hbm) | copy-start | bytes 1572868
  60.9 10.7 %collective-permute-start.3 = (f32[256,256]{1,0:T(8,128)S(1)}, f32[256,256]{1,0:T(8,128)S(1)}, u32[]{:S(2)}, u32[]{:S(2)}) collective-permute-start(f32[256,256]{1,0:T(8,128)S(1)} %slice.34), channel_id=1, source_target_pairs={{0,1},{1,2},{2,3},{3,0},{4,5},{5,6},{6,7},{7,4},{8,9},{9,10},{10,1... | collective-permute-start | bytes 786440 | tf_op jit(solution)/shard_map/ppermute | solution.py:44
  66.5 5.1 %copy-start.6 = (f32[256,256]{1,0:T(8,128)}, f32[256,256]{1,0:T(8,128)S(1)}, u32[]{:S(2)}) copy-start(f32[256,256]{1,0:T(8,128)S(1)} %collective-permute-done.5.lower_hbm) | copy-start | bytes 786436
  71.6 0.7 copy-start.7
  72.3 0.9 copy-start.5
  76.4 18.4 %copy-start = (f32[512,256]{1,0:T(8,128)S(1)}, f32[512,256]{1,0:T(8,128)}, u32[]{:S(2)}) copy-start(f32[512,256]{1,0:T(8,128)} %screened_ref.3) | copy-start | bytes 1572868

commit v3 on v2

v3 whole, which is shorter than its diff:
```python
import jax
import jax.numpy as jnp
from jax import lax
from jax.experimental import pallas as pl
from jax.experimental.pallas import tpu as pltpu
from jax.sharding import Mesh
from jax.sharding import PartitionSpec as P

ITERS = 2
CENTER = 2.2
HALF_WIDTH = 2.0

ROWS = ("zh", "y")
PTS = ("zh", "y", "core")
Z, X = ("zl_hi", "zl_lo"), ("x_hi", "x_lo")
VAL = Z + X
CROSS = ("zh", "core")

NY, NZ, NX = 8, 4, 4
SEND = ("x_lo", "x_hi", "zl_lo", "zl_hi")
SENT = [int(f"{i:04b}"[::-1], 2) for i in range(NX * NZ)]

F32 = jnp.float32
BF16 = jnp.bfloat16
PARAMS = pltpu.CompilerParams(vmem_limit_bytes=20 * 1024 * 1024)


def split(a):
    hi = a.astype(BF16)
    return hi, (a - hi.astype(F32)).astype(BF16)


def dot(a, b):
    return jnp.dot(a, b, preferred_element_type=F32)


def dot_nt(a, b):
    return lax.dot_general(a, b, (((1,), (1,)), ((), ())), preferred_element_type=F32)


def exchange(blocks, axes):
    return lax.all_to_all(blocks, axes, 0, 0, tiled=True)


def shifted(array, axis, by):
    n = lax.axis_size(axis)
    if axis == CROSS:
        pairs = [(i, i ^ by) for i in range(n)]
    else:
        pairs = [(i, (i + by) % n) for i in range(n)]
    return lax.ppermute(array, axis, pairs)


def copied(array, axes):
    return exchange(jnp.broadcast_to(array[None], (lax.axis_size(axes), *array.shape)), axes)


def packed(block):
    half = block.shape[0] // 2
    return jnp.concatenate([block[:half], block[half:]], axis=1)


def place_pair(a, b, chip, xh_ref, xl_ref):
    half, width = a.shape
    left = lax.broadcasted_iota(jnp.int32, (half, width), 1) < width // 2
    upper = jnp.where(left, a, pltpu.roll(b, width // 2, 1))
    lower = jnp.where(left, pltpu.roll(a, width // 2, 1), b)
    cols = slice(chip * width, (chip + 1) * width)
    for part, rows in ((upper, slice(0, half)), (lower, slice(half, 2 * half))):
        hi, lo = split(part)
        xh_ref[rows, cols] = hi
        xl_ref[rows, cols] = lo


def collect(sources, target_ref, sems, first=0):
    copies = [
        pltpu.make_async_copy(source, target_ref.at[i], sems.at[first + i])
        for i, source in enumerate(sources)
    ]
    for copy in copies:
        copy.start()
    return copies


def begin_kernel(where_ref, ediff_ref, older_ref, own_hbm, other_hbm, *refs):
    conds, refs = refs[: NX + 1], refs[NX + 1 :]
    (pair_ref, ch_ref, cl_ref, vh_ref, vl_ref, th_ref, tl_ref, ediff_out_ref, older_out_ref,
     blocks_ref, cond_ref, xh_ref, xl_ref, block_sems, cond_sems) = refs
    parts = collect((own_hbm, other_hbm), blocks_ref, block_sems)
    part = conds[2].shape[0]
    places = [cond_ref.at[0], cond_ref.at[1], cond_ref.at[2, :part], cond_ref.at[2, part:]]
    conds = [
        pltpu.make_async_copy(ref, place, cond_sems.at[i])
        for i, (ref, place) in enumerate(zip(conds, places + [cond_ref.at[3]]))
    ]
    for copy in conds:
        copy.start()
    ediff_out_ref[...] = ediff_ref[...]
    older_out_ref[...] = older_ref[...]
    for copy in parts:
        copy.wait()
    points = vh_ref.shape[1]

    def block(p):
        return blocks_ref[where_ref[1 + p], where_ref[1 + 2 * NX * NZ + p // 2]]

    for q in range(NX * NZ):
        place_pair(block(2 * q)[:, points:], block(2 * q + 1)[:, points:], q, xh_ref, xl_ref)
    rows = [block(2 * q + half)[:, :points] for q in SENT for half in range(2)]
    whole = jnp.concatenate(rows, axis=0)
    hi, lo = split(whole)
    vh_ref[...] = hi
    vl_ref[...] = lo
    hi, lo = split(whole.T)
    th_ref[...] = hi
    tl_ref[...] = lo
    depth = cond_ref.shape[1] // NZ
    for copy in conds:
        copy.wait()
    for step in range(NX):
        for z in range(NZ):
            chip = z * NX + ((where_ref[0] - step) & (NX - 1))
            rows = pl.ds(pl.multiple_of(chip * depth, depth), depth)
            hi, lo = split(cond_ref[step, z * depth : (z + 1) * depth])
            ch_ref[rows, :] = hi
            cl_ref[rows, :] = lo
    multiply_pair(xh_ref, xl_ref, ch_ref, cl_ref, pair_ref)


def multiply_pair(xh_ref, xl_ref, ch_ref, cl_ref, pair_ref):
    ch, cl = ch_ref[...], cl_ref[...]
    pair = dot(xh_ref[...], ch) + (dot(xh_ref[...], cl) + dot(xl_ref[...], ch))
    pair_ref[...] = jnp.broadcast_to(pair[None], pair_ref.shape)


def pair_kernel(gathered_ref, ch_ref, cl_ref, pair_ref, xh_ref, xl_ref):
    for q in range(NX * NZ):
        place_pair(gathered_ref[2 * q], gathered_ref[2 * q + 1], q, xh_ref, xl_ref)
    multiply_pair(xh_ref, xl_ref, ch_ref, cl_ref, pair_ref)


def screen_kernel(pair_ref, screened_ref, vh_ref, vl_ref, th_ref, tl_ref, back_ref):
    ph, pl_ = split(pair_ref[...])
    mixed = dot(th_ref[...], ph) + (dot(th_ref[...], pl_) + dot(tl_ref[...], ph))
    wh, wl = split(mixed * screened_ref[...])
    back_ref[...] = dot(vh_ref[...], wh) + (dot(vh_ref[...], wl) + dot(vl_ref[...], wh))


def direct_kernel(terms_ref, ch_ref, cl_ref, out_ref):
    bh, bl = split(jnp.sum(terms_ref[...], axis=0))
    ch, cl = ch_ref[...], cl_ref[...]
    direct = dot_nt(bh, ch) + (dot_nt(bl, ch) + dot_nt(bh, cl))
    half, width = out_ref.shape[1:]
    left = lax.broadcasted_iota(jnp.int32, (half, width), 1) < width // 2
    for q in range(NX * NZ):
        upper = direct[:half, q * width : (q + 1) * width]
        lower = direct[half:, q * width : (q + 1) * width]
        out_ref[2 * q] = jnp.where(left, upper, pltpu.roll(lower, width // 2, 1))
        out_ref[2 * q + 1] = jnp.where(left, pltpu.roll(upper, width // 2, 1), lower)


def scaled(terms_ref, vec, ediff_ref):
    hamil = ediff_ref[...] * vec - jnp.sum(terms_ref[...], axis=0)
    return (hamil - CENTER * vec) / HALF_WIDTH


def first_kernel(terms_ref, vec_ref, ediff_ref, new_ref, copies_ref):
    new = scaled(terms_ref, vec_ref[...], ediff_ref)
    new_ref[...] = new
    copies_ref[...] = jnp.broadcast_to(new[None], copies_ref.shape)


def last_kernel(terms_ref, vec_ref, older_ref, ediff_ref, out_ref):
    new = 2.0 * scaled(terms_ref, vec_ref[...], ediff_ref) - older_ref[...]
    half, width = new.shape
    out_ref[:half, :] = new[:, : width // 2]
    out_ref[half:, :] = new[:, width // 2 :]


def call(kernel, out_shapes, operands, scratch=(), far=()):
    shapes = [jax.ShapeDtypeStruct(s, d) for s, d in out_shapes]
    spaces = [pltpu.SMEM if a.dtype == jnp.int32 else pltpu.VMEM for a in operands]
    for i in far:
        spaces[i] = pltpu.HBM
        operands[i] = pltpu.with_memory_space_constraint(operands[i], pltpu.HBM)
    return pl.pallas_call(
        kernel,
        out_shape=shapes if len(shapes) > 1 else shapes[0],
        scratch_shapes=list(scratch),
        in_specs=[pl.BlockSpec(memory_space=space) for space in spaces],
        compiler_params=PARAMS,
    )(*operands)


def per_device(vectors, eval_energy, cond_energy, val_orbitals, cond_orbitals, screened):
    _, rows, cols = vectors.shape
    pts, val = lax.axis_size(PTS), lax.axis_size(VAL)
    depth_c, points_c = cond_orbitals.shape
    depth_v, points_v = val_orbitals.shape
    nv, nc = rows * val, cols * pts
    half, width = rows // 2, cols * 2

    zh, core = lax.axis_index("zh"), lax.axis_index("core")
    p = jnp.arange(pts)
    chip = jnp.arange(val)
    where = [lax.axis_index(X)[None], (p & 1) ^ core, chip % NY * 2 + (chip // NY ^ zh)]
    where = jnp.concatenate(where).astype(jnp.int32)
    older = packed(vectors[0])
    ediff = packed(cond_energy[None, :] - eval_energy[:, None])

    mine = copied(cond_orbitals, Z).reshape(-1, points_c)
    parcel = jnp.concatenate([val_orbitals, older], axis=1)
    parcel = jnp.concatenate([parcel, shifted(parcel, "zh", 1)], axis=0)
    mine, parcel = lax.optimization_barrier((mine, parcel))
    own = copied(parcel, "y").reshape(-1, depth_v, points_v + width)
    other = shifted(own, "core", 1)
    left, right = shifted(mine, X, 1), shifted(mine, X, -1)
    part = mine.shape[0] // 2
    upper, lower = shifted(left[:part], X, 1), shifted(right[part:], X, -1)
    cond = [mine, left, upper, lower, right]

    newer = older
    scratch = [pltpu.VMEM((rows, nc), BF16)] * 2
    pair, ch, cl, vh, vl, th, tl, ediff, older = call(
        begin_kernel,
        [((val, rows, points_c), F32)]
        + [((nc, points_c), BF16)] * 2
        + [((nv, points_v), BF16)] * 2
        + [((points_v, nv), BF16)] * 2
        + [((half, width), F32)] * 2,
        [where, ediff, older, own, other, *cond],
        [pltpu.VMEM((2, *own.shape), F32), pltpu.VMEM((NX, *mine.shape), F32)]
        + scratch
        + [pltpu.SemaphoreType.DMA((2,)), pltpu.SemaphoreType.DMA((NX + 1,))],
        far=range(3, 6 + NX),
    )
    for step in range(ITERS):
        if step > 0:
            pair = call(
                pair_kernel,
                [((val, rows, points_c), F32)],
                [exchange(copies, PTS), ch, cl],
                scratch,
            )
        pair_all = exchange(pair, SEND).reshape(nv, points_c)
        back = call(
            screen_kernel, [((nv, points_c), F32)], [pair_all, screened, vh, vl, th, tl]
        )
        back = exchange(back.reshape(val, rows, points_c), SEND)
        direct = call(direct_kernel, [((pts, half, width), F32)], [back, ch, cl])
        direct = exchange(direct, PTS)
        if step < ITERS - 1:
            newer, copies = call(
                first_kernel,
                [((half, width), F32), ((pts, half, width), F32)],
                [direct, older, ediff],
            )
    out = call(last_kernel, [((rows, cols), F32)], [direct, newer, older, ediff])
    return out[None]


def solution(mesh):
    torus = Mesh(mesh.devices.reshape(2, 8, 2, 2, 2, 2, 2), PTS + Z + X)
    placed = (P(None, VAL, PTS), P(VAL), P(PTS), P(PTS, VAL), P(VAL, PTS), P(VAL, PTS))
    return jax.shard_map(
        per_device, mesh=torus, in_specs=placed, out_specs=P(None, VAL, PTS), check_vma=False
    )
```

time: 226 us -> 223 us (0.987)
  no operation moved by 1% of the time
where the time goes in v3:
time: 223 us; the launch traced here: 222 us
  blocking collectives  138 us (62%)
  starting transfers between devices  40.5 us (18%)
  waiting for transfers between devices  27 us (12%)
  Pallas kernels  11.1 us (5%)
  local copies, waits for them, and re-layouts  5.06 us (2%)
    all_to_all x7, blocking collectives, exchange(): return lax.all_to_all(blocks, axes, 0, 0, tiled=True)  138 us
    ppermute x6, starting transfers between devices, shifted(): return lax.ppermute(array, axis, pairs)  25.7 us
    ppermute x6, waiting for transfers between devices, shifted(): return lax.ppermute(array, axis, pairs)  15.4 us
    all_to_all x2, starting transfers between devices, exchange(): return lax.all_to_all(blocks, axes, 0, 0, tiled=True)  14.8 us
    all_to_all x2, waiting for transfers between devices, exchange(): return lax.all_to_all(blocks, axes, 0, 0, tiled=True)  11.6 us
    pallas_call x8, Pallas kernels, call(): pl.pallas_call(kernel, out_shape=shapes if len(shapes) > 1 else shapes[0]...  11.1 us
  transfers between devices with their start and end apart: 8, of which 4 were waited for; matrix products, arithmetic and copies ran while one was open for 0% of the time, Pallas kernels for 0%

profile of v3, /device:TPU:1, one launch (start us, length us, event | category | flops | bytes accessed | tf_op | source)
XLA Modules:
  0.0 221.9 jit_solution(18061559777997253269)
XLA Ops:
  0.0 1.7 broadcast_in_dim.9
  1.8 7.9 %all-to-all-start = ((f32[4,128,256]{2,1,0:T(8,128)}), f32[4,128,256]{2,1,0:T(8,128)S(1)}, u32[]{:S(2)}, u32[]{:S(2)}) async-start(f32[4,128,256]{2,1,0:T(8,128)} %broadcast_in_dim.9), calls=%async_computation | async-start | bytes 1048576 | tf_op jit(solution)/shard_map/all_to_all | solution.py:42
  10.5 7.9 %collective-permute-start = (f32[16,640]{1,0:T(8,128)S(1)}, f32[16,640]{1,0:T(8,128)S(1)}, u32[]{:S(2)}, u32[]{:S(2)}) collective-permute-start(f32[16,640]{1,0:T(8,128)S(1)} %pad_maximum_fusion.1), channel_id=1, source_target_pairs={{0,256},{256,0},{1,257},{257,1},{2,258},{258,2},{3,259},{259,3},{4... | collective-permute-start | bytes 122888 | tf_op jit(solution)/shard_map/ppermute | solution.py:51
  18.5 6.8 %collective-permute-done = f32[16,640]{1,0:T(8,128)S(1)} collective-permute-done((f32[16,640]{1,0:T(8,128)S(1)}, f32[16,640]{1,0:T(8,128)S(1)}, u32[]{:S(2)}, u32[]{:S(2)}) %collective-permute-start) | collective-permute-done | bytes 40992 | tf_op jit(solution)/shard_map/ppermute | solution.py:51
  26.3 6.8 %all-to-all-start.1 = ((f32[8,32,640]{2,1,0:T(8,128)}), f32[8,32,640]{2,1,0:T(8,128)S(1)}, u32[]{:S(2)}, u32[]{:S(2)}) async-start(f32[8,32,640]{2,1,0:T(8,128)} %broadcast_in_dim.10), calls=%async_computation.1 | async-start | bytes 1310720 | tf_op jit(solution)/shard_map/all_to_all | solution.py:42
  33.2 4.4 %collective-permute-start.4 = (f32[512,256]{1,0:T(8,128)S(1)}, f32[512,256]{1,0:T(8,128)S(1)}, u32[]{:S(2)}, u32[]{:S(2)}) collective-permute-start(f32[512,256]{1,0:T(8,128)S(1)} %bitcast.18), channel_id=1, source_target_pairs={{0,3},{1,0},{2,1},{3,2},{4,7},{5,4},{6,5},{7,6},{8,11},{9,8},{10,9... | collective-permute-start | bytes 1572872 | tf_op jit(solution)/shard_map/ppermute | solution.py:51
  37.6 1.9 collective-permute-start.2
  39.6 11.6 %all-to-all-done.1 = f32[8,32,640]{2,1,0:T(8,128)S(1)} async-done(((f32[8,32,640]{2,1,0:T(8,128)}), f32[8,32,640]{2,1,0:T(8,128)S(1)}, u32[]{:S(2)}, u32[]{:S(2)}) %all-to-all-start.1) | async-done | bytes 655392 | tf_op jit(solution)/shard_map/all_to_all | solution.py:42
  51.2 5.2 %collective-permute-start.1 = (f32[16,16,640]{2,1,0:T(8,128)S(1)}, f32[16,16,640]{2,1,0:T(8,128)S(1)}, u32[]{:S(2)}, u32[]{:S(2)}) collective-permute-start(f32[16,16,640]{2,1,0:T(8,128)S(1)} %bitcast.16), channel_id=1, source_target_pairs={{0,16},{16,0},{1,17},{17,1},{2,18},{18,2},{3,19},{19,3},{4,20},{20... | collective-permute-start | bytes 1966088 | tf_op jit(solution)/shard_map/ppermute | solution.py:51
  56.4 4.4 %collective-permute-start.5 = (f32[256,256]{1,0:T(8,128)S(1)}, f32[256,256]{1,0:T(8,128)S(1)}, u32[]{:S(2)}, u32[]{:S(2)}) collective-permute-start(f32[256,256]{1,0:T(8,128)S(1)} %slice.35), channel_id=1, source_target_pairs={{0,3},{1,0},{2,1},{3,2},{4,7},{5,4},{6,5},{7,6},{8,11},{9,8},{10,9... | collective-permute-start | bytes 786440 | tf_op jit(solution)/shard_map/ppermute | solution.py:51
  60.9 1.9 collective-permute-start.3
  63.0 3.5 %collective-permute-done.5.refs_3_ = f32[256,256]{1,0:T(8,128)S(1)} collective-permute-done((f32[256,256]{1,0:T(8,128)S(1)}, f32[256,256]{1,0:T(8,128)S(1)}, u32[]{:S(2)}, u32[]{:S(2)}) %collective-permute-start.5) | collective-permute-done | bytes 262176 | tf_op jit(solution)/shard_map/ppermute | solution.py:51
  66.5 5.1 %collective-permute-done.3.refs_2_ = f32[256,256]{1,0:T(8,128)S(1)} collective-permute-done((f32[256,256]{1,0:T(8,128)S(1)}, f32[256,256]{1,0:T(8,128)S(1)}, u32[]{:S(2)}, u32[]{:S(2)}) %collective-permute-start.3) | collective-permute-done | bytes 262176 | tf_op jit(solution)/shard_map/ppermute | solution.py:51
  73.2 3.8 %shard_map.64 = (f32[16,32,256]{2,1,0:T(8,128)S(1)}, bf16[2048,256]{1,0:T(8,128)(2,1)S(1)}, bf16[2048,256]{1,0:T(8,128)(2,1)S(1)}, bf16[512,512]{1,0:T(8,128)(2,...) custom-call(s32[49]{0:T(128)S(1)} %pad_add_fusion.where_ref, ...), custom_call_target="tpu_custom_call" | custom-call | tf_op jit(solution)/shard_map/pallas_call | solution.py:186
  76.9 18.0 %all_to_all.45 = f32[16,32,256]{2,1,0:T(8,128)S(1)} all-to-all(f32[16,32,256]{2,1,0:T(8,128)S(1)} %get-tuple-element.20), channel_id=1, replica_groups=mesh['zh'=2,'y'=8,'core'=2,'zl_hi'=2,'zl_lo'=2,'x_hi'=2,'x_lo'=2] {'x_lo..., dimensions={0} | all-to-all | bytes 1048576 | tf_op jit(solution)/shard_map/all_to_all | solution.py:42
  94.9 1.8 shard_map.65
  96.8 17.4 %all_to_all.46.terms_ref = f32[16,32,256]{2,1,0:T(8,128)S(1)} all-to-all(f32[16,32,256]{2,1,0:T(8,128)S(1)} %bitcast.15), channel_id=1, replica_groups=mesh['zh'=2,'y'=8,'core'=2,'zl_hi'=2,'zl_lo'=2,'x_hi'=2,'x_lo'=2] {'x_lo..., dimensions={0} | all-to-all | bytes 1048576 | tf_op jit(solution)/shard_map/all_to_all | solution.py:42
  115.3 25.3 %all_to_all.47.terms_ref = f32[32,16,128]{2,1,0:T(8,128)S(1)} all-to-all(f32[32,16,128]{2,1,0:T(8,128)S(1)} %shard_map.66), channel_id=1, replica_groups=mesh['zh'=2,'y'=8,'core'=2,'zl_hi'=2,'zl_lo'=2,'x_hi'=2,'x_lo'=2] {'zh',..., dimensions={0} | all-to-all | bytes 524288 | tf_op jit(solution)/shard_map/all_to_all | solution.py:42
  140.7 20.1 %all_to_all.48.gathered_ref = f32[32,16,128]{2,1,0:T(8,128)S(1)} all-to-all(f32[32,16,128]{2,1,0:T(8,128)S(1)} %get-tuple-element.29), channel_id=1, replica_groups=mesh['zh'=2,'y'=8,'core'=2,'zl_hi'=2,'zl_lo'=2,'x_hi'=2,'x_lo'=2] {'zh',..., dimensions={0} | all-to-all | bytes 524288 | tf_op jit(solution)/shard_map/all_to_all | solution.py:42
  161.5 15.6 %all_to_all.49 = f32[16,32,256]{2,1,0:T(8,128)S(1)} all-to-all(f32[16,32,256]{2,1,0:T(8,128)S(1)} %shard_map.68), channel_id=1, replica_groups=mesh['zh'=2,'y'=8,'core'=2,'zl_hi'=2,'zl_lo'=2,'x_hi'=2,'x_lo'=2] {'x_lo..., dimensions={0} | all-to-all | bytes 1048576 | tf_op jit(solution)/shard_map/all_to_all | solution.py:42
  177.1 1.8 shard_map.69
  178.9 17.6 %all_to_all.50.terms_ref = f32[16,32,256]{2,1,0:T(8,128)S(1)} all-to-all(f32[16,32,256]{2,1,0:T(8,128)S(1)} %bitcast.13), channel_id=1, replica_groups=mesh['zh'=2,'y'=8,'core'=2,'zl_hi'=2,'zl_lo'=2,'x_hi'=2,'x_lo'=2] {'x_lo..., dimensions={0} | all-to-all | bytes 1048576 | tf_op jit(solution)/shard_map/all_to_all | solution.py:42
  196.5 1.1 shard_map.70
  197.6 23.6 %all_to_all.51.terms_ref = f32[32,16,128]{2,1,0:T(8,128)S(1)} all-to-all(f32[32,16,128]{2,1,0:T(8,128)S(1)} %shard_map.70), channel_id=1, replica_groups=mesh['zh'=2,'y'=8,'core'=2,'zl_hi'=2,'zl_lo'=2,'x_hi'=2,'x_lo'=2] {'zh',..., dimensions={0} | all-to-all | bytes 524288 | tf_op jit(solution)/shard_map/all_to_all | solution.py:42
  (45 shorter events, 6.4 us)
Async XLA Ops:
  1.7 7.9 %copy-start.9 = (f32[1,32,64]{2,1,0:T(8,128)S(1)}, f32[1,32,64]{2,1,0:T(8,128)}, u32[]{:S(2)}) copy-start(f32[1,32,64]{2,1,0:T(8,128)} %param.6) | copy-start | bytes 24580
  1.8 23.6 %all-to-all-start = ((f32[4,128,256]{2,1,0:T(8,128)}), f32[4,128,256]{2,1,0:T(8,128)S(1)}, u32[]{:S(2)}, u32[]{:S(2)}) async-start(f32[4,128,256]{2,1,0:T(8,128)} %broadcast_in_dim.9), calls=%async_computation | async-start | bytes 1048576 | tf_op jit(solution)/shard_map/all_to_all | solution.py:42
  9.7 0.8 copy-start.8
  10.5 14.8 %collective-permute-start = (f32[16,640]{1,0:T(8,128)S(1)}, f32[16,640]{1,0:T(8,128)S(1)}, u32[]{:S(2)}, u32[]{:S(2)}) collective-permute-start(f32[16,640]{1,0:T(8,128)S(1)} %pad_maximum_fusion.1), channel_id=1, source_target_pairs={{0,256},{256,0},{1,257},{257,1},{2,258},{258,2},{3,259},{259,3},{4... | collective-permute-start | bytes 122888 | tf_op jit(solution)/shard_map/ppermute | solution.py:51
  25.4 12.2 %copy-start.2 = (f32[4,128,256]{2,1,0:T(8,128)}, f32[4,128,256]{2,1,0:T(8,128)S(1)}, u32[]{:S(2)}) copy-start(f32[4,128,256]{2,1,0:T(8,128)S(1)} %all-to-all-done) | copy-start | bytes 1572868
  26.3 24.8 %all-to-all-start.1 = ((f32[8,32,640]{2,1,0:T(8,128)}), f32[8,32,640]{2,1,0:T(8,128)S(1)}, u32[]{:S(2)}, u32[]{:S(2)}) async-start(f32[8,32,640]{2,1,0:T(8,128)} %broadcast_in_dim.10), calls=%async_computation.1 | async-start | bytes 1310720 | tf_op jit(solution)/shard_map/all_to_all | solution.py:42
  33.2 6.4 %copy-start.10 = (f32[32]{0:T(128)S(1)}, f32[32]{0:T(128)}, u32[]{:S(2)}) copy-start(f32[32]{0:T(128)} %param.7) | copy-start | bytes 388
  33.2 6.4 %copy-start.11 = (f32[64]{0:T(128)S(1)}, f32[64]{0:T(128)}, u32[]{:S(2)}) copy-start(f32[64]{0:T(128)} %param.8) | copy-start | bytes 772
  33.2 23.2 %collective-permute-start.4 = (f32[512,256]{1,0:T(8,128)S(1)}, f32[512,256]{1,0:T(8,128)S(1)}, u32[]{:S(2)}, u32[]{:S(2)}) collective-permute-start(f32[512,256]{1,0:T(8,128)S(1)} %bitcast.18), channel_id=1, source_target_pairs={{0,3},{1,0},{2,1},{3,2},{4,7},{5,4},{6,5},{7,6},{8,11},{9,8},{10,9... | collective-permute-start | bytes 1572872 | tf_op jit(solution)/shard_map/ppermute | solution.py:51
  37.6 23.2 %collective-permute-start.2 = (f32[512,256]{1,0:T(8,128)S(1)}, f32[512,256]{1,0:T(8,128)S(1)}, u32[]{:S(2)}, u32[]{:S(2)}) collective-permute-start(f32[512,256]{1,0:T(8,128)S(1)} %bitcast.19), channel_id=1, source_target_pairs={{0,1},{1,2},{2,3},{3,0},{4,5},{5,6},{6,7},{7,4},{8,9},{9,10},{10,1... | collective-permute-start | bytes 1572872 | tf_op jit(solution)/shard_map/ppermute | solution.py:51
  51.2 20.4 %copy-start.1 = (f32[8,32,640]{2,1,0:T(8,128)}, f32[8,32,640]{2,1,0:T(8,128)S(1)}, u32[]{:S(2)}) copy-start(f32[8,32,640]{2,1,0:T(8,128)S(1)} %all-to-all-done.1) | copy-start | bytes 1966084
  51.2 20.4 %collective-permute-start.1 = (f32[16,16,640]{2,1,0:T(8,128)S(1)}, f32[16,16,640]{2,1,0:T(8,128)S(1)}, u32[]{:S(2)}, u32[]{:S(2)}) collective-permute-start(f32[16,16,640]{2,1,0:T(8,128)S(1)} %bitcast.16), channel_id=1, source_target_pairs={{0,16},{16,0},{1,17},{17,1},{2,18},{18,2},{3,19},{19,3},{4,20},{20... | collective-permute-start | bytes 1966088 | tf_op jit(solution)/shard_map/ppermute | solution.py:51
  56.4 15.2 %copy-start.3 = (f32[512,256]{1,0:T(8,128)}, f32[512,256]{1,0:T(8,128)S(1)}, u32[]{:S(2)}) copy-start(f32[512,256]{1,0:T(8,128)S(1)} %collective-permute-done.4.refs_4_) | copy-start | bytes 1572868
  56.4 10.1 %collective-permute-start.5 = (f32[256,256]{1,0:T(8,128)S(1)}, f32[256,256]{1,0:T(8,128)S(1)}, u32[]{:S(2)}, u32[]{:S(2)}) collective-permute-start(f32[256,256]{1,0:T(8,128)S(1)} %slice.35), channel_id=1, source_target_pairs={{0,3},{1,0},{2,1},{3,2},{4,7},{5,4},{6,5},{7,6},{8,11},{9,8},{10,9... | collective-permute-start | bytes 786440 | tf_op jit(solution)/shard_map/ppermute | solution.py:51
  60.9 10.8 %copy-start.4 = (f32[512,256]{1,0:T(8,128)}, f32[512,256]{1,0:T(8,128)S(1)}, u32[]{:S(2)}) copy-start(f32[512,256]{1,0:T(8,128)S(1)} %collective-permute-done.2.refs_1_) | copy-start | bytes 1572868
  60.9 10.7 %collective-permute-start.3 = (f32[256,256]{1,0:T(8,128)S(1)}, f32[256,256]{1,0:T(8,128)S(1)}, u32[]{:S(2)}, u32[]{:S(2)}) collective-permute-start(f32[256,256]{1,0:T(8,128)S(1)} %slice.34), channel_id=1, source_target_pairs={{0,1},{1,2},{2,3},{3,0},{4,5},{5,6},{6,7},{7,4},{8,9},{9,10},{10,1... | collective-permute-start | bytes 786440 | tf_op jit(solution)/shard_map/ppermute | solution.py:51
  66.5 5.1 %copy-start.6 = (f32[256,256]{1,0:T(8,128)}, f32[256,256]{1,0:T(8,128)S(1)}, u32[]{:S(2)}) copy-start(f32[256,256]{1,0:T(8,128)S(1)} %collective-permute-done.5.refs_3_) | copy-start | bytes 786436
  71.6 0.7 copy-start.7
  72.3 0.9 copy-start.5
  76.9 18.0 %copy-start = (f32[512,256]{1,0:T(8,128)S(1)}, f32[512,256]{1,0:T(8,128)}, u32[]{:S(2)}) copy-start(f32[512,256]{1,0:T(8,128)} %screened_ref.3) | copy-start | bytes 1572868

commit v4 on v3

--- a/solution.py
+++ b/solution.py
@@ -17,7 +17,10 @@
 CROSS = ("zh", "core")
 
 NY, NZ, NX = 8, 4, 4
+EARLY, LATE = (0, 1, 3), (2,)
+WIDTH = 128
 SEND = ("x_lo", "x_hi", "zl_lo", "zl_hi")
+SWEEP = ("y", "core", "zh")
 SENT = [int(f"{i:04b}"[::-1], 2) for i in range(NX * NZ)]
 
 F32 = jnp.float32
@@ -58,6 +61,10 @@
 def packed(block):
     half = block.shape[0] // 2
     return jnp.concatenate([block[:half], block[half:]], axis=1)
+
+
+def sent_at(p):
+    return p % (2 * NY) * 2 + p // (2 * NY)
 
 
 def place_pair(a, b, chip, xh_ref, xl_ref):
@@ -82,31 +89,46 @@
     return copies
 
 
-def begin_kernel(where_ref, ediff_ref, older_ref, own_hbm, other_hbm, *refs):
-    conds, refs = refs[: NX + 1], refs[NX + 1 :]
-    (pair_ref, ch_ref, cl_ref, vh_ref, vl_ref, th_ref, tl_ref, ediff_out_ref, older_out_ref,
+def block_of(where_ref, blocks_ref, p):
+    return blocks_ref[where_ref[1 + p], where_ref[1 + 2 * NX * NZ + p // 2]]
+
+
+def chip_at(where_ref, step, z):
+    return z * NX + ((where_ref[0] - step) & (NX - 1))
+
+
+def split_rows(where_ref, step, block, ch_ref, cl_ref):
+    hi, lo = split(block)
+    depth = block.shape[0] // NZ
+    for z in range(NZ):
+        at = pl.multiple_of(chip_at(where_ref, step, z) * depth, depth)
+        ch_ref[pl.ds(at, depth), :] = hi[z * depth : (z + 1) * depth]
+        cl_ref[pl.ds(at, depth), :] = lo[z * depth : (z + 1) * depth]
+    return hi, lo
+
+
+def early_kernel(where_ref, ediff_ref, older_ref, own_hbm, other_hbm, *refs):
+    conds, refs = refs[: len(EARLY)], refs[len(EARLY) :]
+    (vh_ref, vl_ref, th_ref, tl_ref, ch_ref, cl_ref, part_ref, far_h_ref, far_l_ref,
+     ediff_out_ref, older_out_ref,
      blocks_ref, cond_ref, xh_ref, xl_ref, block_sems, cond_sems) = refs
     parts = collect((own_hbm, other_hbm), blocks_ref, block_sems)
-    part = conds[2].shape[0]
-    places = [cond_ref.at[0], cond_ref.at[1], cond_ref.at[2, :part], cond_ref.at[2, part:]]
-    conds = [
-        pltpu.make_async_copy(ref, place, cond_sems.at[i])
-        for i, (ref, place) in enumerate(zip(conds, places + [cond_ref.at[3]]))
-    ]
-    for copy in conds:
-        copy.start()
+    conds = collect(conds, cond_ref, cond_sems)
     ediff_out_ref[...] = ediff_ref[...]
     older_out_ref[...] = older_ref[...]
     for copy in parts:
         copy.wait()
+    for i, step in enumerate(EARLY + LATE):
+        for z in range(NZ):
+            chip = chip_at(where_ref, step, z)
+            a, b = (
+                block_of(where_ref, blocks_ref, 2 * chip + core)[:, -WIDTH:] for core in range(2)
+            )
+            place_pair(a, b, i * NZ + z, xh_ref, xl_ref)
     points = vh_ref.shape[1]
-
-    def block(p):
-        return blocks_ref[where_ref[1 + p], where_ref[1 + 2 * NX * NZ + p // 2]]
-
-    for q in range(NX * NZ):
-        place_pair(block(2 * q)[:, points:], block(2 * q + 1)[:, points:], q, xh_ref, xl_ref)
-    rows = [block(2 * q + half)[:, :points] for q in SENT for half in range(2)]
+    rows = [
+        block_of(where_ref, blocks_ref, 2 * q + core)[:, :points] for q in SENT for core in range(2)
+    ]
     whole = jnp.concatenate(rows, axis=0)
     hi, lo = split(whole)
     vh_ref[...] = hi
@@ -114,17 +136,30 @@
     hi, lo = split(whole.T)
     th_ref[...] = hi
     tl_ref[...] = lo
-    depth = cond_ref.shape[1] // NZ
-    for copy in conds:
+    far_h_ref[...] = xh_ref[:, len(EARLY) * NZ * WIDTH :]
+    far_l_ref[...] = xl_ref[:, len(EARLY) * NZ * WIDTH :]
+    total = jnp.zeros_like(part_ref)
+    for i, step in enumerate(EARLY):
+        conds[i].wait()
+        ch, cl = split_rows(where_ref, step, cond_ref[i], ch_ref, cl_ref)
+        cols = slice(i * NZ * WIDTH, (i + 1) * NZ * WIDTH)
+        xh, xl = xh_ref[:, cols], xl_ref[:, cols]
+        total += dot(xh, ch) + (dot(xh, cl) + dot(xl, ch))
+    part_ref[...] = total
+
+
+def late_kernel(
+    where_ref, part_ref, far_h_ref, far_l_ref, upper_hbm, lower_hbm, ch_in_ref, cl_in_ref,
+    pair_ref, ch_ref, cl_ref, cond_ref, sems,
+):
+    del ch_in_ref, cl_in_ref
+    for copy in collect((upper_hbm, lower_hbm), cond_ref, sems):
         copy.wait()
-    for step in range(NX):
-        for z in range(NZ):
-            chip = z * NX + ((where_ref[0] - step) & (NX - 1))
-            rows = pl.ds(pl.multiple_of(chip * depth, depth), depth)
-            hi, lo = split(cond_ref[step, z * depth : (z + 1) * depth])
-            ch_ref[rows, :] = hi
-            cl_ref[rows, :] = lo
-    multiply_pair(xh_ref, xl_ref, ch_ref, cl_ref, pair_ref)
+    block = cond_ref[...].reshape(-1, cond_ref.shape[2])
+    ch, cl = split_rows(where_ref, LATE[0], block, ch_ref, cl_ref)
+    xh, xl = far_h_ref[...], far_l_ref[...]
+    pair = part_ref[...] + (dot(xh, ch) + (dot(xh, cl) + dot(xl, ch)))
+    pair_ref[...] = jnp.broadcast_to(pair[None], pair_ref.shape)
 
 
 def multiply_pair(xh_ref, xl_ref, ch_ref, cl_ref, pair_ref):
@@ -135,7 +170,8 @@
 
 def pair_kernel(gathered_ref, ch_ref, cl_ref, pair_ref, xh_ref, xl_ref):
     for q in range(NX * NZ):
-        place_pair(gathered_ref[2 * q], gathered_ref[2 * q + 1], q, xh_ref, xl_ref)
+        a, b = gathered_ref[sent_at(2 * q)], gathered_ref[sent_at(2 * q + 1)]
+        place_pair(a, b, q, xh_ref, xl_ref)
     multiply_pair(xh_ref, xl_ref, ch_ref, cl_ref, pair_ref)
 
 
@@ -155,8 +191,8 @@
     for q in range(NX * NZ):
         upper = direct[:half, q * width : (q + 1) * width]
         lower = direct[half:, q * width : (q + 1) * width]
-        out_ref[2 * q] = jnp.where(left, upper, pltpu.roll(lower, width // 2, 1))
-        out_ref[2 * q + 1] = jnp.where(left, pltpu.roll(upper, width // 2, 1), lower)
+        out_ref[sent_at(2 * q)] = jnp.where(left, upper, pltpu.roll(lower, width // 2, 1))
+        out_ref[sent_at(2 * q + 1)] = jnp.where(left, pltpu.roll(upper, width // 2, 1), lower)
 
 
 def scaled(terms_ref, vec, ediff_ref):
@@ -177,7 +213,7 @@
     out_ref[half:, :] = new[:, width // 2 :]
 
 
-def call(kernel, out_shapes, operands, scratch=(), far=()):
+def call(kernel, out_shapes, operands, scratch=(), far=(), aliases=None):
     shapes = [jax.ShapeDtypeStruct(s, d) for s, d in out_shapes]
     spaces = [pltpu.SMEM if a.dtype == jnp.int32 else pltpu.VMEM for a in operands]
     for i in far:
@@ -188,6 +224,7 @@
         out_shape=shapes if len(shapes) > 1 else shapes[0],
         scratch_shapes=list(scratch),
         in_specs=[pl.BlockSpec(memory_space=space) for space in spaces],
+        input_output_aliases=aliases or {},
         compiler_params=PARAMS,
     )(*operands)
 
@@ -217,29 +254,39 @@
     left, right = shifted(mine, X, 1), shifted(mine, X, -1)
     part = mine.shape[0] // 2
     upper, lower = shifted(left[:part], X, 1), shifted(right[part:], X, -1)
-    cond = [mine, left, upper, lower, right]
 
     newer = older
     scratch = [pltpu.VMEM((rows, nc), BF16)] * 2
-    pair, ch, cl, vh, vl, th, tl, ediff, older = call(
-        begin_kernel,
-        [((val, rows, points_c), F32)]
-        + [((nc, points_c), BF16)] * 2
-        + [((nv, points_v), BF16)] * 2
+    far = nc // NX
+    conds = [((nc, points_c), BF16)] * 2
+    vh, vl, th, tl, ch, cl, pair, far_h, far_l, ediff, older = call(
+        early_kernel,
+        [((nv, points_v), BF16)] * 2
         + [((points_v, nv), BF16)] * 2
+        + conds
+        + [((rows, points_c), F32)]
+        + [((rows, far), BF16)] * 2
         + [((half, width), F32)] * 2,
-        [where, ediff, older, own, other, *cond],
-        [pltpu.VMEM((2, *own.shape), F32), pltpu.VMEM((NX, *mine.shape), F32)]
+        [where, ediff, older, own, other, mine, left, right],
+        [pltpu.VMEM((2, *own.shape), F32), pltpu.VMEM((len(EARLY), *mine.shape), F32)]
         + scratch
-        + [pltpu.SemaphoreType.DMA((2,)), pltpu.SemaphoreType.DMA((NX + 1,))],
-        far=range(3, 6 + NX),
+        + [pltpu.SemaphoreType.DMA((2,)), pltpu.SemaphoreType.DMA((len(EARLY),))],
+        far=range(3, 8),
+    )
+    pair, ch, cl = call(
+        late_kernel,
+        [((val, rows, points_c), F32)] + conds,
+        [where, pair, far_h, far_l, upper, lower, ch, cl],
+        [pltpu.VMEM((2, *upper.shape), F32), pltpu.SemaphoreType.DMA((2,))],
+        far=(4, 5),
+        aliases={6: 1, 7: 2},
     )
     for step in range(ITERS):
         if step > 0:
             pair = call(
                 pair_kernel,
                 [((val, rows, points_c), F32)],
-                [exchange(copies, PTS), ch, cl],
+                [exchange(copies, SWEEP), ch, cl],
                 scratch,
             )
         pair_all = exchange(pair, SEND).reshape(nv, points_c)
@@ -248,7 +295,7 @@
         )
         back = exchange(back.reshape(val, rows, points_c), SEND)
         direct = call(direct_kernel, [((pts, half, width), F32)], [back, ch, cl])
-        direct = exchange(direct, PTS)
+        direct = exchange(direct, SWEEP)
         if step < ITERS - 1:
             newer, copies = call(
                 first_kernel,

time: 223 us -> 217 us (0.973)
  waiting for transfers between devices: 27 us -> 19.6 us
    ppermute x6, waiting for transfers between devices: 15.4 us -> 8.21 us  [shifted(): return lax.ppermute(array, axis, pairs)]
    pallas_call x8 -> x9, Pallas kernels: 11.1 us -> 12.8 us  [call(): pl.pallas_call(kernel, out_shape=shapes if len(shapes) > 1 else shapes[0]...]
  transfers between devices with their start and end apart: 8 -> 8, of which waited for: 4 -> 3; matrix products, arithmetic and copies ran while one was open for 0% -> 0% of each run, Pallas kernels for 0% -> 2%
where the time goes in v4:
time: 217 us; the launch traced here: 216 us
  blocking collectives  137 us (63%)
  starting transfers between devices  40.9 us (19%)
  waiting for transfers between devices  19.6 us (9%)
  Pallas kernels  12.8 us (6%)
  local copies, waits for them, and re-layouts  5.09 us (2%)
    all_to_all x7, blocking collectives, exchange(): return lax.all_to_all(blocks, axes, 0, 0, tiled=True)  137 us
    ppermute x6, starting transfers between devices, shifted(): return lax.ppermute(array, axis, pairs)  26.1 us
    all_to_all x2, starting transfers between devices, exchange(): return lax.all_to_all(blocks, axes, 0, 0, tiled=True)  14.8 us
    pallas_call x9, Pallas kernels, call(): pl.pallas_call(kernel, out_shape=shapes if len(shapes) > 1 else shapes[0]...  12.8 us
    all_to_all x2, waiting for transfers between devices, exchange(): return lax.all_to_all(blocks, axes, 0, 0, tiled=True)  11.4 us
    ppermute x6, waiting for transfers between devices, shifted(): return lax.ppermute(array, axis, pairs)  8.21 us
  transfers between devices with their start and end apart: 8, of which 3 were waited for; matrix products, arithmetic and copies ran while one was open for 0% of the time, Pallas kernels for 2%

profile of v4, /device:TPU:1, one launch (start us, length us, event | category | flops | bytes accessed | tf_op | source)
XLA Modules:
  0.0 215.8 jit_solution(7399359412408712244)
XLA Ops:
  0.0 1.7 broadcast_in_dim.9
  1.7 7.9 %all-to-all-start = ((f32[4,128,256]{2,1,0:T(8,128)}), f32[4,128,256]{2,1,0:T(8,128)S(1)}, u32[]{:S(2)}, u32[]{:S(2)}) async-start(f32[4,128,256]{2,1,0:T(8,128)} %broadcast_in_dim.9), calls=%async_computation | async-start | bytes 1048576 | tf_op jit(solution)/shard_map/all_to_all | solution.py:45
  10.5 7.9 %collective-permute-start = (f32[16,640]{1,0:T(8,128)S(1)}, f32[16,640]{1,0:T(8,128)S(1)}, u32[]{:S(2)}, u32[]{:S(2)}) collective-permute-start(f32[16,640]{1,0:T(8,128)S(1)} %pad_maximum_fusion.1), channel_id=1, source_target_pairs={{0,256},{256,0},{1,257},{257,1},{2,258},{258,2},{3,259},{259,3},{4... | collective-permute-start | bytes 122888 | tf_op jit(solution)/shard_map/ppermute | solution.py:54
  18.5 6.8 %collective-permute-done = f32[16,640]{1,0:T(8,128)S(1)} collective-permute-done((f32[16,640]{1,0:T(8,128)S(1)}, f32[16,640]{1,0:T(8,128)S(1)}, u32[]{:S(2)}, u32[]{:S(2)}) %collective-permute-start) | collective-permute-done | bytes 40992 | tf_op jit(solution)/shard_map/ppermute | solution.py:54
  26.3 6.8 %all-to-all-start.1 = ((f32[8,32,640]{2,1,0:T(8,128)}), f32[8,32,640]{2,1,0:T(8,128)S(1)}, u32[]{:S(2)}, u32[]{:S(2)}) async-start(f32[8,32,640]{2,1,0:T(8,128)} %broadcast_in_dim.10), calls=%async_computation.1 | async-start | bytes 1310720 | tf_op jit(solution)/shard_map/all_to_all | solution.py:45
  33.2 3.1 %collective-permute-start.2 = (f32[512,256]{1,0:T(8,128)S(1)}, f32[512,256]{1,0:T(8,128)S(1)}, u32[]{:S(2)}, u32[]{:S(2)}) collective-permute-start(f32[512,256]{1,0:T(8,128)S(1)} %bitcast.18), channel_id=1, source_target_pairs={{0,1},{1,2},{2,3},{3,0},{4,5},{5,6},{6,7},{7,4},{8,9},{9,10},{10,1... | collective-permute-start | bytes 1572872 | tf_op jit(solution)/shard_map/ppermute | solution.py:54
  36.3 3.4 %collective-permute-start.3 = (f32[512,256]{1,0:T(8,128)S(1)}, f32[512,256]{1,0:T(8,128)S(1)}, u32[]{:S(2)}, u32[]{:S(2)}) collective-permute-start(f32[512,256]{1,0:T(8,128)S(1)} %bitcast.19), channel_id=1, source_target_pairs={{0,3},{1,0},{2,1},{3,2},{4,7},{5,4},{6,5},{7,6},{8,11},{9,8},{10,9... | collective-permute-start | bytes 1572872 | tf_op jit(solution)/shard_map/ppermute | solution.py:54
  39.8 11.4 %all-to-all-done.1 = f32[8,32,640]{2,1,0:T(8,128)S(1)} async-done(((f32[8,32,640]{2,1,0:T(8,128)}), f32[8,32,640]{2,1,0:T(8,128)S(1)}, u32[]{:S(2)}, u32[]{:S(2)}) %all-to-all-start.1) | async-done | bytes 655392 | tf_op jit(solution)/shard_map/all_to_all | solution.py:45
  51.2 5.2 %collective-permute-start.1 = (f32[16,16,640]{2,1,0:T(8,128)S(1)}, f32[16,16,640]{2,1,0:T(8,128)S(1)}, u32[]{:S(2)}, u32[]{:S(2)}) collective-permute-start(f32[16,16,640]{2,1,0:T(8,128)S(1)} %bitcast.16), channel_id=1, source_target_pairs={{0,16},{16,0},{1,17},{17,1},{2,18},{18,2},{3,19},{19,3},{4,20},{20... | collective-permute-start | bytes 1966088 | tf_op jit(solution)/shard_map/ppermute | solution.py:54
  56.4 3.1 %collective-permute-start.4 = (f32[256,256]{1,0:T(8,128)S(1)}, f32[256,256]{1,0:T(8,128)S(1)}, u32[]{:S(2)}, u32[]{:S(2)}) collective-permute-start(f32[256,256]{1,0:T(8,128)S(1)} %slice.34), channel_id=1, source_target_pairs={{0,1},{1,2},{2,3},{3,0},{4,5},{5,6},{6,7},{7,4},{8,9},{9,10},{10,1... | collective-permute-start | bytes 786440 | tf_op jit(solution)/shard_map/ppermute | solution.py:54
  59.6 3.4 %collective-permute-start.5 = (f32[256,256]{1,0:T(8,128)S(1)}, f32[256,256]{1,0:T(8,128)S(1)}, u32[]{:S(2)}, u32[]{:S(2)}) collective-permute-start(f32[256,256]{1,0:T(8,128)S(1)} %slice.35), channel_id=1, source_target_pairs={{0,3},{1,0},{2,1},{3,2},{4,7},{5,4},{6,5},{7,6},{8,11},{9,8},{10,9... | collective-permute-start | bytes 786440 | tf_op jit(solution)/shard_map/ppermute | solution.py:54
  64.1 3.6 %shard_map.64 = (bf16[512,512]{1,0:T(8,128)(2,1)S(1)}, bf16[512,512]{1,0:T(8,128)(2,1)S(1)}, bf16[512,512]{1,0:T(8,128)(2,1)S(1)}, bf16[512,512]{1,0:T(8,128)(2,...) custom-call(s32[49]{0:T(128)S(1)} %pad_add_fusion.where_ref, ...), custom_call_target="tpu_custom_call" | custom-call | tf_op jit(solution)/shard_map/pallas_call | solution.py:222
  67.8 1.4 collective-permute-done.5.lower_hbm
  69.8 1.9 shard_map.65
  71.7 20.4 %all_to_all.45 = f32[16,32,256]{2,1,0:T(8,128)S(1)} all-to-all(f32[16,32,256]{2,1,0:T(8,128)S(1)} %get-tuple-element.30), channel_id=1, replica_groups=mesh['zh'=2,'y'=8,'core'=2,'zl_hi'=2,'zl_lo'=2,'x_hi'=2,'x_lo'=2] {'x_lo..., dimensions={0} | all-to-all | bytes 1048576 | tf_op jit(solution)/shard_map/all_to_all | solution.py:45
  92.1 1.8 shard_map.66
  93.9 17.4 %all_to_all.46.terms_ref = f32[16,32,256]{2,1,0:T(8,128)S(1)} all-to-all(f32[16,32,256]{2,1,0:T(8,128)S(1)} %bitcast.15), channel_id=1, replica_groups=mesh['zh'=2,'y'=8,'core'=2,'zl_hi'=2,'zl_lo'=2,'x_hi'=2,'x_lo'=2] {'x_lo..., dimensions={0} | all-to-all | bytes 1048576 | tf_op jit(solution)/shard_map/all_to_all | solution.py:45
  112.5 22.6 %all_to_all.47.terms_ref = f32[32,16,128]{2,1,0:T(8,128)S(1)} all-to-all(f32[32,16,128]{2,1,0:T(8,128)S(1)} %shard_map.67), channel_id=1, replica_groups=mesh['zh'=2,'y'=8,'core'=2,'zl_hi'=2,'zl_lo'=2,'x_hi'=2,'x_lo'=2] {'y','..., dimensions={0} | all-to-all | bytes 524288 | tf_op jit(solution)/shard_map/all_to_all | solution.py:45
  135.2 19.4 %all_to_all.48.gathered_ref = f32[32,16,128]{2,1,0:T(8,128)S(1)} all-to-all(f32[32,16,128]{2,1,0:T(8,128)S(1)} %get-tuple-element.39), channel_id=1, replica_groups=mesh['zh'=2,'y'=8,'core'=2,'zl_hi'=2,'zl_lo'=2,'x_hi'=2,'x_lo'=2] {'y','..., dimensions={0} | all-to-all | bytes 524288 | tf_op jit(solution)/shard_map/all_to_all | solution.py:45
  155.3 15.4 %all_to_all.49 = f32[16,32,256]{2,1,0:T(8,128)S(1)} all-to-all(f32[16,32,256]{2,1,0:T(8,128)S(1)} %shard_map.69), channel_id=1, replica_groups=mesh['zh'=2,'y'=8,'core'=2,'zl_hi'=2,'zl_lo'=2,'x_hi'=2,'x_lo'=2] {'x_lo..., dimensions={0} | all-to-all | bytes 1048576 | tf_op jit(solution)/shard_map/all_to_all | solution.py:45
  170.7 1.8 shard_map.70
  172.6 17.6 %all_to_all.50.terms_ref = f32[16,32,256]{2,1,0:T(8,128)S(1)} all-to-all(f32[16,32,256]{2,1,0:T(8,128)S(1)} %bitcast.13), channel_id=1, replica_groups=mesh['zh'=2,'y'=8,'core'=2,'zl_hi'=2,'zl_lo'=2,'x_hi'=2,'x_lo'=2] {'x_lo..., dimensions={0} | all-to-all | bytes 1048576 | tf_op jit(solution)/shard_map/all_to_all | solution.py:45
  190.2 1.1 shard_map.71
  191.3 23.8 %all_to_all.51.terms_ref = f32[32,16,128]{2,1,0:T(8,128)S(1)} all-to-all(f32[32,16,128]{2,1,0:T(8,128)S(1)} %shard_map.71), channel_id=1, replica_groups=mesh['zh'=2,'y'=8,'core'=2,'zl_hi'=2,'zl_lo'=2,'x_hi'=2,'x_lo'=2] {'y','..., dimensions={0} | all-to-all | bytes 524288 | tf_op jit(solution)/shard_map/all_to_all | solution.py:45
  (46 shorter events, 6.4 us)
Async XLA Ops:
  1.7 7.9 %copy-start.9 = (f32[1,32,64]{2,1,0:T(8,128)S(1)}, f32[1,32,64]{2,1,0:T(8,128)}, u32[]{:S(2)}) copy-start(f32[1,32,64]{2,1,0:T(8,128)} %param.6) | copy-start | bytes 24580
  1.7 23.6 %all-to-all-start = ((f32[4,128,256]{2,1,0:T(8,128)}), f32[4,128,256]{2,1,0:T(8,128)S(1)}, u32[]{:S(2)}, u32[]{:S(2)}) async-start(f32[4,128,256]{2,1,0:T(8,128)} %broadcast_in_dim.9), calls=%async_computation | async-start | bytes 1048576 | tf_op jit(solution)/shard_map/all_to_all | solution.py:45
  9.7 0.8 copy-start.8
  10.5 14.8 %collective-permute-start = (f32[16,640]{1,0:T(8,128)S(1)}, f32[16,640]{1,0:T(8,128)S(1)}, u32[]{:S(2)}, u32[]{:S(2)}) collective-permute-start(f32[16,640]{1,0:T(8,128)S(1)} %pad_maximum_fusion.1), channel_id=1, source_target_pairs={{0,256},{256,0},{1,257},{257,1},{2,258},{258,2},{3,259},{259,3},{4... | collective-permute-start | bytes 122888 | tf_op jit(solution)/shard_map/ppermute | solution.py:54
  25.4 10.9 %copy-start.2 = (f32[4,128,256]{2,1,0:T(8,128)}, f32[4,128,256]{2,1,0:T(8,128)S(1)}, u32[]{:S(2)}) copy-start(f32[4,128,256]{2,1,0:T(8,128)S(1)} %all-to-all-done) | copy-start | bytes 1572868
  26.3 24.8 %all-to-all-start.1 = ((f32[8,32,640]{2,1,0:T(8,128)}), f32[8,32,640]{2,1,0:T(8,128)S(1)}, u32[]{:S(2)}, u32[]{:S(2)}) async-start(f32[8,32,640]{2,1,0:T(8,128)} %broadcast_in_dim.10), calls=%async_computation.1 | async-start | bytes 1310720 | tf_op jit(solution)/shard_map/all_to_all | solution.py:45
  33.2 6.5 %copy-start.10 = (f32[32]{0:T(128)S(1)}, f32[32]{0:T(128)}, u32[]{:S(2)}) copy-start(f32[32]{0:T(128)} %param.7) | copy-start | bytes 388
  33.2 6.6 %copy-start.11 = (f32[64]{0:T(128)S(1)}, f32[64]{0:T(128)}, u32[]{:S(2)}) copy-start(f32[64]{0:T(128)} %param.8) | copy-start | bytes 772
  33.2 23.2 %collective-permute-start.2 = (f32[512,256]{1,0:T(8,128)S(1)}, f32[512,256]{1,0:T(8,128)S(1)}, u32[]{:S(2)}, u32[]{:S(2)}) collective-permute-start(f32[512,256]{1,0:T(8,128)S(1)} %bitcast.18), channel_id=1, source_target_pairs={{0,1},{1,2},{2,3},{3,0},{4,5},{5,6},{6,7},{7,4},{8,9},{9,10},{10,1... | collective-permute-start | bytes 1572872 | tf_op jit(solution)/shard_map/ppermute | solution.py:54
  36.3 23.2 %collective-permute-start.3 = (f32[512,256]{1,0:T(8,128)S(1)}, f32[512,256]{1,0:T(8,128)S(1)}, u32[]{:S(2)}, u32[]{:S(2)}) collective-permute-start(f32[512,256]{1,0:T(8,128)S(1)} %bitcast.19), channel_id=1, source_target_pairs={{0,3},{1,0},{2,1},{3,2},{4,7},{5,4},{6,5},{7,6},{8,11},{9,8},{10,9... | collective-permute-start | bytes 1572872 | tf_op jit(solution)/shard_map/ppermute | solution.py:54
  51.2 12.1 %copy-start.1 = (f32[8,32,640]{2,1,0:T(8,128)}, f32[8,32,640]{2,1,0:T(8,128)S(1)}, u32[]{:S(2)}) copy-start(f32[8,32,640]{2,1,0:T(8,128)S(1)} %all-to-all-done.1) | copy-start | bytes 1966084
  51.2 12.1 %collective-permute-start.1 = (f32[16,16,640]{2,1,0:T(8,128)S(1)}, f32[16,16,640]{2,1,0:T(8,128)S(1)}, u32[]{:S(2)}, u32[]{:S(2)}) collective-permute-start(f32[16,16,640]{2,1,0:T(8,128)S(1)} %bitcast.16), channel_id=1, source_target_pairs={{0,16},{16,0},{1,17},{17,1},{2,18},{18,2},{3,19},{19,3},{4,20},{20... | collective-permute-start | bytes 1966088 | tf_op jit(solution)/shard_map/ppermute | solution.py:54
  56.4 6.8 %copy-start.3 = (f32[512,256]{1,0:T(8,128)}, f32[512,256]{1,0:T(8,128)S(1)}, u32[]{:S(2)}) copy-start(f32[512,256]{1,0:T(8,128)S(1)} %collective-permute-done.2.refs_1_) | copy-start | bytes 1572868
  56.4 11.3 %collective-permute-start.4 = (f32[256,256]{1,0:T(8,128)S(1)}, f32[256,256]{1,0:T(8,128)S(1)}, u32[]{:S(2)}, u32[]{:S(2)}) collective-permute-start(f32[256,256]{1,0:T(8,128)S(1)} %slice.34), channel_id=1, source_target_pairs={{0,1},{1,2},{2,3},{3,0},{4,5},{5,6},{6,7},{7,4},{8,9},{9,10},{10,1... | collective-permute-start | bytes 786440 | tf_op jit(solution)/shard_map/ppermute | solution.py:54
  59.6 3.7 %copy-start.4 = (f32[512,256]{1,0:T(8,128)}, f32[512,256]{1,0:T(8,128)S(1)}, u32[]{:S(2)}) copy-start(f32[512,256]{1,0:T(8,128)S(1)} %collective-permute-done.3.refs_2_) | copy-start | bytes 1572868
  59.6 9.5 %collective-permute-start.5 = (f32[256,256]{1,0:T(8,128)S(1)}, f32[256,256]{1,0:T(8,128)S(1)}, u32[]{:S(2)}, u32[]{:S(2)}) collective-permute-start(f32[256,256]{1,0:T(8,128)S(1)} %slice.35), channel_id=1, source_target_pairs={{0,3},{1,0},{2,1},{3,2},{4,7},{5,4},{6,5},{7,6},{8,11},{9,8},{10,9... | collective-permute-start | bytes 786440 | tf_op jit(solution)/shard_map/ppermute | solution.py:54
  63.3 0.9 copy-start.5
  67.8 1.4 copy-start.6
  69.1 0.7 copy-start.7
  71.7 20.4 %copy-start = (f32[512,256]{1,0:T(8,128)S(1)}, f32[512,256]{1,0:T(8,128)}, u32[]{:S(2)}) copy-start(f32[512,256]{1,0:T(8,128)} %screened_ref.3) | copy-start | bytes 1572868

commit v5 on v4

--- a/solution.py
+++ b/solution.py
@@ -149,13 +149,11 @@
 
 
 def late_kernel(
-    where_ref, part_ref, far_h_ref, far_l_ref, upper_hbm, lower_hbm, ch_in_ref, cl_in_ref,
-    pair_ref, ch_ref, cl_ref, cond_ref, sems,
+    where_ref, part_ref, far_h_ref, far_l_ref, upper_ref, lower_ref, ch_in_ref, cl_in_ref,
+    pair_ref, ch_ref, cl_ref,
 ):
     del ch_in_ref, cl_in_ref
-    for copy in collect((upper_hbm, lower_hbm), cond_ref, sems):
-        copy.wait()
-    block = cond_ref[...].reshape(-1, cond_ref.shape[2])
+    block = jnp.concatenate([upper_ref[...], lower_ref[...]], axis=0)
     ch, cl = split_rows(where_ref, LATE[0], block, ch_ref, cl_ref)
     xh, xl = far_h_ref[...], far_l_ref[...]
     pair = part_ref[...] + (dot(xh, ch) + (dot(xh, cl) + dot(xl, ch)))
@@ -277,8 +275,6 @@
         late_kernel,
         [((val, rows, points_c), F32)] + conds,
         [where, pair, far_h, far_l, upper, lower, ch, cl],
-        [pltpu.VMEM((2, *upper.shape), F32), pltpu.SemaphoreType.DMA((2,))],
-        far=(4, 5),
         aliases={6: 1, 7: 2},
     )
     for step in range(ITERS):

time: 217 us -> 216 us (level)
  no operation moved by 1% of the time
where the time goes in v5:
time: 216 us; the launch traced here: 214 us
  blocking collectives  137 us (63%)
  starting transfers between devices  40.9 us (19%)
  waiting for transfers between devices  19.6 us (9%)
  Pallas kernels  11.8 us (5%)
  local copies, waits for them, and re-layouts  4.4 us (2%)
    all_to_all x7, blocking collectives, exchange(): return lax.all_to_all(blocks, axes, 0, 0, tiled=True)  137 us
    ppermute x6, starting transfers between devices, shifted(): return lax.ppermute(array, axis, pairs)  26.1 us
    all_to_all x2, starting transfers between devices, exchange(): return lax.all_to_all(blocks, axes, 0, 0, tiled=True)  14.8 us
    pallas_call x9, Pallas kernels, call(): pl.pallas_call(kernel, out_shape=shapes if len(shapes) > 1 else shapes[0]...  11.8 us
    all_to_all x2, waiting for transfers between devices, exchange(): return lax.all_to_all(blocks, axes, 0, 0, tiled=True)  11.4 us
    ppermute x6, waiting for transfers between devices, shifted(): return lax.ppermute(array, axis, pairs)  8.24 us
  transfers between devices with their start and end apart: 8, of which 3 were waited for; matrix products, arithmetic and copies ran while one was open for 0% of the time, Pallas kernels for 2%

profile of v5, /device:TPU:1, one launch (start us, length us, event | category | flops | bytes accessed | tf_op | source)
XLA Modules:
  0.0 214.1 jit_solution(8194390013041442344)
XLA Ops:
  0.0 1.8 broadcast_in_dim.9
  1.8 7.9 %all-to-all-start = ((f32[4,128,256]{2,1,0:T(8,128)}), f32[4,128,256]{2,1,0:T(8,128)S(1)}, u32[]{:S(2)}, u32[]{:S(2)}) async-start(f32[4,128,256]{2,1,0:T(8,128)} %broadcast_in_dim.9), calls=%async_computation | async-start | bytes 1048576 | tf_op jit(solution)/shard_map/all_to_all | solution.py:45
  10.5 7.9 %collective-permute-start = (f32[16,640]{1,0:T(8,128)S(1)}, f32[16,640]{1,0:T(8,128)S(1)}, u32[]{:S(2)}, u32[]{:S(2)}) collective-permute-start(f32[16,640]{1,0:T(8,128)S(1)} %pad_maximum_fusion.1), channel_id=1, source_target_pairs={{0,256},{256,0},{1,257},{257,1},{2,258},{258,2},{3,259},{259,3},{4... | collective-permute-start | bytes 122888 | tf_op jit(solution)/shard_map/ppermute | solution.py:54
  18.5 6.8 %collective-permute-done = f32[16,640]{1,0:T(8,128)S(1)} collective-permute-done((f32[16,640]{1,0:T(8,128)S(1)}, f32[16,640]{1,0:T(8,128)S(1)}, u32[]{:S(2)}, u32[]{:S(2)}) %collective-permute-start) | collective-permute-done | bytes 40992 | tf_op jit(solution)/shard_map/ppermute | solution.py:54
  26.4 6.8 %all-to-all-start.1 = ((f32[8,32,640]{2,1,0:T(8,128)}), f32[8,32,640]{2,1,0:T(8,128)S(1)}, u32[]{:S(2)}, u32[]{:S(2)}) async-start(f32[8,32,640]{2,1,0:T(8,128)} %broadcast_in_dim.10), calls=%async_computation.1 | async-start | bytes 1310720 | tf_op jit(solution)/shard_map/all_to_all | solution.py:45
  33.2 3.1 %collective-permute-start.2 = (f32[512,256]{1,0:T(8,128)S(1)}, f32[512,256]{1,0:T(8,128)S(1)}, u32[]{:S(2)}, u32[]{:S(2)}) collective-permute-start(f32[512,256]{1,0:T(8,128)S(1)} %bitcast.18), channel_id=1, source_target_pairs={{0,1},{1,2},{2,3},{3,0},{4,5},{5,6},{6,7},{7,4},{8,9},{9,10},{10,1... | collective-permute-start | bytes 1572872 | tf_op jit(solution)/shard_map/ppermute | solution.py:54
  36.4 3.4 %collective-permute-start.3 = (f32[512,256]{1,0:T(8,128)S(1)}, f32[512,256]{1,0:T(8,128)S(1)}, u32[]{:S(2)}, u32[]{:S(2)}) collective-permute-start(f32[512,256]{1,0:T(8,128)S(1)} %bitcast.19), channel_id=1, source_target_pairs={{0,3},{1,0},{2,1},{3,2},{4,7},{5,4},{6,5},{7,6},{8,11},{9,8},{10,9... | collective-permute-start | bytes 1572872 | tf_op jit(solution)/shard_map/ppermute | solution.py:54
  39.8 11.4 %all-to-all-done.1 = f32[8,32,640]{2,1,0:T(8,128)S(1)} async-done(((f32[8,32,640]{2,1,0:T(8,128)}), f32[8,32,640]{2,1,0:T(8,128)S(1)}, u32[]{:S(2)}, u32[]{:S(2)}) %all-to-all-start.1) | async-done | bytes 655392 | tf_op jit(solution)/shard_map/all_to_all | solution.py:45
  51.2 5.2 %collective-permute-start.1 = (f32[16,16,640]{2,1,0:T(8,128)S(1)}, f32[16,16,640]{2,1,0:T(8,128)S(1)}, u32[]{:S(2)}, u32[]{:S(2)}) collective-permute-start(f32[16,16,640]{2,1,0:T(8,128)S(1)} %bitcast.16), channel_id=1, source_target_pairs={{0,16},{16,0},{1,17},{17,1},{2,18},{18,2},{3,19},{19,3},{4,20},{20... | collective-permute-start | bytes 1966088 | tf_op jit(solution)/shard_map/ppermute | solution.py:54
  56.5 3.1 %collective-permute-start.4 = (f32[256,256]{1,0:T(8,128)S(1)}, f32[256,256]{1,0:T(8,128)S(1)}, u32[]{:S(2)}, u32[]{:S(2)}) collective-permute-start(f32[256,256]{1,0:T(8,128)S(1)} %slice.34), channel_id=1, source_target_pairs={{0,1},{1,2},{2,3},{3,0},{4,5},{5,6},{6,7},{7,4},{8,9},{9,10},{10,1... | collective-permute-start | bytes 786440 | tf_op jit(solution)/shard_map/ppermute | solution.py:54
  59.6 3.4 %collective-permute-start.5 = (f32[256,256]{1,0:T(8,128)S(1)}, f32[256,256]{1,0:T(8,128)S(1)}, u32[]{:S(2)}, u32[]{:S(2)}) collective-permute-start(f32[256,256]{1,0:T(8,128)S(1)} %slice.35), channel_id=1, source_target_pairs={{0,3},{1,0},{2,1},{3,2},{4,7},{5,4},{6,5},{7,6},{8,11},{9,8},{10,9... | collective-permute-start | bytes 786440 | tf_op jit(solution)/shard_map/ppermute | solution.py:54
  64.1 3.6 %shard_map.64 = (bf16[512,512]{1,0:T(8,128)(2,1)S(1)}, bf16[512,512]{1,0:T(8,128)(2,1)S(1)}, bf16[512,512]{1,0:T(8,128)(2,1)S(1)}, bf16[512,512]{1,0:T(8,128)(2,...) custom-call(s32[49]{0:T(128)S(1)} %pad_add_fusion.where_ref, ...), custom_call_target="tpu_custom_call" | custom-call | tf_op jit(solution)/shard_map/pallas_call | solution.py:220
  67.8 1.4 collective-permute-done.5.lower_ref
  70.0 20.4 %all_to_all.45 = f32[16,32,256]{2,1,0:T(8,128)S(1)} all-to-all(f32[16,32,256]{2,1,0:T(8,128)S(1)} %get-tuple-element.30), channel_id=1, replica_groups=mesh['zh'=2,'y'=8,'core'=2,'zl_hi'=2,'zl_lo'=2,'x_hi'=2,'x_lo'=2] {'x_lo..., dimensions={0} | all-to-all | bytes 1048576 | tf_op jit(solution)/shard_map/all_to_all | solution.py:45
  90.4 1.8 shard_map.66
  92.2 17.4 %all_to_all.46.terms_ref = f32[16,32,256]{2,1,0:T(8,128)S(1)} all-to-all(f32[16,32,256]{2,1,0:T(8,128)S(1)} %bitcast.15), channel_id=1, replica_groups=mesh['zh'=2,'y'=8,'core'=2,'zl_hi'=2,'zl_lo'=2,'x_hi'=2,'x_lo'=2] {'x_lo..., dimensions={0} | all-to-all | bytes 1048576 | tf_op jit(solution)/shard_map/all_to_all | solution.py:45
  109.6 1.1 shard_map.67
  110.7 22.7 %all_to_all.47.terms_ref = f32[32,16,128]{2,1,0:T(8,128)S(1)} all-to-all(f32[32,16,128]{2,1,0:T(8,128)S(1)} %shard_map.67), channel_id=1, replica_groups=mesh['zh'=2,'y'=8,'core'=2,'zl_hi'=2,'zl_lo'=2,'x_hi'=2,'x_lo'=2] {'y','..., dimensions={0} | all-to-all | bytes 524288 | tf_op jit(solution)/shard_map/all_to_all | solution.py:45
  133.5 19.4 %all_to_all.48.gathered_ref = f32[32,16,128]{2,1,0:T(8,128)S(1)} all-to-all(f32[32,16,128]{2,1,0:T(8,128)S(1)} %get-tuple-element.39), channel_id=1, replica_groups=mesh['zh'=2,'y'=8,'core'=2,'zl_hi'=2,'zl_lo'=2,'x_hi'=2,'x_lo'=2] {'y','..., dimensions={0} | all-to-all | bytes 524288 | tf_op jit(solution)/shard_map/all_to_all | solution.py:45
  153.6 15.4 %all_to_all.49 = f32[16,32,256]{2,1,0:T(8,128)S(1)} all-to-all(f32[16,32,256]{2,1,0:T(8,128)S(1)} %shard_map.69), channel_id=1, replica_groups=mesh['zh'=2,'y'=8,'core'=2,'zl_hi'=2,'zl_lo'=2,'x_hi'=2,'x_lo'=2] {'x_lo..., dimensions={0} | all-to-all | bytes 1048576 | tf_op jit(solution)/shard_map/all_to_all | solution.py:45
  169.0 1.8 shard_map.70
  170.8 17.6 %all_to_all.50.terms_ref = f32[16,32,256]{2,1,0:T(8,128)S(1)} all-to-all(f32[16,32,256]{2,1,0:T(8,128)S(1)} %bitcast.13), channel_id=1, replica_groups=mesh['zh'=2,'y'=8,'core'=2,'zl_hi'=2,'zl_lo'=2,'x_hi'=2,'x_lo'=2] {'x_lo..., dimensions={0} | all-to-all | bytes 1048576 | tf_op jit(solution)/shard_map/all_to_all | solution.py:45
  188.5 1.1 shard_map.71
  189.6 23.8 %all_to_all.51.terms_ref = f32[32,16,128]{2,1,0:T(8,128)S(1)} all-to-all(f32[32,16,128]{2,1,0:T(8,128)S(1)} %shard_map.71), channel_id=1, replica_groups=mesh['zh'=2,'y'=8,'core'=2,'zl_hi'=2,'zl_lo'=2,'x_hi'=2,'x_lo'=2] {'y','..., dimensions={0} | all-to-all | bytes 524288 | tf_op jit(solution)/shard_map/all_to_all | solution.py:45
  (42 shorter events, 5.5 us)
Async XLA Ops:
  1.8 7.9 %copy-start.7 = (f32[1,32,64]{2,1,0:T(8,128)S(1)}, f32[1,32,64]{2,1,0:T(8,128)}, u32[]{:S(2)}) copy-start(f32[1,32,64]{2,1,0:T(8,128)} %param.6) | copy-start | bytes 24580
  1.8 23.6 %all-to-all-start = ((f32[4,128,256]{2,1,0:T(8,128)}), f32[4,128,256]{2,1,0:T(8,128)S(1)}, u32[]{:S(2)}, u32[]{:S(2)}) async-start(f32[4,128,256]{2,1,0:T(8,128)} %broadcast_in_dim.9), calls=%async_computation | async-start | bytes 1048576 | tf_op jit(solution)/shard_map/all_to_all | solution.py:45
  9.7 0.8 copy-start.6
  10.5 14.8 %collective-permute-start = (f32[16,640]{1,0:T(8,128)S(1)}, f32[16,640]{1,0:T(8,128)S(1)}, u32[]{:S(2)}, u32[]{:S(2)}) collective-permute-start(f32[16,640]{1,0:T(8,128)S(1)} %pad_maximum_fusion.1), channel_id=1, source_target_pairs={{0,256},{256,0},{1,257},{257,1},{2,258},{258,2},{3,259},{259,3},{4... | collective-permute-start | bytes 122888 | tf_op jit(solution)/shard_map/ppermute | solution.py:54
  25.4 11.0 %copy-start.2 = (f32[4,128,256]{2,1,0:T(8,128)}, f32[4,128,256]{2,1,0:T(8,128)S(1)}, u32[]{:S(2)}) copy-start(f32[4,128,256]{2,1,0:T(8,128)S(1)} %all-to-all-done) | copy-start | bytes 1572868
  26.4 24.8 %all-to-all-start.1 = ((f32[8,32,640]{2,1,0:T(8,128)}), f32[8,32,640]{2,1,0:T(8,128)S(1)}, u32[]{:S(2)}, u32[]{:S(2)}) async-start(f32[8,32,640]{2,1,0:T(8,128)} %broadcast_in_dim.10), calls=%async_computation.1 | async-start | bytes 1310720 | tf_op jit(solution)/shard_map/all_to_all | solution.py:45
  33.2 6.5 %copy-start.8 = (f32[32]{0:T(128)S(1)}, f32[32]{0:T(128)}, u32[]{:S(2)}) copy-start(f32[32]{0:T(128)} %param.7) | copy-start | bytes 388
  33.2 6.6 %copy-start.9 = (f32[64]{0:T(128)S(1)}, f32[64]{0:T(128)}, u32[]{:S(2)}) copy-start(f32[64]{0:T(128)} %param.8) | copy-start | bytes 772
  33.2 23.2 %collective-permute-start.2 = (f32[512,256]{1,0:T(8,128)S(1)}, f32[512,256]{1,0:T(8,128)S(1)}, u32[]{:S(2)}, u32[]{:S(2)}) collective-permute-start(f32[512,256]{1,0:T(8,128)S(1)} %bitcast.18), channel_id=1, source_target_pairs={{0,1},{1,2},{2,3},{3,0},{4,5},{5,6},{6,7},{7,4},{8,9},{9,10},{10,1... | collective-permute-start | bytes 1572872 | tf_op jit(solution)/shard_map/ppermute | solution.py:54
  36.4 23.2 %collective-permute-start.3 = (f32[512,256]{1,0:T(8,128)S(1)}, f32[512,256]{1,0:T(8,128)S(1)}, u32[]{:S(2)}, u32[]{:S(2)}) collective-permute-start(f32[512,256]{1,0:T(8,128)S(1)} %bitcast.19), channel_id=1, source_target_pairs={{0,3},{1,0},{2,1},{3,2},{4,7},{5,4},{6,5},{7,6},{8,11},{9,8},{10,9... | collective-permute-start | bytes 1572872 | tf_op jit(solution)/shard_map/ppermute | solution.py:54
  51.2 12.1 %copy-start.1 = (f32[8,32,640]{2,1,0:T(8,128)}, f32[8,32,640]{2,1,0:T(8,128)S(1)}, u32[]{:S(2)}) copy-start(f32[8,32,640]{2,1,0:T(8,128)S(1)} %all-to-all-done.1) | copy-start | bytes 1966084
  51.2 12.1 %collective-permute-start.1 = (f32[16,16,640]{2,1,0:T(8,128)S(1)}, f32[16,16,640]{2,1,0:T(8,128)S(1)}, u32[]{:S(2)}, u32[]{:S(2)}) collective-permute-start(f32[16,16,640]{2,1,0:T(8,128)S(1)} %bitcast.16), channel_id=1, source_target_pairs={{0,16},{16,0},{1,17},{17,1},{2,18},{18,2},{3,19},{19,3},{4,20},{20... | collective-permute-start | bytes 1966088 | tf_op jit(solution)/shard_map/ppermute | solution.py:54
  56.4 6.8 %copy-start.3 = (f32[512,256]{1,0:T(8,128)}, f32[512,256]{1,0:T(8,128)S(1)}, u32[]{:S(2)}) copy-start(f32[512,256]{1,0:T(8,128)S(1)} %collective-permute-done.2.refs_1_) | copy-start | bytes 1572868
  56.5 11.3 %collective-permute-start.4 = (f32[256,256]{1,0:T(8,128)S(1)}, f32[256,256]{1,0:T(8,128)S(1)}, u32[]{:S(2)}, u32[]{:S(2)}) collective-permute-start(f32[256,256]{1,0:T(8,128)S(1)} %slice.34), channel_id=1, source_target_pairs={{0,1},{1,2},{2,3},{3,0},{4,5},{5,6},{6,7},{7,4},{8,9},{9,10},{10,1... | collective-permute-start | bytes 786440 | tf_op jit(solution)/shard_map/ppermute | solution.py:54
  59.6 3.7 %copy-start.4 = (f32[512,256]{1,0:T(8,128)}, f32[512,256]{1,0:T(8,128)S(1)}, u32[]{:S(2)}) copy-start(f32[512,256]{1,0:T(8,128)S(1)} %collective-permute-done.3.refs_2_) | copy-start | bytes 1572868
  59.6 9.5 %collective-permute-start.5 = (f32[256,256]{1,0:T(8,128)S(1)}, f32[256,256]{1,0:T(8,128)S(1)}, u32[]{:S(2)}, u32[]{:S(2)}) collective-permute-start(f32[256,256]{1,0:T(8,128)S(1)} %slice.35), channel_id=1, source_target_pairs={{0,3},{1,0},{2,1},{3,2},{4,7},{5,4},{6,5},{7,6},{8,11},{9,8},{10,9... | collective-permute-start | bytes 786440 | tf_op jit(solution)/shard_map/ppermute | solution.py:54
  63.3 0.9 copy-start.5
  70.0 20.4 %copy-start = (f32[512,256]{1,0:T(8,128)S(1)}, f32[512,256]{1,0:T(8,128)}, u32[]{:S(2)}) copy-start(f32[512,256]{1,0:T(8,128)} %screened_ref.3) | copy-start | bytes 1572868

commit v6 on v5

--- a/solution.py
+++ b/solution.py
@@ -175,8 +175,13 @@
 
 def screen_kernel(pair_ref, screened_ref, vh_ref, vl_ref, th_ref, tl_ref, back_ref):
     ph, pl_ = split(pair_ref[...])
-    mixed = dot(th_ref[...], ph) + (dot(th_ref[...], pl_) + dot(tl_ref[...], ph))
-    wh, wl = split(mixed * screened_ref[...])
+    half = th_ref.shape[0] // 2
+    parts = []
+    for at in (slice(0, half), slice(half, 2 * half)):
+        th, tl = th_ref[at, :], tl_ref[at, :]
+        mixed = dot(th, ph) + (dot(th, pl_) + dot(tl, ph))
+        parts.append(split(mixed * screened_ref[at, :]))
+    wh, wl = (jnp.concatenate(p, axis=0) for p in zip(*parts))
     back_ref[...] = dot(vh_ref[...], wh) + (dot(vh_ref[...], wl) + dot(vl_ref[...], wh))
 
 

time: 216 us -> 214 us (level)
  no operation moved by 1% of the time
where the time goes in v6:
time: 214 us; the launch traced here: 213 us
  blocking collectives  137 us (64%)
  starting transfers between devices  40.9 us (19%)
  waiting for transfers between devices  19.6 us (9%)
  Pallas kernels  10.4 us (5%)
  local copies, waits for them, and re-layouts  4.4 us (2%)
    all_to_all x7, blocking collectives, exchange(): return lax.all_to_all(blocks, axes, 0, 0, tiled=True)  137 us
    ppermute x6, starting transfers between devices, shifted(): return lax.ppermute(array, axis, pairs)  26.1 us
    all_to_all x2, starting transfers between devices, exchange(): return lax.all_to_all(blocks, axes, 0, 0, tiled=True)  14.8 us
    all_to_all x2, waiting for transfers between devices, exchange(): return lax.all_to_all(blocks, axes, 0, 0, tiled=True)  11.4 us
    pallas_call x9, Pallas kernels, call(): pl.pallas_call(kernel, out_shape=shapes if len(shapes) > 1 else shapes[0]...  10.4 us
    ppermute x6, waiting for transfers between devices, shifted(): return lax.ppermute(array, axis, pairs)  8.24 us
  transfers between devices with their start and end apart: 8, of which 3 were waited for; matrix products, arithmetic and copies ran while one was open for 0% of the time, Pallas kernels for 2%

profile of v6, /device:TPU:1, one launch (start us, length us, event | category | flops | bytes accessed | tf_op | source)
XLA Modules:
  0.0 212.7 jit_solution(16862176157624165667)
XLA Ops:
  0.0 1.8 broadcast_in_dim.9
  1.8 7.9 %all-to-all-start = ((f32[4,128,256]{2,1,0:T(8,128)}), f32[4,128,256]{2,1,0:T(8,128)S(1)}, u32[]{:S(2)}, u32[]{:S(2)}) async-start(f32[4,128,256]{2,1,0:T(8,128)} %broadcast_in_dim.9), calls=%async_computation | async-start | bytes 1048576 | tf_op jit(solution)/shard_map/all_to_all | solution.py:45
  10.5 7.9 %collective-permute-start = (f32[16,640]{1,0:T(8,128)S(1)}, f32[16,640]{1,0:T(8,128)S(1)}, u32[]{:S(2)}, u32[]{:S(2)}) collective-permute-start(f32[16,640]{1,0:T(8,128)S(1)} %pad_maximum_fusion.1), channel_id=1, source_target_pairs={{0,256},{256,0},{1,257},{257,1},{2,258},{258,2},{3,259},{259,3},{4... | collective-permute-start | bytes 122888 | tf_op jit(solution)/shard_map/ppermute | solution.py:54
  18.5 6.8 %collective-permute-done = f32[16,640]{1,0:T(8,128)S(1)} collective-permute-done((f32[16,640]{1,0:T(8,128)S(1)}, f32[16,640]{1,0:T(8,128)S(1)}, u32[]{:S(2)}, u32[]{:S(2)}) %collective-permute-start) | collective-permute-done | bytes 40992 | tf_op jit(solution)/shard_map/ppermute | solution.py:54
  26.4 6.8 %all-to-all-start.1 = ((f32[8,32,640]{2,1,0:T(8,128)}), f32[8,32,640]{2,1,0:T(8,128)S(1)}, u32[]{:S(2)}, u32[]{:S(2)}) async-start(f32[8,32,640]{2,1,0:T(8,128)} %broadcast_in_dim.10), calls=%async_computation.1 | async-start | bytes 1310720 | tf_op jit(solution)/shard_map/all_to_all | solution.py:45
  33.2 3.1 %collective-permute-start.2 = (f32[512,256]{1,0:T(8,128)S(1)}, f32[512,256]{1,0:T(8,128)S(1)}, u32[]{:S(2)}, u32[]{:S(2)}) collective-permute-start(f32[512,256]{1,0:T(8,128)S(1)} %bitcast.18), channel_id=1, source_target_pairs={{0,1},{1,2},{2,3},{3,0},{4,5},{5,6},{6,7},{7,4},{8,9},{9,10},{10,1... | collective-permute-start | bytes 1572872 | tf_op jit(solution)/shard_map/ppermute | solution.py:54
  36.4 3.4 %collective-permute-start.3 = (f32[512,256]{1,0:T(8,128)S(1)}, f32[512,256]{1,0:T(8,128)S(1)}, u32[]{:S(2)}, u32[]{:S(2)}) collective-permute-start(f32[512,256]{1,0:T(8,128)S(1)} %bitcast.19), channel_id=1, source_target_pairs={{0,3},{1,0},{2,1},{3,2},{4,7},{5,4},{6,5},{7,6},{8,11},{9,8},{10,9... | collective-permute-start | bytes 1572872 | tf_op jit(solution)/shard_map/ppermute | solution.py:54
  39.8 11.4 %all-to-all-done.1 = f32[8,32,640]{2,1,0:T(8,128)S(1)} async-done(((f32[8,32,640]{2,1,0:T(8,128)}), f32[8,32,640]{2,1,0:T(8,128)S(1)}, u32[]{:S(2)}, u32[]{:S(2)}) %all-to-all-start.1) | async-done | bytes 655392 | tf_op jit(solution)/shard_map/all_to_all | solution.py:45
  51.2 5.2 %collective-permute-start.1 = (f32[16,16,640]{2,1,0:T(8,128)S(1)}, f32[16,16,640]{2,1,0:T(8,128)S(1)}, u32[]{:S(2)}, u32[]{:S(2)}) collective-permute-start(f32[16,16,640]{2,1,0:T(8,128)S(1)} %bitcast.16), channel_id=1, source_target_pairs={{0,16},{16,0},{1,17},{17,1},{2,18},{18,2},{3,19},{19,3},{4,20},{20... | collective-permute-start | bytes 1966088 | tf_op jit(solution)/shard_map/ppermute | solution.py:54
  56.5 3.1 %collective-permute-start.4 = (f32[256,256]{1,0:T(8,128)S(1)}, f32[256,256]{1,0:T(8,128)S(1)}, u32[]{:S(2)}, u32[]{:S(2)}) collective-permute-start(f32[256,256]{1,0:T(8,128)S(1)} %slice.34), channel_id=1, source_target_pairs={{0,1},{1,2},{2,3},{3,0},{4,5},{5,6},{6,7},{7,4},{8,9},{9,10},{10,1... | collective-permute-start | bytes 786440 | tf_op jit(solution)/shard_map/ppermute | solution.py:54
  59.6 3.4 %collective-permute-start.5 = (f32[256,256]{1,0:T(8,128)S(1)}, f32[256,256]{1,0:T(8,128)S(1)}, u32[]{:S(2)}, u32[]{:S(2)}) collective-permute-start(f32[256,256]{1,0:T(8,128)S(1)} %slice.35), channel_id=1, source_target_pairs={{0,3},{1,0},{2,1},{3,2},{4,7},{5,4},{6,5},{7,6},{8,11},{9,8},{10,9... | collective-permute-start | bytes 786440 | tf_op jit(solution)/shard_map/ppermute | solution.py:54
  64.1 3.6 %shard_map.64 = (bf16[512,512]{1,0:T(8,128)(2,1)S(1)}, bf16[512,512]{1,0:T(8,128)(2,1)S(1)}, bf16[512,512]{1,0:T(8,128)(2,1)S(1)}, bf16[512,512]{1,0:T(8,128)(2,...) custom-call(s32[49]{0:T(128)S(1)} %pad_add_fusion.where_ref, ...), custom_call_target="tpu_custom_call" | custom-call | tf_op jit(solution)/shard_map/pallas_call | solution.py:225
  67.8 1.4 collective-permute-done.5.lower_ref
  70.0 20.4 %all_to_all.45 = f32[16,32,256]{2,1,0:T(8,128)S(1)} all-to-all(f32[16,32,256]{2,1,0:T(8,128)S(1)} %get-tuple-element.30), channel_id=1, replica_groups=mesh['zh'=2,'y'=8,'core'=2,'zl_hi'=2,'zl_lo'=2,'x_hi'=2,'x_lo'=2] {'x_lo..., dimensions={0} | all-to-all | bytes 1048576 | tf_op jit(solution)/shard_map/all_to_all | solution.py:45
  90.4 1.1 shard_map.66
  91.5 17.4 %all_to_all.46.terms_ref = f32[16,32,256]{2,1,0:T(8,128)S(1)} all-to-all(f32[16,32,256]{2,1,0:T(8,128)S(1)} %bitcast.15), channel_id=1, replica_groups=mesh['zh'=2,'y'=8,'core'=2,'zl_hi'=2,'zl_lo'=2,'x_hi'=2,'x_lo'=2] {'x_lo..., dimensions={0} | all-to-all | bytes 1048576 | tf_op jit(solution)/shard_map/all_to_all | solution.py:45
  108.9 1.1 shard_map.67
  110.1 22.6 %all_to_all.47.terms_ref = f32[32,16,128]{2,1,0:T(8,128)S(1)} all-to-all(f32[32,16,128]{2,1,0:T(8,128)S(1)} %shard_map.67), channel_id=1, replica_groups=mesh['zh'=2,'y'=8,'core'=2,'zl_hi'=2,'zl_lo'=2,'x_hi'=2,'x_lo'=2] {'y','..., dimensions={0} | all-to-all | bytes 524288 | tf_op jit(solution)/shard_map/all_to_all | solution.py:45
  132.8 19.4 %all_to_all.48.gathered_ref = f32[32,16,128]{2,1,0:T(8,128)S(1)} all-to-all(f32[32,16,128]{2,1,0:T(8,128)S(1)} %get-tuple-element.39), channel_id=1, replica_groups=mesh['zh'=2,'y'=8,'core'=2,'zl_hi'=2,'zl_lo'=2,'x_hi'=2,'x_lo'=2] {'y','..., dimensions={0} | all-to-all | bytes 524288 | tf_op jit(solution)/shard_map/all_to_all | solution.py:45
  152.9 15.4 %all_to_all.49 = f32[16,32,256]{2,1,0:T(8,128)S(1)} all-to-all(f32[16,32,256]{2,1,0:T(8,128)S(1)} %shard_map.69), channel_id=1, replica_groups=mesh['zh'=2,'y'=8,'core'=2,'zl_hi'=2,'zl_lo'=2,'x_hi'=2,'x_lo'=2] {'x_lo..., dimensions={0} | all-to-all | bytes 1048576 | tf_op jit(solution)/shard_map/all_to_all | solution.py:45
  168.3 1.1 shard_map.70
  169.5 17.6 %all_to_all.50.terms_ref = f32[16,32,256]{2,1,0:T(8,128)S(1)} all-to-all(f32[16,32,256]{2,1,0:T(8,128)S(1)} %bitcast.13), channel_id=1, replica_groups=mesh['zh'=2,'y'=8,'core'=2,'zl_hi'=2,'zl_lo'=2,'x_hi'=2,'x_lo'=2] {'x_lo..., dimensions={0} | all-to-all | bytes 1048576 | tf_op jit(solution)/shard_map/all_to_all | solution.py:45
  187.1 1.1 shard_map.71
  188.2 23.8 %all_to_all.51.terms_ref = f32[32,16,128]{2,1,0:T(8,128)S(1)} all-to-all(f32[32,16,128]{2,1,0:T(8,128)S(1)} %shard_map.71), channel_id=1, replica_groups=mesh['zh'=2,'y'=8,'core'=2,'zl_hi'=2,'zl_lo'=2,'x_hi'=2,'x_lo'=2] {'y','..., dimensions={0} | all-to-all | bytes 524288 | tf_op jit(solution)/shard_map/all_to_all | solution.py:45
  (42 shorter events, 5.5 us)
Async XLA Ops:
  1.8 7.9 %copy-start.7 = (f32[1,32,64]{2,1,0:T(8,128)S(1)}, f32[1,32,64]{2,1,0:T(8,128)}, u32[]{:S(2)}) copy-start(f32[1,32,64]{2,1,0:T(8,128)} %param.6) | copy-start | bytes 24580
  1.8 23.6 %all-to-all-start = ((f32[4,128,256]{2,1,0:T(8,128)}), f32[4,128,256]{2,1,0:T(8,128)S(1)}, u32[]{:S(2)}, u32[]{:S(2)}) async-start(f32[4,128,256]{2,1,0:T(8,128)} %broadcast_in_dim.9), calls=%async_computation | async-start | bytes 1048576 | tf_op jit(solution)/shard_map/all_to_all | solution.py:45
  9.7 0.8 copy-start.6
  10.5 14.8 %collective-permute-start = (f32[16,640]{1,0:T(8,128)S(1)}, f32[16,640]{1,0:T(8,128)S(1)}, u32[]{:S(2)}, u32[]{:S(2)}) collective-permute-start(f32[16,640]{1,0:T(8,128)S(1)} %pad_maximum_fusion.1), channel_id=1, source_target_pairs={{0,256},{256,0},{1,257},{257,1},{2,258},{258,2},{3,259},{259,3},{4... | collective-permute-start | bytes 122888 | tf_op jit(solution)/shard_map/ppermute | solution.py:54
  25.4 11.0 %copy-start.2 = (f32[4,128,256]{2,1,0:T(8,128)}, f32[4,128,256]{2,1,0:T(8,128)S(1)}, u32[]{:S(2)}) copy-start(f32[4,128,256]{2,1,0:T(8,128)S(1)} %all-to-all-done) | copy-start | bytes 1572868
  26.4 24.8 %all-to-all-start.1 = ((f32[8,32,640]{2,1,0:T(8,128)}), f32[8,32,640]{2,1,0:T(8,128)S(1)}, u32[]{:S(2)}, u32[]{:S(2)}) async-start(f32[8,32,640]{2,1,0:T(8,128)} %broadcast_in_dim.10), calls=%async_computation.1 | async-start | bytes 1310720 | tf_op jit(solution)/shard_map/all_to_all | solution.py:45
  33.2 6.5 %copy-start.8 = (f32[32]{0:T(128)S(1)}, f32[32]{0:T(128)}, u32[]{:S(2)}) copy-start(f32[32]{0:T(128)} %param.7) | copy-start | bytes 388
  33.2 6.6 %copy-start.9 = (f32[64]{0:T(128)S(1)}, f32[64]{0:T(128)}, u32[]{:S(2)}) copy-start(f32[64]{0:T(128)} %param.8) | copy-start | bytes 772
  33.2 23.2 %collective-permute-start.2 = (f32[512,256]{1,0:T(8,128)S(1)}, f32[512,256]{1,0:T(8,128)S(1)}, u32[]{:S(2)}, u32[]{:S(2)}) collective-permute-start(f32[512,256]{1,0:T(8,128)S(1)} %bitcast.18), channel_id=1, source_target_pairs={{0,1},{1,2},{2,3},{3,0},{4,5},{5,6},{6,7},{7,4},{8,9},{9,10},{10,1... | collective-permute-start | bytes 1572872 | tf_op jit(solution)/shard_map/ppermute | solution.py:54
  36.4 23.2 %collective-permute-start.3 = (f32[512,256]{1,0:T(8,128)S(1)}, f32[512,256]{1,0:T(8,128)S(1)}, u32[]{:S(2)}, u32[]{:S(2)}) collective-permute-start(f32[512,256]{1,0:T(8,128)S(1)} %bitcast.19), channel_id=1, source_target_pairs={{0,3},{1,0},{2,1},{3,2},{4,7},{5,4},{6,5},{7,6},{8,11},{9,8},{10,9... | collective-permute-start | bytes 1572872 | tf_op jit(solution)/shard_map/ppermute | solution.py:54
  51.2 12.1 %copy-start.1 = (f32[8,32,640]{2,1,0:T(8,128)}, f32[8,32,640]{2,1,0:T(8,128)S(1)}, u32[]{:S(2)}) copy-start(f32[8,32,640]{2,1,0:T(8,128)S(1)} %all-to-all-done.1) | copy-start | bytes 1966084
  51.2 12.1 %collective-permute-start.1 = (f32[16,16,640]{2,1,0:T(8,128)S(1)}, f32[16,16,640]{2,1,0:T(8,128)S(1)}, u32[]{:S(2)}, u32[]{:S(2)}) collective-permute-start(f32[16,16,640]{2,1,0:T(8,128)S(1)} %bitcast.16), channel_id=1, source_target_pairs={{0,16},{16,0},{1,17},{17,1},{2,18},{18,2},{3,19},{19,3},{4,20},{20... | collective-permute-start | bytes 1966088 | tf_op jit(solution)/shard_map/ppermute | solution.py:54
  56.4 6.8 %copy-start.3 = (f32[512,256]{1,0:T(8,128)}, f32[512,256]{1,0:T(8,128)S(1)}, u32[]{:S(2)}) copy-start(f32[512,256]{1,0:T(8,128)S(1)} %collective-permute-done.2.refs_1_) | copy-start | bytes 1572868
  56.5 11.3 %collective-permute-start.4 = (f32[256,256]{1,0:T(8,128)S(1)}, f32[256,256]{1,0:T(8,128)S(1)}, u32[]{:S(2)}, u32[]{:S(2)}) collective-permute-start(f32[256,256]{1,0:T(8,128)S(1)} %slice.34), channel_id=1, source_target_pairs={{0,1},{1,2},{2,3},{3,0},{4,5},{5,6},{6,7},{7,4},{8,9},{9,10},{10,1... | collective-permute-start | bytes 786440 | tf_op jit(solution)/shard_map/ppermute | solution.py:54
  59.6 3.7 %copy-start.4 = (f32[512,256]{1,0:T(8,128)}, f32[512,256]{1,0:T(8,128)S(1)}, u32[]{:S(2)}) copy-start(f32[512,256]{1,0:T(8,128)S(1)} %collective-permute-done.3.refs_2_) | copy-start | bytes 1572868
  59.6 9.5 %collective-permute-start.5 = (f32[256,256]{1,0:T(8,128)S(1)}, f32[256,256]{1,0:T(8,128)S(1)}, u32[]{:S(2)}, u32[]{:S(2)}) collective-permute-start(f32[256,256]{1,0:T(8,128)S(1)} %slice.35), channel_id=1, source_target_pairs={{0,3},{1,0},{2,1},{3,2},{4,7},{5,4},{6,5},{7,6},{8,11},{9,8},{10,9... | collective-permute-start | bytes 786440 | tf_op jit(solution)/shard_map/ppermute | solution.py:54
  63.3 0.9 copy-start.5
  70.0 20.4 %copy-start = (f32[512,256]{1,0:T(8,128)S(1)}, f32[512,256]{1,0:T(8,128)}, u32[]{:S(2)}) copy-start(f32[512,256]{1,0:T(8,128)} %screened_ref.3) | copy-start | bytes 1572868

commit v7 on v6

--- a/solution.py
+++ b/solution.py
@@ -10,8 +10,8 @@
 CENTER = 2.2
 HALF_WIDTH = 2.0
 
-ROWS = ("zh", "y")
-PTS = ("zh", "y", "core")
+Y = ("y_hi", "y_mid", "y_lo")
+PTS = ("zh",) + Y + ("core",)
 Z, X = ("zl_hi", "zl_lo"), ("x_hi", "x_lo")
 VAL = Z + X
 CROSS = ("zh", "core")
@@ -20,7 +20,7 @@
 EARLY, LATE = (0, 1, 3), (2,)
 WIDTH = 128
 SEND = ("x_lo", "x_hi", "zl_lo", "zl_hi")
-SWEEP = ("y", "core", "zh")
+SWEEP = Y + ("core", "zh")
 SENT = [int(f"{i:04b}"[::-1], 2) for i in range(NX * NZ)]
 
 F32 = jnp.float32
@@ -243,7 +243,7 @@
     zh, core = lax.axis_index("zh"), lax.axis_index("core")
     p = jnp.arange(pts)
     chip = jnp.arange(val)
-    where = [lax.axis_index(X)[None], (p & 1) ^ core, chip % NY * 2 + (chip // NY ^ zh)]
+    where = [lax.axis_index(X)[None], (p & 1) ^ core, (chip & 1) * 8 + (chip & 2) * 2 + (chip & 4) // 2 + (chip // NY ^ zh)]
     where = jnp.concatenate(where).astype(jnp.int32)
     older = packed(vectors[0])
     ediff = packed(cond_energy[None, :] - eval_energy[:, None])
@@ -252,7 +252,7 @@
     parcel = jnp.concatenate([val_orbitals, older], axis=1)
     parcel = jnp.concatenate([parcel, shifted(parcel, "zh", 1)], axis=0)
     mine, parcel = lax.optimization_barrier((mine, parcel))
-    own = copied(parcel, "y").reshape(-1, depth_v, points_v + width)
+    own = copied(parcel, Y[::-1]).reshape(-1, depth_v, points_v + width)
     other = shifted(own, "core", 1)
     left, right = shifted(mine, X, 1), shifted(mine, X, -1)
     part = mine.shape[0] // 2
@@ -308,7 +308,7 @@
 
 
 def solution(mesh):
-    torus = Mesh(mesh.devices.reshape(2, 8, 2, 2, 2, 2, 2), PTS + Z + X)
+    torus = Mesh(mesh.devices.reshape((2,) * 9), PTS + Z + X)
     placed = (P(None, VAL, PTS), P(VAL), P(PTS), P(PTS, VAL), P(VAL, PTS), P(VAL, PTS))
     return jax.shard_map(
         per_device, mesh=torus, in_specs=placed, out_specs=P(None, VAL, PTS), check_vma=False

time: 214 us -> 214 us (level)
  blocking collectives: 137 us -> 140 us
    all_to_all x7, blocking collectives: 137 us -> 140 us  [exchange(): return lax.all_to_all(blocks, axes, 0, 0, tiled=True)]
where the time goes in v7:
time: 214 us; the launch traced here: 213 us
  blocking collectives  140 us (65%)
  starting transfers between devices  39.6 us (19%)
  waiting for transfers between devices  17.9 us (8%)
  Pallas kernels  10.4 us (5%)
  local copies, waits for them, and re-layouts  4.4 us (2%)
    all_to_all x7, blocking collectives, exchange(): return lax.all_to_all(blocks, axes, 0, 0, tiled=True)  140 us
    ppermute x6, starting transfers between devices, shifted(): return lax.ppermute(array, axis, pairs)  24.8 us
    all_to_all x2, starting transfers between devices, exchange(): return lax.all_to_all(blocks, axes, 0, 0, tiled=True)  14.8 us
    pallas_call x9, Pallas kernels, call(): pl.pallas_call(kernel, out_shape=shapes if len(shapes) > 1 else shapes[0]...  10.4 us
    all_to_all x2, waiting for transfers between devices, exchange(): return lax.all_to_all(blocks, axes, 0, 0, tiled=True)  9.68 us
    ppermute x6, waiting for transfers between devices, shifted(): return lax.ppermute(array, axis, pairs)  8.24 us
  transfers between devices with their start and end apart: 8, of which 3 were waited for; matrix products, arithmetic and copies ran while one was open for 0% of the time, Pallas kernels for 2%

profile of v7, /device:TPU:1, one launch (start us, length us, event | category | flops | bytes accessed | tf_op | source)
XLA Modules:
  0.0 212.6 jit_solution(6955744651479021321)
XLA Ops:
  0.0 1.8 broadcast_in_dim.9
  1.8 7.9 %all-to-all-start = ((f32[4,128,256]{2,1,0:T(8,128)}), f32[4,128,256]{2,1,0:T(8,128)S(1)}, u32[]{:S(2)}, u32[]{:S(2)}) async-start(f32[4,128,256]{2,1,0:T(8,128)} %broadcast_in_dim.9), calls=%async_computation | async-start | bytes 1048576 | tf_op jit(solution)/shard_map/all_to_all | solution.py:45
  10.5 7.9 %collective-permute-start = (f32[16,640]{1,0:T(8,128)S(1)}, f32[16,640]{1,0:T(8,128)S(1)}, u32[]{:S(2)}, u32[]{:S(2)}) collective-permute-start(f32[16,640]{1,0:T(8,128)S(1)} %pad_maximum_fusion.1), channel_id=1, source_target_pairs={{0,256},{256,0},{1,257},{257,1},{2,258},{258,2},{3,259},{259,3},{4... | collective-permute-start | bytes 122888 | tf_op jit(solution)/shard_map/ppermute | solution.py:54
  18.5 6.8 %collective-permute-done = f32[16,640]{1,0:T(8,128)S(1)} collective-permute-done((f32[16,640]{1,0:T(8,128)S(1)}, f32[16,640]{1,0:T(8,128)S(1)}, u32[]{:S(2)}, u32[]{:S(2)}) %collective-permute-start) | collective-permute-done | bytes 40992 | tf_op jit(solution)/shard_map/ppermute | solution.py:54
  26.4 6.8 %all-to-all-start.1 = ((f32[8,32,640]{2,1,0:T(8,128)}), f32[8,32,640]{2,1,0:T(8,128)S(1)}, u32[]{:S(2)}, u32[]{:S(2)}) async-start(f32[8,32,640]{2,1,0:T(8,128)} %broadcast_in_dim.10), calls=%async_computation.1 | async-start | bytes 1310720 | tf_op jit(solution)/shard_map/all_to_all | solution.py:45
  33.2 3.1 %collective-permute-start.2 = (f32[512,256]{1,0:T(8,128)S(1)}, f32[512,256]{1,0:T(8,128)S(1)}, u32[]{:S(2)}, u32[]{:S(2)}) collective-permute-start(f32[512,256]{1,0:T(8,128)S(1)} %bitcast.18), channel_id=1, source_target_pairs={{0,1},{1,2},{2,3},{3,0},{4,5},{5,6},{6,7},{7,4},{8,9},{9,10},{10,1... | collective-permute-start | bytes 1572872 | tf_op jit(solution)/shard_map/ppermute | solution.py:54
  36.4 3.4 %collective-permute-start.3 = (f32[512,256]{1,0:T(8,128)S(1)}, f32[512,256]{1,0:T(8,128)S(1)}, u32[]{:S(2)}, u32[]{:S(2)}) collective-permute-start(f32[512,256]{1,0:T(8,128)S(1)} %bitcast.19), channel_id=1, source_target_pairs={{0,3},{1,0},{2,1},{3,2},{4,7},{5,4},{6,5},{7,6},{8,11},{9,8},{10,9... | collective-permute-start | bytes 1572872 | tf_op jit(solution)/shard_map/ppermute | solution.py:54
  39.8 9.7 %all-to-all-done.1 = f32[8,32,640]{2,1,0:T(8,128)S(1)} async-done(((f32[8,32,640]{2,1,0:T(8,128)}), f32[8,32,640]{2,1,0:T(8,128)S(1)}, u32[]{:S(2)}, u32[]{:S(2)}) %all-to-all-start.1) | async-done | bytes 655392 | tf_op jit(solution)/shard_map/all_to_all | solution.py:45
  49.5 3.9 %collective-permute-start.1 = (f32[16,16,640]{2,1,0:T(8,128)S(1)}, f32[16,16,640]{2,1,0:T(8,128)S(1)}, u32[]{:S(2)}, u32[]{:S(2)}) collective-permute-start(f32[16,16,640]{2,1,0:T(8,128)S(1)} %bitcast.16), channel_id=1, source_target_pairs={{0,16},{16,0},{1,17},{17,1},{2,18},{18,2},{3,19},{19,3},{4,20},{20... | collective-permute-start | bytes 1966088 | tf_op jit(solution)/shard_map/ppermute | solution.py:54
  53.5 3.1 %collective-permute-start.4 = (f32[256,256]{1,0:T(8,128)S(1)}, f32[256,256]{1,0:T(8,128)S(1)}, u32[]{:S(2)}, u32[]{:S(2)}) collective-permute-start(f32[256,256]{1,0:T(8,128)S(1)} %slice.34), channel_id=1, source_target_pairs={{0,1},{1,2},{2,3},{3,0},{4,5},{5,6},{6,7},{7,4},{8,9},{9,10},{10,1... | collective-permute-start | bytes 786440 | tf_op jit(solution)/shard_map/ppermute | solution.py:54
  56.7 3.4 %collective-permute-start.5 = (f32[256,256]{1,0:T(8,128)S(1)}, f32[256,256]{1,0:T(8,128)S(1)}, u32[]{:S(2)}, u32[]{:S(2)}) collective-permute-start(f32[256,256]{1,0:T(8,128)S(1)} %slice.35), channel_id=1, source_target_pairs={{0,3},{1,0},{2,1},{3,2},{4,7},{5,4},{6,5},{7,6},{8,11},{9,8},{10,9... | collective-permute-start | bytes 786440 | tf_op jit(solution)/shard_map/ppermute | solution.py:54
  61.2 3.6 %shard_map.64 = (bf16[512,512]{1,0:T(8,128)(2,1)S(1)}, bf16[512,512]{1,0:T(8,128)(2,1)S(1)}, bf16[512,512]{1,0:T(8,128)(2,1)S(1)}, bf16[512,512]{1,0:T(8,128)(2,...) custom-call(s32[49]{0:T(128)S(1)} %pad_add_fusion.where_ref, ...), custom_call_target="tpu_custom_call" | custom-call | tf_op jit(solution)/shard_map/pallas_call | solution.py:225
  64.8 1.4 collective-permute-done.5.lower_ref
  67.0 20.4 %all_to_all.45 = f32[16,32,256]{2,1,0:T(8,128)S(1)} all-to-all(f32[16,32,256]{2,1,0:T(8,128)S(1)} %get-tuple-element.30), channel_id=1, replica_groups=mesh['zh'=2,'y_hi'=2,'y_mid'=2,'y_lo'=2,'core'=2,'zl_hi'=2,'zl_lo'=2,'x_..., dimensions={0} | all-to-all | bytes 1048576 | tf_op jit(solution)/shard_map/all_to_all | solution.py:45
  87.4 1.1 shard_map.66
  88.5 17.4 %all_to_all.46.terms_ref = f32[16,32,256]{2,1,0:T(8,128)S(1)} all-to-all(f32[16,32,256]{2,1,0:T(8,128)S(1)} %bitcast.15), channel_id=1, replica_groups=mesh['zh'=2,'y_hi'=2,'y_mid'=2,'y_lo'=2,'core'=2,'zl_hi'=2,'zl_lo'=2,'x_..., dimensions={0} | all-to-all | bytes 1048576 | tf_op jit(solution)/shard_map/all_to_all | solution.py:45
  106.0 1.1 shard_map.67
  107.1 25.6 %all_to_all.47.terms_ref = f32[32,16,128]{2,1,0:T(8,128)S(1)} all-to-all(f32[32,16,128]{2,1,0:T(8,128)S(1)} %shard_map.67), channel_id=1, replica_groups=mesh['zh'=2,'y_hi'=2,'y_mid'=2,'y_lo'=2,'core'=2,'zl_hi'=2,'zl_lo'=2,'x_..., dimensions={0} | all-to-all | bytes 524288 | tf_op jit(solution)/shard_map/all_to_all | solution.py:45
  132.7 19.4 %all_to_all.48.gathered_ref = f32[32,16,128]{2,1,0:T(8,128)S(1)} all-to-all(f32[32,16,128]{2,1,0:T(8,128)S(1)} %get-tuple-element.39), channel_id=1, replica_groups=mesh['zh'=2,'y_hi'=2,'y_mid'=2,'y_lo'=2,'core'=2,'zl_hi'=2,'zl_lo'=2,'x_..., dimensions={0} | all-to-all | bytes 524288 | tf_op jit(solution)/shard_map/all_to_all | solution.py:45
  152.8 15.4 %all_to_all.49 = f32[16,32,256]{2,1,0:T(8,128)S(1)} all-to-all(f32[16,32,256]{2,1,0:T(8,128)S(1)} %shard_map.69), channel_id=1, replica_groups=mesh['zh'=2,'y_hi'=2,'y_mid'=2,'y_lo'=2,'core'=2,'zl_hi'=2,'zl_lo'=2,'x_..., dimensions={0} | all-to-all | bytes 1048576 | tf_op jit(solution)/shard_map/all_to_all | solution.py:45
  168.3 1.1 shard_map.70
  169.4 17.6 %all_to_all.50.terms_ref = f32[16,32,256]{2,1,0:T(8,128)S(1)} all-to-all(f32[16,32,256]{2,1,0:T(8,128)S(1)} %bitcast.13), channel_id=1, replica_groups=mesh['zh'=2,'y_hi'=2,'y_mid'=2,'y_lo'=2,'core'=2,'zl_hi'=2,'zl_lo'=2,'x_..., dimensions={0} | all-to-all | bytes 1048576 | tf_op jit(solution)/shard_map/all_to_all | solution.py:45
  187.0 1.1 shard_map.71
  188.1 23.8 %all_to_all.51.terms_ref = f32[32,16,128]{2,1,0:T(8,128)S(1)} all-to-all(f32[32,16,128]{2,1,0:T(8,128)S(1)} %shard_map.71), channel_id=1, replica_groups=mesh['zh'=2,'y_hi'=2,'y_mid'=2,'y_lo'=2,'core'=2,'zl_hi'=2,'zl_lo'=2,'x_..., dimensions={0} | all-to-all | bytes 524288 | tf_op jit(solution)/shard_map/all_to_all | solution.py:45
  (42 shorter events, 5.5 us)
Async XLA Ops:
  1.8 7.9 %copy-start.7 = (f32[1,32,64]{2,1,0:T(8,128)S(1)}, f32[1,32,64]{2,1,0:T(8,128)}, u32[]{:S(2)}) copy-start(f32[1,32,64]{2,1,0:T(8,128)} %param.6) | copy-start | bytes 24580
  1.8 23.6 %all-to-all-start = ((f32[4,128,256]{2,1,0:T(8,128)}), f32[4,128,256]{2,1,0:T(8,128)S(1)}, u32[]{:S(2)}, u32[]{:S(2)}) async-start(f32[4,128,256]{2,1,0:T(8,128)} %broadcast_in_dim.9), calls=%async_computation | async-start | bytes 1048576 | tf_op jit(solution)/shard_map/all_to_all | solution.py:45
  9.7 0.8 copy-start.6
  10.5 14.8 %collective-permute-start = (f32[16,640]{1,0:T(8,128)S(1)}, f32[16,640]{1,0:T(8,128)S(1)}, u32[]{:S(2)}, u32[]{:S(2)}) collective-permute-start(f32[16,640]{1,0:T(8,128)S(1)} %pad_maximum_fusion.1), channel_id=1, source_target_pairs={{0,256},{256,0},{1,257},{257,1},{2,258},{258,2},{3,259},{259,3},{4... | collective-permute-start | bytes 122888 | tf_op jit(solution)/shard_map/ppermute | solution.py:54
  25.4 11.0 %copy-start.2 = (f32[4,128,256]{2,1,0:T(8,128)}, f32[4,128,256]{2,1,0:T(8,128)S(1)}, u32[]{:S(2)}) copy-start(f32[4,128,256]{2,1,0:T(8,128)S(1)} %all-to-all-done) | copy-start | bytes 1572868
  26.4 23.1 %all-to-all-start.1 = ((f32[8,32,640]{2,1,0:T(8,128)}), f32[8,32,640]{2,1,0:T(8,128)S(1)}, u32[]{:S(2)}, u32[]{:S(2)}) async-start(f32[8,32,640]{2,1,0:T(8,128)} %broadcast_in_dim.10), calls=%async_computation.1 | async-start | bytes 1310720 | tf_op jit(solution)/shard_map/all_to_all | solution.py:45
  33.2 6.5 %copy-start.8 = (f32[32]{0:T(128)S(1)}, f32[32]{0:T(128)}, u32[]{:S(2)}) copy-start(f32[32]{0:T(128)} %param.7) | copy-start | bytes 388
  33.2 6.6 %copy-start.9 = (f32[64]{0:T(128)S(1)}, f32[64]{0:T(128)}, u32[]{:S(2)}) copy-start(f32[64]{0:T(128)} %param.8) | copy-start | bytes 772
  33.2 20.2 %collective-permute-start.2 = (f32[512,256]{1,0:T(8,128)S(1)}, f32[512,256]{1,0:T(8,128)S(1)}, u32[]{:S(2)}, u32[]{:S(2)}) collective-permute-start(f32[512,256]{1,0:T(8,128)S(1)} %bitcast.18), channel_id=1, source_target_pairs={{0,1},{1,2},{2,3},{3,0},{4,5},{5,6},{6,7},{7,4},{8,9},{9,10},{10,1... | collective-permute-start | bytes 1572872 | tf_op jit(solution)/shard_map/ppermute | solution.py:54
  36.4 20.3 %collective-permute-start.3 = (f32[512,256]{1,0:T(8,128)S(1)}, f32[512,256]{1,0:T(8,128)S(1)}, u32[]{:S(2)}, u32[]{:S(2)}) collective-permute-start(f32[512,256]{1,0:T(8,128)S(1)} %bitcast.19), channel_id=1, source_target_pairs={{0,3},{1,0},{2,1},{3,2},{4,7},{5,4},{6,5},{7,6},{8,11},{9,8},{10,9... | collective-permute-start | bytes 1572872 | tf_op jit(solution)/shard_map/ppermute | solution.py:54
  49.5 10.8 %copy-start.1 = (f32[8,32,640]{2,1,0:T(8,128)}, f32[8,32,640]{2,1,0:T(8,128)S(1)}, u32[]{:S(2)}) copy-start(f32[8,32,640]{2,1,0:T(8,128)S(1)} %all-to-all-done.1) | copy-start | bytes 1966084
  49.5 10.8 %collective-permute-start.1 = (f32[16,16,640]{2,1,0:T(8,128)S(1)}, f32[16,16,640]{2,1,0:T(8,128)S(1)}, u32[]{:S(2)}, u32[]{:S(2)}) collective-permute-start(f32[16,16,640]{2,1,0:T(8,128)S(1)} %bitcast.16), channel_id=1, source_target_pairs={{0,16},{16,0},{1,17},{17,1},{2,18},{18,2},{3,19},{19,3},{4,20},{20... | collective-permute-start | bytes 1966088 | tf_op jit(solution)/shard_map/ppermute | solution.py:54
  53.5 6.8 %copy-start.3 = (f32[512,256]{1,0:T(8,128)}, f32[512,256]{1,0:T(8,128)S(1)}, u32[]{:S(2)}) copy-start(f32[512,256]{1,0:T(8,128)S(1)} %collective-permute-done.2.refs_1_) | copy-start | bytes 1572868
  53.5 11.3 %collective-permute-start.4 = (f32[256,256]{1,0:T(8,128)S(1)}, f32[256,256]{1,0:T(8,128)S(1)}, u32[]{:S(2)}, u32[]{:S(2)}) collective-permute-start(f32[256,256]{1,0:T(8,128)S(1)} %slice.34), channel_id=1, source_target_pairs={{0,1},{1,2},{2,3},{3,0},{4,5},{5,6},{6,7},{7,4},{8,9},{9,10},{10,1... | collective-permute-start | bytes 786440 | tf_op jit(solution)/shard_map/ppermute | solution.py:54
  56.6 3.7 %copy-start.4 = (f32[512,256]{1,0:T(8,128)}, f32[512,256]{1,0:T(8,128)S(1)}, u32[]{:S(2)}) copy-start(f32[512,256]{1,0:T(8,128)S(1)} %collective-permute-done.3.refs_2_) | copy-start | bytes 1572868
  56.7 9.5 %collective-permute-start.5 = (f32[256,256]{1,0:T(8,128)S(1)}, f32[256,256]{1,0:T(8,128)S(1)}, u32[]{:S(2)}, u32[]{:S(2)}) collective-permute-start(f32[256,256]{1,0:T(8,128)S(1)} %slice.35), channel_id=1, source_target_pairs={{0,3},{1,0},{2,1},{3,2},{4,7},{5,4},{6,5},{7,6},{8,11},{9,8},{10,9... | collective-permute-start | bytes 786440 | tf_op jit(solution)/shard_map/ppermute | solution.py:54
  60.3 0.9 copy-start.5
  67.0 20.4 %copy-start = (f32[512,256]{1,0:T(8,128)S(1)}, f32[512,256]{1,0:T(8,128)}, u32[]{:S(2)}) copy-start(f32[512,256]{1,0:T(8,128)} %screened_ref.3) | copy-start | bytes 1572868

commit v8 on v6

--- a/solution.py
+++ b/solution.py
@@ -167,10 +167,15 @@
 
 
 def pair_kernel(gathered_ref, ch_ref, cl_ref, pair_ref, xh_ref, xl_ref):
-    for q in range(NX * NZ):
-        a, b = gathered_ref[sent_at(2 * q)], gathered_ref[sent_at(2 * q + 1)]
-        place_pair(a, b, q, xh_ref, xl_ref)
-    multiply_pair(xh_ref, xl_ref, ch_ref, cl_ref, pair_ref)
+    pair = jnp.zeros(pair_ref.shape[1:], F32)
+    for z in range(NZ):
+        for q in range(z * NX, (z + 1) * NX):
+            a, b = gathered_ref[sent_at(2 * q)], gathered_ref[sent_at(2 * q + 1)]
+            place_pair(a, b, q, xh_ref, xl_ref)
+        at = slice(z * NX * WIDTH, (z + 1) * NX * WIDTH)
+        xh, xl, ch, cl = xh_ref[:, at], xl_ref[:, at], ch_ref[at, :], cl_ref[at, :]
+        pair += dot(xh, ch) + (dot(xh, cl) + dot(xl, ch))
+    pair_ref[...] = jnp.broadcast_to(pair[None], pair_ref.shape)
 
 
 def screen_kernel(pair_ref, screened_ref, vh_ref, vl_ref, th_ref, tl_ref, back_ref):
@@ -251,7 +256,6 @@
     mine = copied(cond_orbitals, Z).reshape(-1, points_c)
     parcel = jnp.concatenate([val_orbitals, older], axis=1)
     parcel = jnp.concatenate([parcel, shifted(parcel, "zh", 1)], axis=0)
-    mine, parcel = lax.optimization_barrier((mine, parcel))
     own = copied(parcel, "y").reshape(-1, depth_v, points_v + width)
     other = shifted(own, "core", 1)
     left, right = shifted(mine, X, 1), shifted(mine, X, -1)

time: 214 us -> 214 us (level)
  no operation moved by 1% of the time
where the time goes in v8:
time: 214 us; the launch traced here: 213 us
  blocking collectives  137 us (64%)
  starting transfers between devices  40.9 us (19%)
  waiting for transfers between devices  19.6 us (9%)
  Pallas kernels  10.4 us (5%)
  local copies, waits for them, and re-layouts  4.4 us (2%)
    all_to_all x7, blocking collectives, exchange(): return lax.all_to_all(blocks, axes, 0, 0, tiled=True)  137 us
    ppermute x6, starting transfers between devices, shifted(): return lax.ppermute(array, axis, pairs)  26.1 us
    all_to_all x2, starting transfers between devices, exchange(): return lax.all_to_all(blocks, axes, 0, 0, tiled=True)  14.8 us
    all_to_all x2, waiting for transfers between devices, exchange(): return lax.all_to_all(blocks, axes, 0, 0, tiled=True)  11.4 us
    pallas_call x9, Pallas kernels, call(): pl.pallas_call(kernel, out_shape=shapes if len(shapes) > 1 else shapes[0]...  10.4 us
    ppermute x6, waiting for transfers between devices, shifted(): return lax.ppermute(array, axis, pairs)  8.24 us
  transfers between devices with their start and end apart: 8, of which 3 were waited for; matrix products, arithmetic and copies ran while one was open for 0% of the time, Pallas kernels for 2%

profile of v8, /device:TPU:1, one launch (start us, length us, event | category | flops | bytes accessed | tf_op | source)
XLA Modules:
  0.0 212.6 jit_solution(7113803349892790096)
XLA Ops:
  0.0 1.8 broadcast_in_dim.10
  1.8 7.9 %all-to-all-start.1 = ((f32[4,128,256]{2,1,0:T(8,128)}), f32[4,128,256]{2,1,0:T(8,128)S(1)}, u32[]{:S(2)}, u32[]{:S(2)}) async-start(f32[4,128,256]{2,1,0:T(8,128)} %broadcast_in_dim.10), calls=%async_computation.1 | async-start | bytes 1048576 | tf_op jit(solution)/shard_map/all_to_all | solution.py:45
  10.5 7.9 %collective-permute-start = (f32[16,640]{1,0:T(8,128)S(1)}, f32[16,640]{1,0:T(8,128)S(1)}, u32[]{:S(2)}, u32[]{:S(2)}) collective-permute-start(f32[16,640]{1,0:T(8,128)S(1)} %pad_maximum_fusion.1), channel_id=1, source_target_pairs={{0,256},{256,0},{1,257},{257,1},{2,258},{258,2},{3,259},{259,3},{4... | collective-permute-start | bytes 122888 | tf_op jit(solution)/shard_map/ppermute | solution.py:54
  18.5 6.8 %collective-permute-done = f32[16,640]{1,0:T(8,128)S(1)} collective-permute-done((f32[16,640]{1,0:T(8,128)S(1)}, f32[16,640]{1,0:T(8,128)S(1)}, u32[]{:S(2)}, u32[]{:S(2)}) %collective-permute-start) | collective-permute-done | bytes 40992 | tf_op jit(solution)/shard_map/ppermute | solution.py:54
  26.4 6.8 %all-to-all-start = ((f32[8,32,640]{2,1,0:T(8,128)}), f32[8,32,640]{2,1,0:T(8,128)S(1)}, u32[]{:S(2)}, u32[]{:S(2)}) async-start(f32[8,32,640]{2,1,0:T(8,128)} %broadcast_in_dim.9), calls=%async_computation | async-start | bytes 1310720 | tf_op jit(solution)/shard_map/all_to_all | solution.py:45
  33.2 3.1 %collective-permute-start.2 = (f32[512,256]{1,0:T(8,128)S(1)}, f32[512,256]{1,0:T(8,128)S(1)}, u32[]{:S(2)}, u32[]{:S(2)}) collective-permute-start(f32[512,256]{1,0:T(8,128)S(1)} %bitcast.18), channel_id=1, source_target_pairs={{0,1},{1,2},{2,3},{3,0},{4,5},{5,6},{6,7},{7,4},{8,9},{9,10},{10,1... | collective-permute-start | bytes 1572872 | tf_op jit(solution)/shard_map/ppermute | solution.py:54
  36.4 3.4 %collective-permute-start.3 = (f32[512,256]{1,0:T(8,128)S(1)}, f32[512,256]{1,0:T(8,128)S(1)}, u32[]{:S(2)}, u32[]{:S(2)}) collective-permute-start(f32[512,256]{1,0:T(8,128)S(1)} %bitcast.19), channel_id=1, source_target_pairs={{0,3},{1,0},{2,1},{3,2},{4,7},{5,4},{6,5},{7,6},{8,11},{9,8},{10,9... | collective-permute-start | bytes 1572872 | tf_op jit(solution)/shard_map/ppermute | solution.py:54
  39.8 11.4 %all-to-all-done = f32[8,32,640]{2,1,0:T(8,128)S(1)} async-done(((f32[8,32,640]{2,1,0:T(8,128)}), f32[8,32,640]{2,1,0:T(8,128)S(1)}, u32[]{:S(2)}, u32[]{:S(2)}) %all-to-all-start) | async-done | bytes 655392 | tf_op jit(solution)/shard_map/all_to_all | solution.py:45
  51.2 5.2 %collective-permute-start.1 = (f32[16,16,640]{2,1,0:T(8,128)S(1)}, f32[16,16,640]{2,1,0:T(8,128)S(1)}, u32[]{:S(2)}, u32[]{:S(2)}) collective-permute-start(f32[16,16,640]{2,1,0:T(8,128)S(1)} %bitcast.16), channel_id=1, source_target_pairs={{0,16},{16,0},{1,17},{17,1},{2,18},{18,2},{3,19},{19,3},{4,20},{20... | collective-permute-start | bytes 1966088 | tf_op jit(solution)/shard_map/ppermute | solution.py:54
  56.5 3.1 %collective-permute-start.4 = (f32[256,256]{1,0:T(8,128)S(1)}, f32[256,256]{1,0:T(8,128)S(1)}, u32[]{:S(2)}, u32[]{:S(2)}) collective-permute-start(f32[256,256]{1,0:T(8,128)S(1)} %slice.34), channel_id=1, source_target_pairs={{0,1},{1,2},{2,3},{3,0},{4,5},{5,6},{6,7},{7,4},{8,9},{9,10},{10,1... | collective-permute-start | bytes 786440 | tf_op jit(solution)/shard_map/ppermute | solution.py:54
  59.6 3.4 %collective-permute-start.5 = (f32[256,256]{1,0:T(8,128)S(1)}, f32[256,256]{1,0:T(8,128)S(1)}, u32[]{:S(2)}, u32[]{:S(2)}) collective-permute-start(f32[256,256]{1,0:T(8,128)S(1)} %slice.35), channel_id=1, source_target_pairs={{0,3},{1,0},{2,1},{3,2},{4,7},{5,4},{6,5},{7,6},{8,11},{9,8},{10,9... | collective-permute-start | bytes 786440 | tf_op jit(solution)/shard_map/ppermute | solution.py:54
  64.1 3.6 %shard_map.64 = (bf16[512,512]{1,0:T(8,128)(2,1)S(1)}, bf16[512,512]{1,0:T(8,128)(2,1)S(1)}, bf16[512,512]{1,0:T(8,128)(2,1)S(1)}, bf16[512,512]{1,0:T(8,128)(2,...) custom-call(s32[49]{0:T(128)S(1)} %pad_add_fusion.where_ref, ...), custom_call_target="tpu_custom_call" | custom-call | tf_op jit(solution)/shard_map/pallas_call | solution.py:230
  67.8 1.4 collective-permute-done.5.lower_ref
  70.0 20.4 %all_to_all.45 = f32[16,32,256]{2,1,0:T(8,128)S(1)} all-to-all(f32[16,32,256]{2,1,0:T(8,128)S(1)} %get-tuple-element.26), channel_id=1, replica_groups=mesh['zh'=2,'y'=8,'core'=2,'zl_hi'=2,'zl_lo'=2,'x_hi'=2,'x_lo'=2] {'x_lo..., dimensions={0} | all-to-all | bytes 1048576 | tf_op jit(solution)/shard_map/all_to_all | solution.py:45
  90.4 1.1 shard_map.66
  91.5 17.4 %all_to_all.46.terms_ref = f32[16,32,256]{2,1,0:T(8,128)S(1)} all-to-all(f32[16,32,256]{2,1,0:T(8,128)S(1)} %bitcast.15), channel_id=1, replica_groups=mesh['zh'=2,'y'=8,'core'=2,'zl_hi'=2,'zl_lo'=2,'x_hi'=2,'x_lo'=2] {'x_lo..., dimensions={0} | all-to-all | bytes 1048576 | tf_op jit(solution)/shard_map/all_to_all | solution.py:45
  108.9 1.1 shard_map.67
  110.1 22.6 %all_to_all.47.terms_ref = f32[32,16,128]{2,1,0:T(8,128)S(1)} all-to-all(f32[32,16,128]{2,1,0:T(8,128)S(1)} %shard_map.67), channel_id=1, replica_groups=mesh['zh'=2,'y'=8,'core'=2,'zl_hi'=2,'zl_lo'=2,'x_hi'=2,'x_lo'=2] {'y','..., dimensions={0} | all-to-all | bytes 524288 | tf_op jit(solution)/shard_map/all_to_all | solution.py:45
  132.8 19.4 %all_to_all.48.gathered_ref = f32[32,16,128]{2,1,0:T(8,128)S(1)} all-to-all(f32[32,16,128]{2,1,0:T(8,128)S(1)} %get-tuple-element.35), channel_id=1, replica_groups=mesh['zh'=2,'y'=8,'core'=2,'zl_hi'=2,'zl_lo'=2,'x_hi'=2,'x_lo'=2] {'y','..., dimensions={0} | all-to-all | bytes 524288 | tf_op jit(solution)/shard_map/all_to_all | solution.py:45
  152.9 15.4 %all_to_all.49 = f32[16,32,256]{2,1,0:T(8,128)S(1)} all-to-all(f32[16,32,256]{2,1,0:T(8,128)S(1)} %shard_map.69), channel_id=1, replica_groups=mesh['zh'=2,'y'=8,'core'=2,'zl_hi'=2,'zl_lo'=2,'x_hi'=2,'x_lo'=2] {'x_lo..., dimensions={0} | all-to-all | bytes 1048576 | tf_op jit(solution)/shard_map/all_to_all | solution.py:45
  168.3 1.1 shard_map.70
  169.4 17.6 %all_to_all.50.terms_ref = f32[16,32,256]{2,1,0:T(8,128)S(1)} all-to-all(f32[16,32,256]{2,1,0:T(8,128)S(1)} %bitcast.13), channel_id=1, replica_groups=mesh['zh'=2,'y'=8,'core'=2,'zl_hi'=2,'zl_lo'=2,'x_hi'=2,'x_lo'=2] {'x_lo..., dimensions={0} | all-to-all | bytes 1048576 | tf_op jit(solution)/shard_map/all_to_all | solution.py:45
  187.0 1.1 shard_map.71
  188.1 23.8 %all_to_all.51.terms_ref = f32[32,16,128]{2,1,0:T(8,128)S(1)} all-to-all(f32[32,16,128]{2,1,0:T(8,128)S(1)} %shard_map.71), channel_id=1, replica_groups=mesh['zh'=2,'y'=8,'core'=2,'zl_hi'=2,'zl_lo'=2,'x_hi'=2,'x_lo'=2] {'y','..., dimensions={0} | all-to-all | bytes 524288 | tf_op jit(solution)/shard_map/all_to_all | solution.py:45
  (42 shorter events, 5.4 us)
Async XLA Ops:
  1.8 7.9 %copy-start.7 = (f32[1,32,64]{2,1,0:T(8,128)S(1)}, f32[1,32,64]{2,1,0:T(8,128)}, u32[]{:S(2)}) copy-start(f32[1,32,64]{2,1,0:T(8,128)} %param.6) | copy-start | bytes 24580
  1.8 23.6 %all-to-all-start.1 = ((f32[4,128,256]{2,1,0:T(8,128)}), f32[4,128,256]{2,1,0:T(8,128)S(1)}, u32[]{:S(2)}, u32[]{:S(2)}) async-start(f32[4,128,256]{2,1,0:T(8,128)} %broadcast_in_dim.10), calls=%async_computation.1 | async-start | bytes 1048576 | tf_op jit(solution)/shard_map/all_to_all | solution.py:45
  9.7 0.8 copy-start.6
  10.5 14.8 %collective-permute-start = (f32[16,640]{1,0:T(8,128)S(1)}, f32[16,640]{1,0:T(8,128)S(1)}, u32[]{:S(2)}, u32[]{:S(2)}) collective-permute-start(f32[16,640]{1,0:T(8,128)S(1)} %pad_maximum_fusion.1), channel_id=1, source_target_pairs={{0,256},{256,0},{1,257},{257,1},{2,258},{258,2},{3,259},{259,3},{4... | collective-permute-start | bytes 122888 | tf_op jit(solution)/shard_map/ppermute | solution.py:54
  25.4 11.0 %copy-start.2 = (f32[4,128,256]{2,1,0:T(8,128)}, f32[4,128,256]{2,1,0:T(8,128)S(1)}, u32[]{:S(2)}) copy-start(f32[4,128,256]{2,1,0:T(8,128)S(1)} %all-to-all-done.1) | copy-start | bytes 1572868
  26.4 24.8 %all-to-all-start = ((f32[8,32,640]{2,1,0:T(8,128)}), f32[8,32,640]{2,1,0:T(8,128)S(1)}, u32[]{:S(2)}, u32[]{:S(2)}) async-start(f32[8,32,640]{2,1,0:T(8,128)} %broadcast_in_dim.9), calls=%async_computation | async-start | bytes 1310720 | tf_op jit(solution)/shard_map/all_to_all | solution.py:45
  33.2 6.5 %copy-start.8 = (f32[32]{0:T(128)S(1)}, f32[32]{0:T(128)}, u32[]{:S(2)}) copy-start(f32[32]{0:T(128)} %param.7) | copy-start | bytes 388
  33.2 6.5 %copy-start.9 = (f32[64]{0:T(128)S(1)}, f32[64]{0:T(128)}, u32[]{:S(2)}) copy-start(f32[64]{0:T(128)} %param.8) | copy-start | bytes 772
  33.2 23.2 %collective-permute-start.2 = (f32[512,256]{1,0:T(8,128)S(1)}, f32[512,256]{1,0:T(8,128)S(1)}, u32[]{:S(2)}, u32[]{:S(2)}) collective-permute-start(f32[512,256]{1,0:T(8,128)S(1)} %bitcast.18), channel_id=1, source_target_pairs={{0,1},{1,2},{2,3},{3,0},{4,5},{5,6},{6,7},{7,4},{8,9},{9,10},{10,1... | collective-permute-start | bytes 1572872 | tf_op jit(solution)/shard_map/ppermute | solution.py:54
  36.4 23.2 %collective-permute-start.3 = (f32[512,256]{1,0:T(8,128)S(1)}, f32[512,256]{1,0:T(8,128)S(1)}, u32[]{:S(2)}, u32[]{:S(2)}) collective-permute-start(f32[512,256]{1,0:T(8,128)S(1)} %bitcast.19), channel_id=1, source_target_pairs={{0,3},{1,0},{2,1},{3,2},{4,7},{5,4},{6,5},{7,6},{8,11},{9,8},{10,9... | collective-permute-start | bytes 1572872 | tf_op jit(solution)/shard_map/ppermute | solution.py:54
  51.2 12.1 %copy-start.1 = (f32[8,32,640]{2,1,0:T(8,128)}, f32[8,32,640]{2,1,0:T(8,128)S(1)}, u32[]{:S(2)}) copy-start(f32[8,32,640]{2,1,0:T(8,128)S(1)} %all-to-all-done) | copy-start | bytes 1966084
  51.2 12.1 %collective-permute-start.1 = (f32[16,16,640]{2,1,0:T(8,128)S(1)}, f32[16,16,640]{2,1,0:T(8,128)S(1)}, u32[]{:S(2)}, u32[]{:S(2)}) collective-permute-start(f32[16,16,640]{2,1,0:T(8,128)S(1)} %bitcast.16), channel_id=1, source_target_pairs={{0,16},{16,0},{1,17},{17,1},{2,18},{18,2},{3,19},{19,3},{4,20},{20... | collective-permute-start | bytes 1966088 | tf_op jit(solution)/shard_map/ppermute | solution.py:54
  56.4 6.8 %copy-start.3 = (f32[512,256]{1,0:T(8,128)}, f32[512,256]{1,0:T(8,128)S(1)}, u32[]{:S(2)}) copy-start(f32[512,256]{1,0:T(8,128)S(1)} %collective-permute-done.2.refs_1_) | copy-start | bytes 1572868
  56.5 11.3 %collective-permute-start.4 = (f32[256,256]{1,0:T(8,128)S(1)}, f32[256,256]{1,0:T(8,128)S(1)}, u32[]{:S(2)}, u32[]{:S(2)}) collective-permute-start(f32[256,256]{1,0:T(8,128)S(1)} %slice.34), channel_id=1, source_target_pairs={{0,1},{1,2},{2,3},{3,0},{4,5},{5,6},{6,7},{7,4},{8,9},{9,10},{10,1... | collective-permute-start | bytes 786440 | tf_op jit(solution)/shard_map/ppermute | solution.py:54
  59.6 3.7 %copy-start.4 = (f32[512,256]{1,0:T(8,128)}, f32[512,256]{1,0:T(8,128)S(1)}, u32[]{:S(2)}) copy-start(f32[512,256]{1,0:T(8,128)S(1)} %collective-permute-done.3.refs_2_) | copy-start | bytes 1572868
  59.6 9.5 %collective-permute-start.5 = (f32[256,256]{1,0:T(8,128)S(1)}, f32[256,256]{1,0:T(8,128)S(1)}, u32[]{:S(2)}, u32[]{:S(2)}) collective-permute-start(f32[256,256]{1,0:T(8,128)S(1)} %slice.35), channel_id=1, source_target_pairs={{0,3},{1,0},{2,1},{3,2},{4,7},{5,4},{6,5},{7,6},{8,11},{9,8},{10,9... | collective-permute-start | bytes 786440 | tf_op jit(solution)/shard_map/ppermute | solution.py:54
  63.3 0.9 copy-start.5
  70.0 20.4 %copy-start = (f32[512,256]{1,0:T(8,128)S(1)}, f32[512,256]{1,0:T(8,128)}, u32[]{:S(2)}) copy-start(f32[512,256]{1,0:T(8,128)} %screened_ref.3) | copy-start | bytes 1572868
